TPU v7x, 32 devices: a whole 2x2x4 slice. The times are simulated.
32 devices in a mesh: dp: 4 (over y, x), seq: 8 (over z, core).
Axes of the slice: x: 2, y: 2, z: 4, core: 2. Of those that a mesh axis runs over, the one named last changes fastest.
Arguments:
- tokens: bfloat16 [4, 1024, 2048], P('dp', 'seq'), may hold values from -6 to 6
- segments: int32 [4, 1024], P('dp', 'seq'), may hold values from 0 to 2, as said below
- norm_one: bfloat16 [2048], P(('dp', 'seq')), may hold values from 0.5 to 1.5
- w_qkv: bfloat16 [2048, 6144], P(('dp', 'seq')), may hold values from -0.125 to 0.125
- w_lr: bfloat16 [2048, 32], P(('dp', 'seq')), may hold values from -0.125 to 0.125
- lr_bias: bfloat16 [32], replicated, may hold values from -3 to 3
- w_gate: bfloat16 [2048, 2048], P(('dp', 'seq')), may hold values from -0.125 to 0.125
- w_out: bfloat16 [2048, 2048], P(('dp', 'seq')), may hold values from -0.125 to 0.125
- w_init: bfloat16 [2048, 64], P(('dp', 'seq')), may hold values from -0.75 to 0.75
- b_init: bfloat16 [2048], P(('dp', 'seq')), may hold values from -3 to 3
- tnorm_w: bfloat16 [2048], P(('dp', 'seq')), may hold values from 0.25 to 1.75
- tnorm_b: bfloat16 [2048], P(('dp', 'seq')), may hold values from -2 to 2
- post_w: bfloat16 [2048], P(('dp', 'seq')), may hold values from 0.5 to 1.5
- post_b: bfloat16 [2048], P(('dp', 'seq')), may hold values from -2 to 2
- norm_two: bfloat16 [2048], P(('dp', 'seq')), may hold values from 0.5 to 1.5
- w_gate_up: bfloat16 [2048, 11008], P(('dp', 'seq')), may hold values from -0.125 to 0.125
- w_down: bfloat16 [5504, 2048], P(('dp', 'seq')), may hold values from -0.078125 to 0.078125
- grad_out: bfloat16 [4, 1024, 2048], P('dp', 'seq'), may hold values from -6 to 6
Outputs:
- block_out: bfloat16 [4, 1024, 2048], P('dp', 'seq')
- d_tokens: bfloat16 [4, 1024, 2048], P('dp', 'seq')
- g_norm_one: float32 [2048], P(('dp', 'seq'))
- g_qkv: float32 [2048, 6144], P(('dp', 'seq'))
- g_lr: float32 [2048, 32], P(('dp', 'seq'))
- g_lr_bias: float32 [32], replicated
- g_gate: float32 [2048, 2048], P(('dp', 'seq'))
- g_out: float32 [2048, 2048], P(('dp', 'seq'))
- g_init_w: float32 [2048, 64], P(('dp', 'seq'))
- g_init_b: float32 [2048], P(('dp', 'seq'))
- g_tnorm_w: float32 [2048], P(('dp', 'seq'))
- g_tnorm_b: float32 [2048], P(('dp', 'seq'))
- g_post_w: float32 [2048], P(('dp', 'seq'))
- g_post_b: float32 [2048], P(('dp', 'seq'))
- g_norm_two: float32 [2048], P(('dp', 'seq'))
- g_gate_up: float32 [2048, 11008], P(('dp', 'seq'))
- g_down: float32 [5504, 2048], P(('dp', 'seq'))
Inputs may be any that keep to these rules, and one draw needn't show every extreme that they name: `segments`: in each pack the document numbers are 0, 1, 2 in order and constant on each aligned block of 16 tokens; document 1 begins within the pack's first 128 tokens and ends within its last 128 tokens; documents 0 and 2 are never empty.
All inputs are finite; a program needn't handle non-finite values.
Results may differ from a plain program's by a relative error of at most 0.0095.
Values may be sent and summed in bfloat16 or wider, within the bound.
A program may use at most 576 MiB of HBM per device.

v0:
```python
import math

import jax
import jax.numpy as jnp
from jax import lax
from jax.sharding import PartitionSpec as P

D = 2048
H = 32
HD = 64
FF = 5504
MB = 16
SPAN = 128


EPSILON = 1e-06
BASE_RATE = 1.0
PRECISE = lax.Precision.HIGHEST


def shifted(array, axis, by):
    count = lax.axis_size(axis)
    pairs = [(i, i + by) for i in range(count) if 0 <= i + by < count]
    return lax.ppermute(array, axis, pairs)


def normalize(values):
    center = values - jnp.mean(values, -1, keepdims=True)
    scale_inv = lax.rsqrt(jnp.mean(center * center, -1, keepdims=True) + EPSILON)
    return (center * scale_inv, scale_inv)


def inner_step(w_mat, b_vec, q_rows, k_rows, v_rows, lr_rows, norm_gain, norm_shift):
    z_one = jnp.einsum("hti,hij->htj", k_rows, w_mat, precision=PRECISE) + b_vec[:, None, :]
    target = v_rows - k_rows
    x_hat, scale_inv = normalize(z_one)
    gain_rows = norm_gain[:, None, :]
    shift_rows = norm_shift[:, None, :]
    error_rows = gain_rows * x_hat + shift_rows - target
    g_hat = error_rows * gain_rows
    slope = scale_inv * (
        g_hat
        - jnp.mean(g_hat, -1, keepdims=True)
        - x_hat * jnp.mean(g_hat * x_hat, -1, keepdims=True)
    )
    places = jnp.arange(q_rows.shape[1])
    causal = places[:, None] >= places[None, :]
    divisor = (places[:, None] + 1).astype(jnp.float32)
    step_size = jnp.where(causal[None, :, :], lr_rows[:, None, :] / divisor[None, :, :], 0.0)
    scores = jnp.einsum("hti,hsi->hts", q_rows, k_rows, precision=PRECISE)
    z_bar = (
        jnp.einsum("hti,hij->htj", q_rows, w_mat, precision=PRECISE)
        + b_vec[:, None, :]
        - jnp.einsum("hts,hsj->htj", step_size * (scores + 1.0), slope, precision=PRECISE)
    )
    last_row = step_size[:, -1, :]
    w_next = w_mat - jnp.einsum(
        "hsi,hsj->hij", k_rows * last_row[:, :, None], slope, precision=PRECISE
    )
    b_next = b_vec - jnp.sum(last_row[:, :, None] * slope, axis=1)
    bar_hat, _ = normalize(z_bar)
    return (w_next, b_next, q_rows + gain_rows * bar_hat + shift_rows)


def cross_rows(left_side, right_side):
    return lax.dot_general(
        left_side, right_side, (((0,), (0,)), ((), ())), preferred_element_type=jnp.float32
    )


def cross_cols(left_side, right_side):
    return lax.dot_general(
        left_side, right_side, (((1,), (1,)), ((), ())), preferred_element_type=jnp.float32
    )


def take_group(tensor, offset, per_group, axis_pos):
    return lax.dynamic_slice_in_dim(tensor, offset, per_group, axis_pos)


def place_group(tensor, fresh_part, offset, is_valid, axis_pos):
    old_part = lax.dynamic_slice_in_dim(tensor, offset, fresh_part.shape[axis_pos], axis_pos)
    return lax.dynamic_update_slice_in_dim(
        tensor, jnp.where(is_valid, fresh_part, old_part), offset, axis_pos
    )


def chain_forward(
    start_w,
    start_b,
    start_tag,
    q_heads,
    k_heads,
    v_heads,
    lr_heads,
    block_tags,
    init_w,
    init_b,
    norm_gain,
    norm_shift,
):

    def advance(state_in, block_in):
        w_mat, b_vec, last_tag = state_in
        q_rows, k_rows, v_rows, lr_rows, blk_tag = block_in
        is_fresh = blk_tag != last_tag[0]
        w_mat = jnp.where(is_fresh, init_w, w_mat)
        b_vec = jnp.where(is_fresh, init_b, b_vec)
        w_next, b_next, out_rows = inner_step(
            w_mat, b_vec, q_rows, k_rows, v_rows, lr_rows, norm_gain, norm_shift
        )
        return ((w_next, b_next, jnp.reshape(blk_tag, (1,))), (out_rows, w_mat, b_vec, is_fresh))

    return lax.scan(
        advance, (start_w, start_b, start_tag), (q_heads, k_heads, v_heads, lr_heads, block_tags)
    )


def chain_backward(
    adj_w,
    adj_b,
    kept_w,
    kept_b,
    fresh_flags,
    q_heads,
    k_heads,
    v_heads,
    lr_heads,
    out_grads,
    norm_gain,
    norm_shift,
):

    def retreat(state_in, block_in):
        grad_w, grad_b, sum_w0, sum_b0, sum_gain, sum_shift = state_in
        w_mat, b_vec, is_fresh, q_rows, k_rows, v_rows, lr_rows, out_grad = block_in
        _, pullback = jax.vjp(
            inner_step, w_mat, b_vec, q_rows, k_rows, v_rows, lr_rows, norm_gain, norm_shift
        )
        back_w, back_b, back_q, back_k, back_v, back_lr, back_gain, back_shift = pullback(
            (grad_w, grad_b, out_grad)
        )
        zero_w = jnp.zeros_like(back_w)
        zero_b = jnp.zeros_like(back_b)
        sum_w0 = sum_w0 + jnp.where(is_fresh, back_w, zero_w)
        sum_b0 = sum_b0 + jnp.where(is_fresh, back_b, zero_b)
        grad_w = jnp.where(is_fresh, zero_w, back_w)
        grad_b = jnp.where(is_fresh, zero_b, back_b)
        carried = (grad_w, grad_b, sum_w0, sum_b0, sum_gain + back_gain, sum_shift + back_shift)
        return (carried, (back_q, back_k, back_v, back_lr))

    start_state = (
        adj_w,
        adj_b,
        jnp.zeros_like(adj_w),
        jnp.zeros_like(adj_b),
        jnp.zeros_like(norm_gain),
        jnp.zeros_like(norm_shift),
    )
    return lax.scan(
        retreat,
        start_state,
        (kept_w, kept_b, fresh_flags, q_heads, k_heads, v_heads, lr_heads, out_grads),
        reverse=True,
    )


def on_device(
    tokens,
    segments,
    norm_one,
    w_qkv,
    w_lr,
    lr_bias,
    w_gate,
    w_out,
    w_init,
    b_init,
    tnorm_w,
    tnorm_b,
    post_w,
    post_b,
    norm_two,
    w_gate_up,
    w_down,
    grad_out,
):
    floats = jnp.float32
    halves = jnp.bfloat16
    blocks = SPAN // MB
    inputs = tokens[0].astype(floats)
    gathered = (
        lax.all_gather(w_qkv, ("dp", "seq"), axis=0, tiled=True),
        lax.all_gather(w_lr, ("dp", "seq"), axis=0, tiled=True),
        lax.all_gather(w_gate, ("dp", "seq"), axis=0, tiled=True),
        lax.all_gather(w_out, ("dp", "seq"), axis=0, tiled=True),
        lax.all_gather(norm_one, ("dp", "seq"), axis=0, tiled=True),
        lax.all_gather(w_init, ("dp", "seq"), axis=0, tiled=True),
        lax.all_gather(b_init, ("dp", "seq"), axis=0, tiled=True),
        lax.all_gather(tnorm_w, ("dp", "seq"), axis=0, tiled=True),
        lax.all_gather(tnorm_b, ("dp", "seq"), axis=0, tiled=True),
        lax.all_gather(post_w, ("dp", "seq"), axis=0, tiled=True),
        lax.all_gather(post_b, ("dp", "seq"), axis=0, tiled=True),
    )
    gain_one = gathered[4].astype(floats)
    init_w = gathered[5].astype(floats).reshape(H, HD, HD)
    init_b = gathered[6].astype(floats).reshape(H, HD)
    norm_gain = gathered[7].astype(floats).reshape(H, HD)
    norm_shift = gathered[8].astype(floats).reshape(H, HD)
    post_gain = gathered[9].astype(floats)
    post_shift = gathered[10].astype(floats)
    scale_one = lax.rsqrt(jnp.mean(inputs * inputs, -1, keepdims=True) + EPSILON)
    normed_in = inputs * scale_one
    x_one = (normed_in * gain_one).astype(halves)
    qkv_rows = jnp.dot(x_one, gathered[0], preferred_element_type=floats)
    lr_logit = jnp.dot(x_one, gathered[1], preferred_element_type=floats) + lr_bias.astype(floats)
    gate_pre = jnp.dot(x_one, gathered[2], preferred_element_type=floats)
    lr_sigm = jax.nn.sigmoid(lr_logit)
    lr_rate = BASE_RATE * lr_sigm / HD

    def split_heads(tensor):
        return tensor.reshape(blocks, MB, H, HD).transpose(0, 2, 1, 3)

    def merge_heads(tensor):
        return tensor.transpose(0, 2, 1, 3).reshape(SPAN, D)

    q_heads = split_heads(qkv_rows[:, :D])
    k_heads = split_heads(qkv_rows[:, D : 2 * D])
    v_heads = split_heads(qkv_rows[:, 2 * D :])
    lr_heads = lr_rate.reshape(blocks, MB, H).transpose(0, 2, 1)
    block_tags = (segments[0].reshape(blocks, MB)[:, 0] + 1).astype(floats)
    seq_count = lax.axis_size("seq")
    seq_place = lax.axis_index("seq")
    zero_w = jnp.zeros((H, HD, HD), floats)
    zero_b = jnp.zeros((H, HD), floats)
    zero_tag = jnp.zeros((1,), floats)
    groups = math.gcd(H, seq_count)
    per_group = H // groups

    def forward_turn(step_turn, state_in):
        recv_w, recv_b, recv_tag, head_outs, kept_w, kept_b, fresh_flags = state_in
        group_id = step_turn - seq_place
        is_valid = (group_id >= 0) & (group_id < groups)
        offset = jnp.clip(group_id, 0, groups - 1) * per_group
        ending, kept_run = chain_forward(
            recv_w,
            recv_b,
            recv_tag,
            take_group(q_heads, offset, per_group, 1),
            take_group(k_heads, offset, per_group, 1),
            take_group(v_heads, offset, per_group, 1),
            take_group(lr_heads, offset, per_group, 1),
            block_tags,
            take_group(init_w, offset, per_group, 0),
            take_group(init_b, offset, per_group, 0),
            take_group(norm_gain, offset, per_group, 0),
            take_group(norm_shift, offset, per_group, 0),
        )
        head_outs = place_group(head_outs, kept_run[0], offset, is_valid, 1)
        kept_w = place_group(kept_w, kept_run[1], offset, is_valid, 1)
        kept_b = place_group(kept_b, kept_run[2], offset, is_valid, 1)
        fresh_flags = jnp.where(is_valid, kept_run[3], fresh_flags)
        sent_state = shifted((ending[0], ending[1], ending[2]), "seq", 1)
        return (sent_state[0], sent_state[1], sent_state[2], head_outs, kept_w, kept_b, fresh_flags)

    start_state = (
        jnp.zeros((per_group, HD, HD), floats),
        jnp.zeros((per_group, HD), floats),
        zero_tag,
        jnp.zeros((blocks, H, MB, HD), floats),
        jnp.zeros((blocks, H, HD, HD), floats),
        jnp.zeros((blocks, H, HD), floats),
        jnp.zeros((blocks,), jnp.bool_),
    )
    final_state = lax.fori_loop(0, groups + seq_count - 1, forward_turn, start_state)
    head_outs, kept_w, kept_b, fresh_flags = (
        final_state[3],
        final_state[4],
        final_state[5],
        final_state[6],
    )
    ttt_mixed = merge_heads(head_outs)
    out_hat, out_scale = normalize(ttt_mixed)
    normed_out = out_hat * post_gain + post_shift
    gelu_gate = jax.nn.gelu(gate_pre)
    gated_unit = (gelu_gate * normed_out).astype(halves)
    residual = inputs + jnp.dot(gated_unit, gathered[3], preferred_element_type=floats)
    outer = (
        lax.all_gather(norm_two, ("dp", "seq"), axis=0, tiled=True),
        lax.all_gather(w_gate_up, ("dp", "seq"), axis=0, tiled=True),
        lax.all_gather(w_down, ("dp", "seq"), axis=0, tiled=True),
    )
    scale_two = lax.rsqrt(jnp.mean(residual * residual, -1, keepdims=True) + EPSILON)
    normed_mid = residual * scale_two
    x_two = (normed_mid * outer[0].astype(floats)).astype(halves)
    gate_up = jnp.dot(x_two, outer[1], preferred_element_type=floats)
    gate_part = gate_up[:, :FF]
    up_part = gate_up[:, FF:]
    silu_sig = jax.nn.sigmoid(gate_part)
    silu_val = jax.nn.silu(gate_part)
    hidden = (silu_val * up_part).astype(halves)
    result = residual + jnp.dot(hidden, outer[2], preferred_element_type=floats)
    back_mlp = (
        lax.all_gather(norm_two, ("dp", "seq"), axis=0, tiled=True),
        lax.all_gather(w_gate_up, ("dp", "seq"), axis=0, tiled=True),
        lax.all_gather(w_down, ("dp", "seq"), axis=0, tiled=True),
    )
    d_top = grad_out[0]
    g_down_term = cross_rows(hidden, d_top)
    d_hidden = cross_cols(d_top, back_mlp[2])
    d_gate = d_hidden * up_part * silu_sig * (1.0 + gate_part * (1.0 - silu_sig))
    d_up = d_hidden * silu_val
    d_gate_up = jnp.concatenate([d_gate, d_up], axis=1).astype(halves)
    g_gu_term = cross_rows(x_two, d_gate_up)
    d_xtwo = cross_cols(d_gate_up, back_mlp[1])
    g_two_term = jnp.sum(d_xtwo * normed_mid, axis=0)
    d_mid = d_xtwo * back_mlp[0].astype(floats)
    d_residual = d_top.astype(floats) + scale_two * (
        d_mid - normed_mid * jnp.mean(d_mid * normed_mid, -1, keepdims=True)
    )
    mlp_grads = (
        lax.psum_scatter(g_two_term, ("dp", "seq"), scatter_dimension=0, tiled=True),
        lax.psum_scatter(g_gu_term, ("dp", "seq"), scatter_dimension=0, tiled=True),
        lax.psum_scatter(g_down_term, ("dp", "seq"), scatter_dimension=0, tiled=True),
    )
    again = (
        lax.all_gather(w_qkv, ("dp", "seq"), axis=0, tiled=True),
        lax.all_gather(w_lr, ("dp", "seq"), axis=0, tiled=True),
        lax.all_gather(w_gate, ("dp", "seq"), axis=0, tiled=True),
        lax.all_gather(w_out, ("dp", "seq"), axis=0, tiled=True),
    )
    d_branch = d_residual.astype(halves)
    g_out_term = cross_rows(gated_unit, d_branch)
    d_unit = cross_cols(d_branch, again[3])
    d_normed = d_unit * gelu_gate
    g_pw_term = jnp.sum(d_normed * out_hat, axis=0)
    g_pb_term = jnp.sum(d_normed, axis=0)
    d_hat = d_normed * post_gain
    d_mixed = out_scale * (
        d_hat
        - jnp.mean(d_hat, -1, keepdims=True)
        - out_hat * jnp.mean(d_hat * out_hat, -1, keepdims=True)
    )
    _, gelu_pull = jax.vjp(jax.nn.gelu, gate_pre)
    d_gate_pre = gelu_pull(d_unit * normed_out)[0].astype(halves)
    out_grads = split_heads(d_mixed)

    def backward_turn(step_turn, state_in):
        recv_w, recv_b, sum_w0, sum_b0, sum_gain, sum_shift, back_q, back_k, back_v, back_lr = (
            state_in
        )
        group_id = step_turn - (seq_count - 1 - seq_place)
        is_valid = (group_id >= 0) & (group_id < groups)
        offset = jnp.clip(group_id, 0, groups - 1) * per_group
        ending, per_block = chain_backward(
            recv_w,
            recv_b,
            take_group(kept_w, offset, per_group, 1),
            take_group(kept_b, offset, per_group, 1),
            fresh_flags,
            take_group(q_heads, offset, per_group, 1),
            take_group(k_heads, offset, per_group, 1),
            take_group(v_heads, offset, per_group, 1),
            take_group(lr_heads, offset, per_group, 1),
            take_group(out_grads, offset, per_group, 1),
            take_group(norm_gain, offset, per_group, 0),
            take_group(norm_shift, offset, per_group, 0),
        )
        sum_w0 = place_group(sum_w0, ending[2], offset, is_valid, 0)
        sum_b0 = place_group(sum_b0, ending[3], offset, is_valid, 0)
        sum_gain = place_group(sum_gain, ending[4], offset, is_valid, 0)
        sum_shift = place_group(sum_shift, ending[5], offset, is_valid, 0)
        back_q = place_group(back_q, per_block[0], offset, is_valid, 1)
        back_k = place_group(back_k, per_block[1], offset, is_valid, 1)
        back_v = place_group(back_v, per_block[2], offset, is_valid, 1)
        back_lr = place_group(back_lr, per_block[3], offset, is_valid, 1)
        sent_state = shifted((ending[0], ending[1]), "seq", -1)
        return (
            sent_state[0],
            sent_state[1],
            sum_w0,
            sum_b0,
            sum_gain,
            sum_shift,
            back_q,
            back_k,
            back_v,
            back_lr,
        )

    start_state = (
        jnp.zeros((per_group, HD, HD), floats),
        jnp.zeros((per_group, HD), floats),
        zero_w,
        zero_b,
        zero_b,
        zero_b,
        jnp.zeros((blocks, H, MB, HD), floats),
        jnp.zeros((blocks, H, MB, HD), floats),
        jnp.zeros((blocks, H, MB, HD), floats),
        jnp.zeros((blocks, H, MB), floats),
    )
    final_state = lax.fori_loop(0, groups + seq_count - 1, backward_turn, start_state)
    sum_w0, sum_b0, sum_gain, sum_shift = (
        final_state[2],
        final_state[3],
        final_state[4],
        final_state[5],
    )
    back_q, back_k, back_v, back_lr = (
        final_state[6],
        final_state[7],
        final_state[8],
        final_state[9],
    )
    back_qkv = jnp.concatenate(
        [merge_heads(back_q), merge_heads(back_k), merge_heads(back_v)], axis=1
    ).astype(halves)
    d_rate = back_lr.transpose(0, 2, 1).reshape(SPAN, H)
    d_logit = (d_rate * (BASE_RATE / HD) * lr_sigm * (1.0 - lr_sigm)).astype(halves)
    g_lr_bias = lax.psum(jnp.sum(d_logit.astype(floats), axis=0), ("dp", "seq"))
    g_qkv_term = cross_rows(x_one, back_qkv)
    g_lr_term = cross_rows(x_one, d_logit)
    g_gate_term = cross_rows(x_one, d_gate_pre)
    d_xone = (
        cross_cols(back_qkv, again[0])
        + cross_cols(d_logit, again[1])
        + cross_cols(d_gate_pre, again[2])
    )
    g_one_term = jnp.sum(d_xone * normed_in, axis=0)
    d_inner = d_xone * gain_one
    d_tokens = d_residual + scale_one * (
        d_inner - normed_in * jnp.mean(d_inner * normed_in, -1, keepdims=True)
    )
    ttt_grads = (
        lax.psum_scatter(g_one_term, ("dp", "seq"), scatter_dimension=0, tiled=True),
        lax.psum_scatter(g_qkv_term, ("dp", "seq"), scatter_dimension=0, tiled=True),
        lax.psum_scatter(g_lr_term, ("dp", "seq"), scatter_dimension=0, tiled=True),
        lax.psum_scatter(g_gate_term, ("dp", "seq"), scatter_dimension=0, tiled=True),
        lax.psum_scatter(g_out_term, ("dp", "seq"), scatter_dimension=0, tiled=True),
        lax.psum_scatter(sum_w0.reshape(D, HD), ("dp", "seq"), scatter_dimension=0, tiled=True),
        lax.psum_scatter(sum_b0.reshape(D), ("dp", "seq"), scatter_dimension=0, tiled=True),
        lax.psum_scatter(sum_gain.reshape(D), ("dp", "seq"), scatter_dimension=0, tiled=True),
        lax.psum_scatter(sum_shift.reshape(D), ("dp", "seq"), scatter_dimension=0, tiled=True),
        lax.psum_scatter(g_pw_term, ("dp", "seq"), scatter_dimension=0, tiled=True),
        lax.psum_scatter(g_pb_term, ("dp", "seq"), scatter_dimension=0, tiled=True),
    )
    return (
        result.astype(halves)[None],
        d_tokens.astype(halves)[None],
        ttt_grads[0],
        ttt_grads[1],
        ttt_grads[2],
        g_lr_bias,
        ttt_grads[3],
        ttt_grads[4],
        ttt_grads[5],
        ttt_grads[6],
        ttt_grads[7],
        ttt_grads[8],
        ttt_grads[9],
        ttt_grads[10],
        mlp_grads[0],
        mlp_grads[1],
        mlp_grads[2],
    )


def solution(mesh):
    placed = (
        P("dp", "seq", None),
        P("dp", "seq"),
        P(("dp", "seq")),
        P(("dp", "seq"), None),
        P(("dp", "seq"), None),
        P(),
        P(("dp", "seq"), None),
        P(("dp", "seq"), None),
        P(("dp", "seq"), None),
        P(("dp", "seq")),
        P(("dp", "seq")),
        P(("dp", "seq")),
        P(("dp", "seq")),
        P(("dp", "seq")),
        P(("dp", "seq")),
        P(("dp", "seq"), None),
        P(("dp", "seq"), None),
        P("dp", "seq", None),
    )
    return jax.shard_map(
        on_device,
        mesh=mesh,
        in_specs=placed,
        out_specs=(
            P("dp", "seq", None),
            P("dp", "seq", None),
            P(("dp", "seq")),
            P(("dp", "seq"), None),
            P(("dp", "seq"), None),
            P(),
            P(("dp", "seq"), None),
            P(("dp", "seq"), None),
            P(("dp", "seq"), None),
            P(("dp", "seq")),
            P(("dp", "seq")),
            P(("dp", "seq")),
            P(("dp", "seq")),
            P(("dp", "seq")),
            P(("dp", "seq")),
            P(("dp", "seq"), None),
            P(("dp", "seq"), None),
        ),
        check_vma=False,
    )
```

profile of v0, /device:TPU:9, one launch (start us, length us, event | category | flops | bytes accessed | tf_op | source)
XLA Modules:
  0.0 5734.1 jit_solution(955072608608746165)
XLA Ops:
  183.6 134.2 %all-gather.10.cloned.1.call-done = bf16[2048,6144]{1,0:T(8,128)(2,1)} async-done(((bf16[64,6144]{1,0:T(8,128)(2,1)}), bf16[2048,6144]{1,0:T(8,128)(2,1)}) %all-gather.10.cloned.1.call-update) | async-done | bytes 25165840 | tf_op jit(solution)/shard_map/all_gather | solution.py:193
  348.4 1066.2 %while.276 = (s32[]{:T(128)}, f32[4,64,64]{2,1,0:T(8,128)S(1)}, f32[4,64]{1,0:T(4,128)S(1)}, f32[1]{0:T(128)}, f32[8,32,16,64]{3,2,1,0:T(8,128)S(1)}, /*index=5*...) while((s32[]{:T(128)}, f32[4,64,64]{2,1,0:T(8,128)S(1)}, ...), condition=%wide.region_11.12_spmd.clone.clone, body=%wide.region_1.11_spmd.clone.sunk.clone | while | flops 11358912 | bytes 6498343 | solution.py:275
  354.2 51.7 while.275
  425.4 51.7 while.275
  496.3 51.7 while.275
  566.8 51.7 while.275
  643.7 51.7 while.275
  717.1 51.7 while.275
  790.0 51.7 while.275
  930.8 51.7 while.275
  1001.2 51.7 while.275
  1281.5 51.7 while.275
  1350.7 51.7 while.275
  1507.8 1862.2 %while.274 = (s32[]{:T(128)}, f32[4,64,64]{2,1,0:T(8,128)S(1)}, f32[4,64]{1,0:T(4,128)S(1)}, f32[32,64,64]{2,1,0:T(8,128)}, f32[32,64]{1,0:T(8,128)}, /*index=5*...) while((s32[]{:T(128)}, f32[4,64,64]{2,1,0:T(8,128)S(1)}, ...), condition=%wide.region_44.45_spmd.clone, body=%wide.region_18.44_spmd.sunk.clone | while | flops 30621804 | bytes 7187116 | solution.py:403
  1519.3 99.7 %while.273 = (s32[]{:T(128)}, f32[4,64,64]{2,1,0:T(8,128)S(1)}, f32[4,64]{1,0:T(4,128)S(1)}, f32[4,64,64]{2,1,0:T(8,128)S(1)}, f32[4,64]{1,0:T(4,128)}, /*index=...) while((s32[]{:T(128)}, f32[4,64,64]{2,1,0:T(8,128)S(1)}, ...), condition=%wide.region_43.43_spmd.clone, body=%wide.region_19.42_spmd.clone.sunk | while | flops 30505828 | bytes 2958302 | solution.py:160
  1645.4 99.7 %while.273 = (s32[]{:T(128)}, f32[4,64,64]{2,1,0:T(8,128)S(1)}, f32[4,64]{1,0:T(4,128)S(1)}, f32[4,64,64]{2,1,0:T(8,128)S(1)}, f32[4,64]{1,0:T(4,128)}, /*index=...) while((s32[]{:T(128)}, f32[4,64,64]{2,1,0:T(8,128)S(1)}, ...), condition=%wide.region_43.43_spmd.clone, body=%wide.region_19.42_spmd.clone.sunk | while | flops 30505828 | bytes 2958302 | solution.py:160
  1769.9 99.7 %while.273 = (s32[]{:T(128)}, f32[4,64,64]{2,1,0:T(8,128)S(1)}, f32[4,64]{1,0:T(4,128)S(1)}, f32[4,64,64]{2,1,0:T(8,128)S(1)}, f32[4,64]{1,0:T(4,128)}, /*index=...) while((s32[]{:T(128)}, f32[4,64,64]{2,1,0:T(8,128)S(1)}, ...), condition=%wide.region_43.43_spmd.clone, body=%wide.region_19.42_spmd.clone.sunk | while | flops 30505828 | bytes 2958302 | solution.py:160
  1893.8 99.7 %while.273 = (s32[]{:T(128)}, f32[4,64,64]{2,1,0:T(8,128)S(1)}, f32[4,64]{1,0:T(4,128)S(1)}, f32[4,64,64]{2,1,0:T(8,128)S(1)}, f32[4,64]{1,0:T(4,128)}, /*index=...) while((s32[]{:T(128)}, f32[4,64,64]{2,1,0:T(8,128)S(1)}, ...), condition=%wide.region_43.43_spmd.clone, body=%wide.region_19.42_spmd.clone.sunk | while | flops 30505828 | bytes 2958302 | solution.py:160
  2017.7 99.7 %while.273 = (s32[]{:T(128)}, f32[4,64,64]{2,1,0:T(8,128)S(1)}, f32[4,64]{1,0:T(4,128)S(1)}, f32[4,64,64]{2,1,0:T(8,128)S(1)}, f32[4,64]{1,0:T(4,128)}, /*index=...) while((s32[]{:T(128)}, f32[4,64,64]{2,1,0:T(8,128)S(1)}, ...), condition=%wide.region_43.43_spmd.clone, body=%wide.region_19.42_spmd.clone.sunk | while | flops 30505828 | bytes 2958302 | solution.py:160
  2141.7 99.7 %while.273 = (s32[]{:T(128)}, f32[4,64,64]{2,1,0:T(8,128)S(1)}, f32[4,64]{1,0:T(4,128)S(1)}, f32[4,64,64]{2,1,0:T(8,128)S(1)}, f32[4,64]{1,0:T(4,128)}, /*index=...) while((s32[]{:T(128)}, f32[4,64,64]{2,1,0:T(8,128)S(1)}, ...), condition=%wide.region_43.43_spmd.clone, body=%wide.region_19.42_spmd.clone.sunk | while | flops 30505828 | bytes 2958302 | solution.py:160
  2265.7 99.7 %while.273 = (s32[]{:T(128)}, f32[4,64,64]{2,1,0:T(8,128)S(1)}, f32[4,64]{1,0:T(4,128)S(1)}, f32[4,64,64]{2,1,0:T(8,128)S(1)}, f32[4,64]{1,0:T(4,128)}, /*index=...) while((s32[]{:T(128)}, f32[4,64,64]{2,1,0:T(8,128)S(1)}, ...), condition=%wide.region_43.43_spmd.clone, body=%wide.region_19.42_spmd.clone.sunk | while | flops 30505828 | bytes 2958302 | solution.py:160
  2389.7 99.7 %while.273 = (s32[]{:T(128)}, f32[4,64,64]{2,1,0:T(8,128)S(1)}, f32[4,64]{1,0:T(4,128)S(1)}, f32[4,64,64]{2,1,0:T(8,128)S(1)}, f32[4,64]{1,0:T(4,128)}, /*index=...) while((s32[]{:T(128)}, f32[4,64,64]{2,1,0:T(8,128)S(1)}, ...), condition=%wide.region_43.43_spmd.clone, body=%wide.region_19.42_spmd.clone.sunk | while | flops 30505828 | bytes 2958302 | solution.py:160
  2513.7 99.7 %while.273 = (s32[]{:T(128)}, f32[4,64,64]{2,1,0:T(8,128)S(1)}, f32[4,64]{1,0:T(4,128)S(1)}, f32[4,64,64]{2,1,0:T(8,128)S(1)}, f32[4,64]{1,0:T(4,128)}, /*index=...) while((s32[]{:T(128)}, f32[4,64,64]{2,1,0:T(8,128)S(1)}, ...), condition=%wide.region_43.43_spmd.clone, body=%wide.region_19.42_spmd.clone.sunk | while | flops 30505828 | bytes 2958302 | solution.py:160
  2637.7 99.7 %while.273 = (s32[]{:T(128)}, f32[4,64,64]{2,1,0:T(8,128)S(1)}, f32[4,64]{1,0:T(4,128)S(1)}, f32[4,64,64]{2,1,0:T(8,128)S(1)}, f32[4,64]{1,0:T(4,128)}, /*index=...) while((s32[]{:T(128)}, f32[4,64,64]{2,1,0:T(8,128)S(1)}, ...), condition=%wide.region_43.43_spmd.clone, body=%wide.region_19.42_spmd.clone.sunk | while | flops 30505828 | bytes 2958302 | solution.py:160
  2761.7 99.7 %while.273 = (s32[]{:T(128)}, f32[4,64,64]{2,1,0:T(8,128)S(1)}, f32[4,64]{1,0:T(4,128)S(1)}, f32[4,64,64]{2,1,0:T(8,128)S(1)}, f32[4,64]{1,0:T(4,128)}, /*index=...) while((s32[]{:T(128)}, f32[4,64,64]{2,1,0:T(8,128)S(1)}, ...), condition=%wide.region_43.43_spmd.clone, body=%wide.region_19.42_spmd.clone.sunk | while | flops 30505828 | bytes 2958302 | solution.py:160
  2885.7 99.7 %while.273 = (s32[]{:T(128)}, f32[4,64,64]{2,1,0:T(8,128)S(1)}, f32[4,64]{1,0:T(4,128)S(1)}, f32[4,64,64]{2,1,0:T(8,128)S(1)}, f32[4,64]{1,0:T(4,128)}, /*index=...) while((s32[]{:T(128)}, f32[4,64,64]{2,1,0:T(8,128)S(1)}, ...), condition=%wide.region_43.43_spmd.clone, body=%wide.region_19.42_spmd.clone.sunk | while | flops 30505828 | bytes 2958302 | solution.py:160
  3009.7 99.7 %while.273 = (s32[]{:T(128)}, f32[4,64,64]{2,1,0:T(8,128)S(1)}, f32[4,64]{1,0:T(4,128)S(1)}, f32[4,64,64]{2,1,0:T(8,128)S(1)}, f32[4,64]{1,0:T(4,128)}, /*index=...) while((s32[]{:T(128)}, f32[4,64,64]{2,1,0:T(8,128)S(1)}, ...), condition=%wide.region_43.43_spmd.clone, body=%wide.region_19.42_spmd.clone.sunk | while | flops 30505828 | bytes 2958302 | solution.py:160
  3133.6 99.7 %while.273 = (s32[]{:T(128)}, f32[4,64,64]{2,1,0:T(8,128)S(1)}, f32[4,64]{1,0:T(4,128)S(1)}, f32[4,64,64]{2,1,0:T(8,128)S(1)}, f32[4,64]{1,0:T(4,128)}, /*index=...) while((s32[]{:T(128)}, f32[4,64,64]{2,1,0:T(8,128)S(1)}, ...), condition=%wide.region_43.43_spmd.clone, body=%wide.region_19.42_spmd.clone.sunk | while | flops 30505828 | bytes 2958302 | solution.py:160
  3257.5 99.7 %while.273 = (s32[]{:T(128)}, f32[4,64,64]{2,1,0:T(8,128)S(1)}, f32[4,64]{1,0:T(4,128)S(1)}, f32[4,64,64]{2,1,0:T(8,128)S(1)}, f32[4,64]{1,0:T(4,128)}, /*index=...) while((s32[]{:T(128)}, f32[4,64,64]{2,1,0:T(8,128)S(1)}, ...), condition=%wide.region_43.43_spmd.clone, body=%wide.region_19.42_spmd.clone.sunk | while | flops 30505828 | bytes 2958302 | solution.py:160
  3484.9 820.2 %fusion = f32[176,2048]{1,0:T(8,128)} fusion(f32[5504,2048]{1,0:T(8,128)} %fusion.134), kind=kCustom, calls=%all-reduce-scatter | all-reduce-scatter fusion | flops 11534337 | bytes 46530560
  4412.6 365.6 %reduce-scatter.11.cloned.1.call-done = f32[64,6144]{1,0:T(8,128)} async-done(((f32[2048,6144]{1,0:T(8,128)}), f32[64,6144]{1,0:T(8,128)}) %reduce-scatter.11.cloned.1.call-update) | async-done | bytes 1572880 | tf_op jit(solution)/shard_map/reduce_scatter | solution.py:437
  4778.2 949.2 %reduce-scatter.19.cloned.1.call-done = f32[64,11008]{1,0:T(8,128)} async-done(((f32[2048,11008]{1,0:T(8,128)}), f32[64,11008]{1,0:T(8,128)}) %reduce-scatter.19.cloned.1.call-update) | async-done | bytes 2818064 | tf_op jit(solution)/shard_map/reduce_scatter | solution.py:323
  (10988 shorter events, 3445.3 us)
Async XLA Ops:
  7.2 154.1 %all-gather.16.cloned.1.call-start = ((), (), s32[]{:S(2)}) async-start(), calls=%async_computation.15 | async-start | bytes 23789568 | tf_op jit(solution)/shard_map/all_gather | solution.py:291
  7.9 309.8 %all-gather.10.cloned.1.call-start = ((), (), s32[]{:S(2)}) async-start(), calls=%async_computation.7 | async-start | bytes 25952256 | tf_op jit(solution)/shard_map/all_gather | solution.py:193
  8.7 1410.9 %all-gather.8.cloned.1.call-start = ((), (), s32[]{:S(2)}) async-start(), calls=%async_computation.6 | async-start | bytes 8650752 | tf_op jit(solution)/shard_map/all_gather | solution.py:195
  9.4 1416.7 %all-gather.12.cloned.1.call-start = ((), (), s32[]{:S(2)}) async-start(), calls=%async_computation.8 | async-start | bytes 8650752 | tf_op jit(solution)/shard_map/all_gather | solution.py:196
  10.0 1421.2 %all-gather.14.cloned.1.call-start = ((), (), s32[]{:S(2)}) async-start(), calls=%async_computation.9 | async-start | bytes 46497792 | tf_op jit(solution)/shard_map/all_gather | solution.py:290
  10.6 4389.6 %reduce-scatter.21.cloned.1.call-start = ((), (), s32[]{:S(2)}) async-start(), calls=%async_computation.16 | async-start | bytes 1081344
  405.9 13.7 collective-permute-start.4
  477.1 13.4 collective-permute-start.4
  548.0 12.9 collective-permute-start.4
  618.5 19.2 collective-permute-start.4
  695.3 15.9 collective-permute-start.4
  768.8 15.3 collective-permute-start.4
  841.6 12.9 collective-permute-start.4
  982.4 12.9 collective-permute-start.4
  1052.9 12.9 collective-permute-start.4
  1123.3 12.9 collective-permute-start.4
  1262.8 12.9 collective-permute-start.4
  1619.1 15.0 collective-permute-start.1
  1745.2 13.3 collective-permute-start.1
  2117.4 12.9 collective-permute-start.1
  2365.4 12.9 collective-permute-start.1
  2489.4 12.8 collective-permute-start.1
  2613.4 12.9 collective-permute-start.1
  2737.4 12.9 collective-permute-start.1
  2861.4 12.9 collective-permute-start.1
  2985.4 12.9 collective-permute-start.1
  3375.1 1037.5 %reduce-scatter.17.cloned.1.call-start = ((), (), s32[]{:S(2)}) async-start(), calls=%async_computation.13 | async-start | bytes 1081344 | tf_op jit(solution)/shard_map/reduce_scatter | solution.py:441
  3375.8 1036.8 %reduce-scatter.15.cloned.1.call-start = ((), (), s32[]{:S(2)}) async-start(), calls=%async_computation.12 | async-start | bytes 17301504 | tf_op jit(solution)/shard_map/reduce_scatter | solution.py:440
  3384.1 1028.5 %reduce-scatter.13.cloned.1.call-start = ((), (), s32[]{:S(2)}) async-start(), calls=%async_computation.11 | async-start | bytes 17301504 | tf_op jit(solution)/shard_map/reduce_scatter | solution.py:439
  3393.6 1384.6 %reduce-scatter.11.cloned.1.call-start = ((), (), s32[]{:S(2)}) async-start(), calls=%async_computation.10 | async-start | bytes 51904512 | tf_op jit(solution)/shard_map/reduce_scatter | solution.py:437
  3431.0 2296.4 %reduce-scatter.19.cloned.1.call-start = ((), (), s32[]{:S(2)}) async-start(), calls=%async_computation.14 | async-start | bytes 92995584 | tf_op jit(solution)/shard_map/reduce_scatter | solution.py:323
  4307.4 94.2 %collective-permute-start.5 = (f32[124,2048]{1,0:T(8,128)}, f32[124,2048]{1,0:T(8,128)}, u32[]{:S(2)}, u32[]{:S(2)}) collective-permute-start(f32[124,2048]{1,0:T(8,128)} %slice.43), channel_id=1, source_target_pairs={{0,1},{1,2},{2,3},{3,4},{4,5},{5,6},{6,7},{7,8},{8,9},{9,10},{10,1... | collective-permute-start | bytes 3047432
  (587 other events, 8253.3 us)
Sparse Core Ops, SparseCore 0:
  10.9 150.3 all-gather.15
  164.3 153.3 all-gather.9
  320.8 77.5 all-gather.7
  401.2 76.4 all-gather.11
  480.4 248.6 all-gather.13
  3375.2 125.2 reduce-scatter.20
  3503.4 138.0 reduce-scatter.16
  3644.4 365.6 reduce-scatter.14
  4012.9 323.7 reduce-scatter.12
  4343.5 434.5 reduce-scatter.10
  4781.1 946.1 reduce-scatter.18
where the time goes:
time: 5780 us; the launch traced here: 5730 us
  waiting for transfers between devices  1470 us (25%)
  matrix products  1100 us (19%)
  blocking collectives  994 us (17%)
  other arithmetic  948 us (16%)
  local copies, waits for them, and re-layouts  816 us (14%)
  loops' own time  212 us (4%)
  starting transfers between devices  178 us (3%)
    reduce_scatter x1, waiting for transfers between devices, on_device(): lax.psum_scatter(g_gu_term, ('dp', 'seq'), scatter_dimension=0, tiled=True)  949 us
    unnamed x3, blocking collectives  908 us
    reduce_scatter x1, waiting for transfers between devices, on_device(): lax.psum_scatter(g_qkv_term, ('dp', 'seq'), scatter_dimension=0, tiled=True)  366 us
    dot_general x480, matrix products, inner_step(): jnp.einsum('hti,hij->htj', k_rows, w_mat, precision=PRECISE)  326 us
    dynamic_update_slice x480, other arithmetic, chain_forward(): lax.scan(advance, (start_w, start_b, start_tag), (q_heads, k_heads, v_hea...  254 us
    dynamic_slice x225, local copies, waits for them, and re-layouts, take_group(): return lax.dynamic_slice_in_dim(tensor, offset, per_group, axis_pos)  217 us
    dynamic_update_slice x135, other arithmetic, place_group(): lax.dynamic_update_slice_in_dim(tensor, jnp.where(is_valid, fresh_part, o...  202 us
    ppermute x75, starting transfers between devices, shifted(): return lax.ppermute(array, axis, pairs)  173 us

commit v1 on v0

v1 whole, which is shorter than its diff:
```python
import functools
import jax
import jax.numpy as jnp
from jax import lax
from jax.experimental import pallas as pl
from jax.experimental.pallas import tpu as pltpu
from jax.sharding import PartitionSpec as P

HD = 64
MB = 16
PER = 8
EPSILON = 1e-06


def nn(left, right):
    return lax.dot_general(left, right, (((1,), (0,)), ((), ())), preferred_element_type=jnp.float32)


def nt(left, right):
    return lax.dot_general(left, right, (((1,), (1,)), ((), ())), preferred_element_type=jnp.float32)


def tn(left, right):
    return lax.dot_general(left, right, (((0,), (0,)), ((), ())), preferred_element_type=jnp.float32)


def halves(value):
    high = value.astype(jnp.bfloat16)
    return high, (value - high.astype(jnp.float32)).astype(jnp.bfloat16)


def head_masks(heads):
    ht, hi = heads * MB, heads * HD

    def iota(shape, axis):
        return lax.broadcasted_iota(jnp.int32, shape, axis)

    own = (iota((ht, hi), 0) // MB == iota((ht, hi), 1) // HD).astype(jnp.float32)
    unit = (iota((HD, hi), 0) == iota((HD, hi), 1) % HD).astype(jnp.bfloat16)
    row, col = iota((ht, ht), 0), iota((ht, ht), 1)
    same = (row // MB == col // MB).astype(jnp.bfloat16)
    ts, tt = row % MB, col % MB
    later = jnp.where((row // MB == col // MB) & (ts <= tt), MB / (tt + 1).astype(jnp.float32), 0.0)
    earlier = jnp.where((row // MB == col // MB) & (tt <= ts), MB / (ts + 1).astype(jnp.float32), 0.0)
    return own, unit, same, later, earlier


def spread(rows, own, heads):
    return (jnp.concatenate([rows] * heads, axis=0) * own).astype(jnp.bfloat16)


def fold(values, heads):
    total = values[:MB]
    for h in range(1, heads):
        total = total + values[h * MB : (h + 1) * MB]
    return total


def turned(rows, own, unit, heads):
    wide = jnp.concatenate([rows] * heads, axis=0) * own
    high, low = halves(wide)
    return nt(unit, high) + nt(unit, low)


def mean0(value):
    return jnp.sum(value, axis=0, keepdims=True) * (1.0 / HD)


def forward_kernel(heads, per, fresh_ref, qkv_ref, e_ref, w0_ref, c0_ref, gain_ref, shift_ref,
                   mixed_ref, wsave_ref, hat_ref, slope_ref, gap_ref, bar_ref, rows_ref, w_ref, c_ref):
    hi = heads * HD
    own, unit, same, later, _ = head_masks(heads)
    gain, shift, w0, c0 = gain_ref[...], shift_ref[...], w0_ref[...], c0_ref[...]
    gain2 = gain * gain

    @pl.when(pl.program_id(0) == 0)
    def _():
        w_ref[...] = jnp.zeros_like(w_ref)
        c_ref[...] = jnp.zeros_like(c_ref)

    w, c = w_ref[...], c_ref[...]
    for b in range(per):
        is_fresh = fresh_ref[pl.program_id(0) * per + b] != 0
        lines = slice(b * MB, (b + 1) * MB)
        q, k, v = qkv_ref[lines, :hi], qkv_ref[lines, hi : 2 * hi], qkv_ref[lines, 2 * hi :]
        e = e_ref[b]
        kb, qb = spread(k, own, heads), spread(q, own, heads)
        gap = shift - turned(v - k, own, unit, heads)
        base = gain * gap
        w = jnp.where(is_fresh, w0, w)
        c = jnp.where(is_fresh, c0, c)
        wb = w.astype(jnp.bfloat16)
        wsave_ref[b] = wb
        z = nt(wb, kb) + c
        gz = gain2 * z
        s = lax.rsqrt(mean0(z * z) + EPSILON)
        mean_g = s * mean0(gz) + mean0(base)
        mean_gx = s * (s * mean0(gz * z) + mean0(base * z))
        hat = s * z
        slope = s * (gain2 * hat + base - mean_g - hat * mean_gx)
        eb = (e * slope).astype(jnp.bfloat16)
        mix = (later * (nt(kb, qb) + 1.0)).astype(jnp.bfloat16)
        zbar = nt(wb, qb) + c - nn(eb, mix)
        w = w - nn(eb, kb)
        c = c - nn(eb, same)
        sbar = lax.rsqrt(mean0(zbar * zbar) + EPSILON)
        bar = zbar * sbar
        high, low = halves(gain * bar + shift)
        mixed_ref[lines, :] = q + fold((tn(high, unit) + tn(low, unit)) * own, heads)
        hat_ref[b] = hat
        slope_ref[b] = slope
        gap_ref[b] = gap
        bar_ref[b] = bar
        rows_ref[b] = jnp.concatenate([s, sbar, mean_g, mean_gx], axis=0)
    w_ref[...] = w
    c_ref[...] = c


def inner_forward(fresh, qkv, e_rows, w0, c0, gain, shift):
    tokens, heads = qkv.shape[0], qkv.shape[1] // (3 * HD)
    ht, hi = heads * MB, heads * HD
    blocks = tokens // MB
    per = PER
    f32 = jnp.float32
    whole = lambda shape: pl.BlockSpec(shape, lambda i: (0, 0))
    save = pl.BlockSpec((per, HD, ht), lambda i: (i, 0, 0))
    return pl.pallas_call(
        functools.partial(forward_kernel, heads, per),
        grid=(blocks // per,),
        in_specs=[
            pl.BlockSpec(memory_space=pltpu.SMEM),
            pl.BlockSpec((per * MB, 3 * hi), lambda i: (i, 0)),
            pl.BlockSpec((per, 1, ht), lambda i: (i, 0, 0)),
            whole((HD, hi)), whole((HD, ht)), whole((HD, ht)), whole((HD, ht)),
        ],
        out_specs=[
            pl.BlockSpec((per * MB, hi), lambda i: (i, 0)),
            pl.BlockSpec((per, HD, hi), lambda i: (i, 0, 0)),
            save, save, save, save,
            pl.BlockSpec((per, 4, ht), lambda i: (i, 0, 0)),
        ],
        out_shape=[
            jax.ShapeDtypeStruct((tokens, hi), f32),
            jax.ShapeDtypeStruct((blocks, HD, hi), jnp.bfloat16),
        ] + [jax.ShapeDtypeStruct((blocks, HD, ht), f32)] * 4 + [jax.ShapeDtypeStruct((blocks, 4, ht), f32)],
        scratch_shapes=[pltpu.VMEM((HD, hi), f32), pltpu.VMEM((HD, ht), f32)],
        compiler_params=pltpu.CompilerParams(vmem_limit_bytes=48 * 1024 * 1024),
        name="inner_forward",
    )(fresh, qkv, e_rows, w0, c0, gain, shift)


def backward_kernel(heads, per, fresh_ref, qkv_ref, e_ref, dmix_ref, wsave_ref, hat_ref, slope_ref, gap_ref,
                    bar_ref, rows_ref, gain_ref, shift_ref,
                    dqkv_ref, drate_ref, dw0_ref, dc0_ref, dgain_ref, dshift_ref, a_ref, ac_ref):
    hi, ht = heads * HD, heads * MB
    own, unit, same, later, earlier = head_masks(heads)
    gain = gain_ref[...]
    gain2 = gain * gain
    step = pl.program_id(0)

    @pl.when(step == 0)
    def _():
        for ref in (a_ref, ac_ref, dw0_ref, dc0_ref, dgain_ref, dshift_ref):
            ref[...] = jnp.zeros_like(ref)

    a, ac = a_ref[...], ac_ref[...]
    dw0, dc0, dgain, dshift = dw0_ref[...], dc0_ref[...], dgain_ref[...], dshift_ref[...]
    for b in reversed(range(per)):
        is_fresh = fresh_ref[(pl.num_programs(0) - 1 - step) * per + b] != 0
        lines = slice(b * MB, (b + 1) * MB)
        q, k = qkv_ref[lines, :hi], qkv_ref[lines, hi : 2 * hi]
        e = e_ref[b]
        wb, hat, slope, gap, bar = wsave_ref[b], hat_ref[b], slope_ref[b], gap_ref[b], bar_ref[b]
        s, sbar, mean_g, mean_gx = (rows_ref[b][i : i + 1] for i in range(4))
        kb, qb = spread(k, own, heads), spread(q, own, heads)
        dout = dmix_ref[lines, :]
        dturn = turned(dout, own, unit, heads)
        head = gain * dturn
        dbar = sbar * (head - mean0(head) - bar * mean0(head * bar))
        dbarb = dbar.astype(jnp.bfloat16)
        scores = nt(qb, kb) + 1.0
        mix = earlier * scores
        s2 = s * s
        gh = gain2 * hat
        alpha = s2 * (gain2 - mean_gx)
        kappa = s2 * (gain2 * hat + gap * gain + gh)
        kappa1 = mean_g + mean0(gh)
        kappa2 = 2.0 * mean_gx + mean0(gh * hat)
        ab = a.astype(jnp.bfloat16)
        ka = nt(ab, kb) + ac
        u = -e * (ka + nn(dbarb, mix.astype(jnp.bfloat16)))
        ug = gain2 * u
        r2 = mean0(u * hat)
        r3 = mean0(ug)
        r4 = mean0(ug * hat)
        r5 = mean0(u * slope)
        row1 = s2 * (r3 - r2 * kappa1)
        row2 = s2 * (r4 - r2 * kappa2) + s * r5
        dz = alpha * u - r2 * kappa - row1 - hat * row2
        dzb = dz.astype(jnp.bfloat16)
        dg = s * (u - hat * r2)
        a_next = a + nn(dbarb, qb) + nn(dzb, kb)
        ac_next = ac + nn(dbarb, same) + nn(dzb, same)
        dm = -tn(dbarb, slope.astype(jnp.bfloat16))
        ds = (earlier * e * dm).astype(jnp.bfloat16)
        drate_ref[b] = (jnp.sum(mix * dm, axis=0, keepdims=True) - jnp.sum(ka * slope, axis=0, keepdims=True)) * (1.0 / MB)
        dgb = (gain * dg)
        ndg = fold(tn(dgb.astype(jnp.bfloat16), unit) * own, heads)
        dq = dout + fold(tn(dbarb, wb) * own + nn(ds, kb), heads)
        dk = ndg + fold((tn(dzb, wb) - tn((e * slope).astype(jnp.bfloat16), ab)) * own + tn(ds, qb), heads)
        dqkv_ref[lines, :hi] = dq.astype(jnp.bfloat16)
        dqkv_ref[lines, hi : 2 * hi] = dk.astype(jnp.bfloat16)
        dqkv_ref[lines, 2 * hi :] = (-ndg).astype(jnp.bfloat16)
        dgain = dgain + dturn * bar + dg * (2.0 * gain * hat + gap)
        dshift = dshift + dturn + dgb
        dw0 = dw0 + jnp.where(is_fresh, a_next, 0.0)
        dc0 = dc0 + jnp.where(is_fresh, ac_next, 0.0)
        a = jnp.where(is_fresh, 0.0, a_next)
        ac = jnp.where(is_fresh, 0.0, ac_next)
    a_ref[...] = a
    ac_ref[...] = ac
    dw0_ref[...] = dw0
    dc0_ref[...] = dc0
    dgain_ref[...] = dgain
    dshift_ref[...] = dshift


def inner_backward(fresh, qkv, e_rows, dmix, saved, gain, shift):
    tokens, heads = qkv.shape[0], qkv.shape[1] // (3 * HD)
    ht, hi = heads * MB, heads * HD
    blocks = tokens // MB
    per = PER
    last = blocks // per - 1
    f32 = jnp.float32
    whole = lambda shape: pl.BlockSpec(shape, lambda i: (0, 0))
    three = lambda shape: pl.BlockSpec(shape, lambda i: (last - i, 0, 0))
    two = lambda shape: pl.BlockSpec(shape, lambda i: (last - i, 0))
    save = three((per, HD, ht))
    return pl.pallas_call(
        functools.partial(backward_kernel, heads, per),
        grid=(blocks // per,),
        in_specs=[
            pl.BlockSpec(memory_space=pltpu.SMEM),
            two((per * MB, 3 * hi)), three((per, 1, ht)), two((per * MB, hi)),
            three((per, HD, hi)), save, save, save, save, three((per, 4, ht)),
            whole((HD, ht)), whole((HD, ht)),
        ],
        out_specs=[
            two((per * MB, 3 * hi)), three((per, 1, ht)),
            whole((HD, hi)), whole((HD, ht)), whole((HD, ht)), whole((HD, ht)),
        ],
        out_shape=[
            jax.ShapeDtypeStruct((tokens, 3 * hi), jnp.bfloat16),
            jax.ShapeDtypeStruct((blocks, 1, ht), f32),
            jax.ShapeDtypeStruct((HD, hi), f32),
        ] + [jax.ShapeDtypeStruct((HD, ht), f32)] * 3,
        scratch_shapes=[pltpu.VMEM((HD, hi), f32), pltpu.VMEM((HD, ht), f32)],
        compiler_params=pltpu.CompilerParams(vmem_limit_bytes=48 * 1024 * 1024),
        name="inner_backward",
    )(fresh, qkv, e_rows, dmix, *saved, gain, shift)


def cross_rows(left_side, right_side):
    return lax.dot_general(left_side, right_side, (((0,), (0,)), ((), ())), preferred_element_type=jnp.float32)


def cross_cols(left_side, right_side):
    return lax.dot_general(left_side, right_side, (((1,), (1,)), ((), ())), preferred_element_type=jnp.float32)


def dot(left_side, right_side):
    return jnp.dot(left_side, right_side, preferred_element_type=jnp.float32)


def on_device(
    tokens,
    segments,
    norm_one,
    w_qkv,
    w_lr,
    lr_bias,
    w_gate,
    w_out,
    w_init,
    b_init,
    tnorm_w,
    tnorm_b,
    post_w,
    post_b,
    norm_two,
    w_gate_up,
    w_down,
    grad_out,
):
    floats = jnp.float32
    bf16 = jnp.bfloat16
    both = ("dp", "seq")
    packs, per_seq = lax.axis_size("dp"), lax.axis_size("seq")
    devices = packs * per_seq
    place = lax.axis_index("seq")
    span, width = tokens.shape[1], tokens.shape[2]
    rows = norm_one.shape[0]
    heads_all = lr_bias.shape[0]
    units = w_down.shape[0]
    length = span * per_seq
    blocks = length // MB
    heads = heads_all // per_seq
    aligned = rows % HD == 0
    outer = packs if aligned else 1
    inner = width // (outer * per_seq)
    mine = outer * inner

    def own_rows(array):
        cut = array.reshape((outer, per_seq, inner) + array.shape[1:])
        cut = lax.dynamic_index_in_dim(cut, place, 1, keepdims=False)
        return cut.reshape((mine,) + array.shape[1:])

    def put_rows(array):
        full = jnp.zeros((outer, per_seq, inner) + array.shape[1:], array.dtype)
        part = array.reshape((outer, 1, inner) + array.shape[1:])
        at = (0, place) + (0,) * (part.ndim - 2)
        return lax.dynamic_update_slice(full, part, at).reshape((width,) + array.shape[1:])

    def by_place(weight, parts, out, last):
        depth = weight.shape[0]
        cut = weight.reshape(depth, parts, out, per_seq, last).transpose(3, 0, 1, 2, 4)
        cut = cut.reshape(per_seq, depth, parts * out * last)
        return cut

    def gather_columns(cut):
        got = lax.all_to_all(cut, "seq", 0, 0, tiled=True)
        got = got.reshape(-1, cut.shape[-1])
        return lax.all_gather(got, "dp", axis=0, tiled=True)

    def return_columns(grad):
        got = lax.psum_scatter(grad, "dp", scatter_dimension=0, tiled=True)
        got = got.reshape(per_seq, -1, grad.shape[1])
        return lax.all_to_all(got, "seq", 0, 0, tiled=True)

    def columns_back(got, parts, out, last):
        depth = got.shape[1]
        got = got.reshape(per_seq, depth, parts, out, last).transpose(1, 2, 3, 0, 4)
        return got.reshape(depth, parts * out * per_seq * last)

    inputs = tokens[0].astype(floats)
    lanes = max(HD, heads_all)
    pad = lambda array: jnp.pad(array, ((0, 0), (0, lanes - array.shape[1])))
    tags = segments[0].reshape(span // MB, MB)[:, 0].astype(bf16)
    vectors = jnp.stack([norm_one, norm_two, b_init, tnorm_w, tnorm_b, post_w, post_b], axis=1)
    small = jnp.concatenate([pad(w_init), pad(w_lr), pad(vectors), pad(jnp.broadcast_to(tags[None], (8, span // MB)))], axis=0)
    small = lax.all_gather(small, both, axis=0)
    init_all = small[:, :rows, :HD].reshape(width, HD)
    lr_all = small[:, rows : 2 * rows, :heads_all].reshape(width, heads_all)
    vec_all = small[:, 2 * rows : 3 * rows, :7].reshape(width, 7)
    pack_tags = lax.dynamic_index_in_dim(
        small[:, 3 * rows, : span // MB].reshape(packs, blocks), lax.axis_index("dp"), 0, keepdims=False
    )
    fresh = jnp.concatenate([jnp.ones((1,), jnp.int32), (pack_tags[1:] != pack_tags[:-1]).astype(jnp.int32)])
    gain_one, gain_two = vec_all[:, 0].astype(floats), vec_all[:, 1].astype(floats)
    vec_own = own_rows(vec_all).astype(floats)
    post_gain, post_shift = vec_own[:, 5], vec_own[:, 6]
    lr_cols = lr_all.reshape(width, outer, per_seq, heads // outer)
    lr_own = lax.dynamic_index_in_dim(lr_cols, place, 2, keepdims=False).reshape(width, heads)
    bias_own = lax.dynamic_index_in_dim(lr_bias.reshape(outer, per_seq, heads // outer), place, 1, keepdims=False)
    bias_own = bias_own.reshape(heads).astype(floats)

    w_mix = gather_columns(
        jnp.concatenate([by_place(w_qkv, 3, outer, inner), by_place(w_gate, 1, outer, inner)], axis=2)
    )
    w_gu = gather_columns(by_place(w_gate_up, 2, packs, units))
    if aligned:
        w_o = lax.all_gather(w_out, "dp", axis=0, tiled=True)
    else:
        w_o = own_rows(lax.all_gather(w_out, both, axis=0, tiled=True))
    w_d = lax.all_gather(w_down, "dp", axis=0, tiled=True)
    d_top = lax.all_gather(grad_out[0], "seq", axis=0, tiled=True)

    scale_one = lax.rsqrt(jnp.mean(inputs * inputs, -1, keepdims=True) + EPSILON)
    normed_in = inputs * scale_one
    x_one = lax.all_gather((normed_in * gain_one).astype(bf16), "seq", axis=0, tiled=True)
    qkv = dot(x_one, w_mix[:, : 3 * mine])
    gate_pre = dot(x_one, w_mix[:, 3 * mine :])
    lr_sigm = jax.nn.sigmoid(dot(x_one, lr_own) + bias_own)
    e_rows = (lr_sigm * (1.0 / (HD * MB))).reshape(blocks, MB, heads).transpose(0, 2, 1).reshape(blocks, 1, heads * MB)

    def by_token(vector):
        return jnp.repeat(vector.reshape(heads, HD).T, MB, axis=1)

    init_w = own_rows(init_all).astype(floats).reshape(heads, HD, HD)
    init_w = (init_w - jnp.mean(init_w, -1, keepdims=True)).transpose(2, 0, 1).reshape(HD, heads * HD)
    init_b = vec_own[:, 2].reshape(heads, HD)
    init_b = (init_b - jnp.mean(init_b, -1, keepdims=True)).reshape(-1)
    gain_t, shift_t = by_token(vec_own[:, 3]), by_token(vec_own[:, 4])
    mixed, *saved = inner_forward(fresh, qkv, e_rows, init_w, by_token(init_b), gain_t, shift_t)

    mean_own = jnp.mean(mixed, -1)
    spread_own = jnp.sum((mixed - mean_own[:, None]) ** 2, -1)
    stats = lax.all_gather(jnp.stack([mean_own, spread_own]), "seq", axis=0)
    mean_all = jnp.mean(stats[:, 0], 0)
    var_all = (jnp.sum(stats[:, 1], 0) + mine * jnp.sum((stats[:, 0] - mean_all) ** 2, 0)) * (1.0 / width)
    out_scale = lax.rsqrt(var_all + EPSILON)[:, None]
    out_hat = (mixed - mean_all[:, None]) * out_scale
    normed_out = out_hat * post_gain + post_shift
    gelu_gate, gelu_pull = jax.vjp(jax.nn.gelu, gate_pre)
    gated_unit = (gelu_gate * normed_out).astype(bf16)
    branch = lax.psum_scatter(dot(gated_unit, w_o), "seq", scatter_dimension=0, tiled=True)
    residual = inputs + branch
    scale_two = lax.rsqrt(jnp.mean(residual * residual, -1, keepdims=True) + EPSILON)
    normed_mid = residual * scale_two
    x_two = lax.all_gather((normed_mid * gain_two).astype(bf16), "seq", axis=0, tiled=True)
    hidden_units = packs * units
    gate_up = dot(x_two, w_gu)
    gate_part, up_part = gate_up[:, :hidden_units], gate_up[:, hidden_units:]
    silu_sig = jax.nn.sigmoid(gate_part)
    silu_val = gate_part * silu_sig
    hidden = (silu_val * up_part).astype(bf16)
    down = lax.psum_scatter(dot(hidden, w_d), "seq", scatter_dimension=0, tiled=True)
    result = residual + down

    g_down = lax.psum_scatter(cross_rows(hidden, d_top), "dp", scatter_dimension=0, tiled=True)
    d_hidden = cross_cols(d_top, w_d)
    d_gate = d_hidden * up_part * silu_sig * (1.0 + gate_part * (1.0 - silu_sig))
    d_up = d_hidden * silu_val
    d_gate_up = jnp.concatenate([d_gate, d_up], axis=1).astype(bf16)
    d_xtwo = lax.psum_scatter(cross_cols(d_gate_up, w_gu), "seq", scatter_dimension=0, tiled=True)
    g_gate_up = return_columns(cross_rows(x_two, d_gate_up))
    g_gate_up = columns_back(g_gate_up, 2, packs, units)
    g_two = jnp.sum(d_xtwo * normed_mid, axis=0)
    d_mid = d_xtwo * gain_two
    d_residual = grad_out[0].astype(floats) + scale_two * (
        d_mid - normed_mid * jnp.mean(d_mid * normed_mid, -1, keepdims=True)
    )
    d_branch = lax.all_gather(d_residual.astype(bf16), "seq", axis=0, tiled=True)
    g_out = cross_rows(gated_unit, d_branch)
    if aligned:
        g_out = lax.psum_scatter(g_out, "dp", scatter_dimension=0, tiled=True)
    else:
        g_out = lax.psum_scatter(put_rows(g_out), both, scatter_dimension=0, tiled=True)
    d_unit = cross_cols(d_branch, w_o)
    d_normed = d_unit * gelu_gate
    g_post_w = jnp.sum(d_normed * out_hat, axis=0)
    g_post_b = jnp.sum(d_normed, axis=0)
    d_hat = d_normed * post_gain
    sums = lax.psum(jnp.stack([jnp.sum(d_hat, -1), jnp.sum(d_hat * out_hat, -1)]), "seq") * (1.0 / width)
    d_mixed = out_scale * (d_hat - sums[0][:, None] - out_hat * sums[1][:, None])
    d_gate_pre = gelu_pull(d_unit * normed_out)[0].astype(bf16)
    d_qkv, d_rate, d_w0, d_c0, d_gain, d_shift = inner_backward(fresh, qkv, e_rows, d_mixed, saved, gain_t, shift_t)
    d_rate = d_rate.reshape(blocks, heads, MB).transpose(0, 2, 1).reshape(length, heads)
    d_logit = (d_rate * (1.0 / HD) * lr_sigm * (1.0 - lr_sigm)).astype(bf16)
    d_mix = jnp.concatenate([d_qkv, d_gate_pre], axis=1)
    g_mix = return_columns(cross_rows(x_one, d_mix))
    g_qkv = columns_back(g_mix[:, :, : 3 * mine], 3, outer, inner)
    g_gate = columns_back(g_mix[:, :, 3 * mine :], 1, outer, inner)
    d_xone = lax.psum_scatter(
        cross_cols(d_mix, w_mix) + cross_cols(d_logit, lr_own), "seq", scatter_dimension=0, tiled=True
    )
    g_one = jnp.sum(d_xone * normed_in, axis=0)
    d_inner = d_xone * gain_one
    d_tokens = d_residual + scale_one * (
        d_inner - normed_in * jnp.mean(d_inner * normed_in, -1, keepdims=True)
    )

    def from_token(array):
        return jnp.sum(array.reshape(HD, heads, MB), -1).T.reshape(mine)

    g_vec = jnp.stack(
        [d_c0.reshape(HD, heads, MB)[:, :, 0].T.reshape(mine), from_token(d_gain), from_token(d_shift), g_post_w, g_post_b],
        axis=1,
    )
    g_vec = jnp.concatenate([jnp.stack([g_one, g_two], axis=1), put_rows(g_vec)], axis=1)
    g_init = put_rows(d_w0.reshape(HD, heads, HD).transpose(1, 2, 0).reshape(mine, HD))
    g_lr = cross_rows(x_one, d_logit).reshape(width, outer, 1, heads // outer)
    g_lr = lax.dynamic_update_slice(
        jnp.zeros((width, outer, per_seq, heads // outer), floats), g_lr, (0, 0, place, 0)
    ).reshape(width, heads_all)
    g_bias = jnp.sum(d_logit.astype(floats), axis=0).reshape(outer, 1, heads // outer)
    g_bias = lax.dynamic_update_slice(
        jnp.zeros((outer, per_seq, heads // outer), floats), g_bias, (0, place, 0)
    ).reshape(heads_all)
    wide = HD + heads_all + 7
    g_small = jnp.concatenate([g_init, g_lr, g_vec], axis=1).reshape(devices, rows, wide)
    g_last = jnp.broadcast_to(jnp.pad(g_bias, (0, wide - heads_all)), (devices, 8, wide))
    g_small = jnp.concatenate([g_small, g_last], axis=1)
    g_small = lax.psum_scatter(g_small, both, scatter_dimension=0, tiled=True)[0]
    g_vec = g_small[:rows, HD + heads_all :]
    return (
        result.astype(bf16)[None],
        d_tokens.astype(bf16)[None],
        g_vec[:, 0],
        g_qkv,
        g_small[:rows, HD : HD + heads_all],
        g_small[rows, :heads_all],
        g_gate,
        g_out,
        g_small[:rows, :HD],
        g_vec[:, 2],
        g_vec[:, 3],
        g_vec[:, 4],
        g_vec[:, 5],
        g_vec[:, 6],
        g_vec[:, 1],
        g_gate_up,
        g_down,
    )


def solution(mesh):
    placed = (
        P("dp", "seq", None),
        P("dp", "seq"),
        P(("dp", "seq")),
        P(("dp", "seq"), None),
        P(("dp", "seq"), None),
        P(),
        P(("dp", "seq"), None),
        P(("dp", "seq"), None),
        P(("dp", "seq"), None),
        P(("dp", "seq")),
        P(("dp", "seq")),
        P(("dp", "seq")),
        P(("dp", "seq")),
        P(("dp", "seq")),
        P(("dp", "seq")),
        P(("dp", "seq"), None),
        P(("dp", "seq"), None),
        P("dp", "seq", None),
    )
    return jax.shard_map(
        on_device,
        mesh=mesh,
        in_specs=placed,
        out_specs=(
            P("dp", "seq", None),
            P("dp", "seq", None),
            P(("dp", "seq")),
            P(("dp", "seq"), None),
            P(("dp", "seq"), None),
            P(),
            P(("dp", "seq"), None),
            P(("dp", "seq"), None),
            P(("dp", "seq"), None),
            P(("dp", "seq")),
            P(("dp", "seq")),
            P(("dp", "seq")),
            P(("dp", "seq")),
            P(("dp", "seq")),
            P(("dp", "seq")),
            P(("dp", "seq"), None),
            P(("dp", "seq"), None),
        ),
        check_vma=False,
    )
```

time: 5780 us -> 1370 us (0.24)
  matrix products: 1100 us -> 111 us
  other arithmetic: 948 us -> 23 us
  blocking collectives: 994 us -> 253 us
  local copies, waits for them, and re-layouts: 816 us -> 106 us
  waiting for transfers between devices: 1470 us -> 773 us
  loops' own time: 212 us -> 0 us
  starting transfers between devices: 178 us -> 15.1 us
  Pallas kernels: 0 us -> 65 us
    reduce_scatter x5 -> x7, waiting for transfers between devices: 1310 us -> 400 us  [the longest x1 134 us: on_device(): lax.psum_scatter(cross_cols(d_mix, w_mix) + cross_cols(d_logit, lr_own),...]
    dot_general x2286 -> x6, matrix products: 943 us -> 41.5 us  [dot(): return jnp.dot(left_side, right_side, preferred_element_type=jnp.float32)]
    unnamed x3 -> x1, blocking collectives: 908 us -> 67.9 us
    dynamic_update_slice x615 -> x0, other arithmetic: 456 us -> none  [the longest x480 254 us: chain_forward(): lax.scan(advance, (start_w, start_b, start_tag), (q_heads, k_heads, v_hea...]
    dynamic_slice x465 -> x3, local copies, waits for them, and re-layouts: 437 us -> 0.06 us  [the longest x1 0.04 us: on_device(): lax.dynamic_index_in_dim(lr_cols, place, 2, keepdims=False)]
    reduce_sum x1563 -> x12, other arithmetic: 335 us -> 6.1 us  [the longest x1 1.89 us: on_device(): g_two = jnp.sum(d_xtwo * normed_mid, axis=0)]
    another operation x32 -> x0, loops' own time: 212 us -> none  [the longest x15 167 us: chain_forward(): lax.scan(advance, (start_w, start_b, start_tag), (q_heads, k_heads, v_hea...]
    ppermute x75 -> x0, starting transfers between devices: 173 us -> none  [shifted(): return lax.ppermute(array, axis, pairs)]
where the time goes in v1:
time: 1370 us; the launch traced here: 1360 us
  waiting for transfers between devices  773 us (56%)
  blocking collectives  253 us (18%)
  matrix products  111 us (8%)
  local copies, waits for them, and re-layouts  106 us (8%)
  Pallas kernels  65 us (5%)
  other arithmetic  23 us (2%)
  between operations  15.7 us (1%)
  starting transfers between devices  15.1 us (1%)
    reduce_scatter x1, waiting for transfers between devices, on_device(): lax.psum_scatter(cross_cols(d_mix, w_mix) + cross_cols(d_logit, lr_own),...  134 us
    all_gather x2, waiting for transfers between devices, gather_columns(): return lax.all_gather(got, 'dp', axis=0, tiled=True)  118 us
    all_to_all x2, blocking collectives, gather_columns(): got = lax.all_to_all(cut, 'seq', 0, 0, tiled=True)  117 us
    unnamed x18, waiting for transfers between devices  97.6 us
    reduce_scatter x2, waiting for transfers between devices, return_columns(): got = lax.psum_scatter(grad, 'dp', scatter_dimension=0, tiled=True)  92.1 us
    reduce_scatter x1, waiting for transfers between devices, on_device(): lax.psum_scatter(cross_cols(d_gate_up, w_gu), 'seq', scatter_dimension=0,...  88 us
    unnamed x1, blocking collectives  67.9 us
    all_gather x1, waiting for transfers between devices, on_device(): lax.all_gather((normed_mid * gain_two).astype(bf16), 'seq', axis=0, tiled...  48.2 us
  transfers between devices with their start and end apart: 19, of which 15 were waited for; matrix products, arithmetic and copies ran while one was open for 19% of the time, Pallas kernels for 5%

profile of v1, /device:TPU:9, one launch (start us, length us, event | category | flops | bytes accessed | tf_op | source)
XLA Modules:
  0.0 1361.3 jit_solution(119422732505501503)
XLA Ops:
  11.9 41.9 %all-gather.3 = bf16[32,200,64]{1,2,0:T(8,128)(2,1)S(1)} all-gather(bf16[1,200,64]{1,2,0:T(8,128)(2,1)S(1)} %fusion.48), channel_id=2, replica_groups=mesh['dp'=4,'seq'=8] {'dp','seq'}, dimensions={0}, use_global_device_ids=true | all-gather | bytes 844800 | tf_op jit(solution)/shard_map/all_gather | solution.py:351
  62.3 57.1 %all_to_all.20 = bf16[8,64,1024]{2,1,0:T(8,128)(2,1)} all-to-all(bf16[8,64,1024]{2,1,0:T(8,128)(2,1)S(1)} %pad_maximum_fusion.7), channel_id=1, replica_groups=mesh['dp'=4,'seq'=8] {'seq'}, dimensions={0} | all-to-all | bytes 2097152 | tf_op jit(solution)/shard_map/all_to_all | solution.py:331
  126.9 53.9 %all-gather.17.cloned.1.call-done = bf16[2048,1024]{1,0:T(8,128)(2,1)} async-done(((bf16[512,1024]{1,0:T(8,128)(2,1)}), bf16[2048,1024]{1,0:T(8,128)(2,1)}) %all-gather.17.cloned.1.call-update) | async-done | bytes 4194320 | tf_op jit(solution)/shard_map/all_gather | solution.py:333
  180.9 8.3 fusion.5.qkv_ref
  189.1 29.3 %inner_forward.1 = (f32[1024,256]{1,0:T(8,128)S(1)}, bf16[64,64,256]{2,1,0:T(8,128)(2,1)S(1)}, f32[64,64,64]{2,1,0:T(8,128)S(1)}, f32[64,64,64]{2,1,0:T(8,128)},...) custom-call(s32[64]{0:T(128)S(1)} %add_convert_fusion.1.fresh_ref, ...), custom_call_target="tpu_custom_call" | custom-call | tf_op jit(solution)/shard_map/inner_forward/pallas_call | solution.py:127
  220.4 14.7 %all-gather.4 = f32[8,2,1024]{2,1,0:T(2,128)S(1)} all-gather(f32[1,2,1024]{2,1,0:T(2,128)S(1)} %maximum_bitcast_fusion), channel_id=3, replica_groups=mesh['dp'=4,'seq'=8] {'seq'}, dimensions={0}, use_global_device_ids=true | all-gather | bytes 73728 | tf_op jit(solution)/shard_map/all_gather | solution.py:398
  247.1 8.2 reshape.284
  264.5 59.6 %all_to_all.21 = bf16[8,64,1376]{2,1,0:T(8,128)(2,1)} all-to-all(bf16[8,64,1376]{2,1,0:T(8,128)(2,1)} %reshape.285), channel_id=1, replica_groups=mesh['dp'=4,'seq'=8] {'seq'}, dimensions={0} | all-to-all | bytes 2818048 | tf_op jit(solution)/shard_map/all_to_all | solution.py:331
  324.1 41.3 %reduce-scatter.13.cloned.1.call-done = f32[128,2048]{1,0:T(8,128)} async-done(((f32[1024,2048]{1,0:T(8,128)}), f32[128,2048]{1,0:T(8,128)}) %reduce-scatter.13.cloned.1.call-update) | async-done | bytes 1048592 | tf_op jit(solution)/shard_map/reduce_scatter | solution.py:406
  370.2 37.4 %all-gather.29.cloned.1.call-done = bf16[4,172,2048]{2,1,0:T(8,128)(2,1)} async-done(((bf16[1,172,2048]{2,1,0:T(8,128)(2,1)}), bf16[4,172,2048]{2,1,0:T(8,128)(2,1)}) %all-gather.29.cloned.1.call-update) | async-done | bytes 2818064 | tf_op jit(solution)/shard_map/all_gather | solution.py:375
  410.8 64.3 %all-gather.23.cloned.1.call-done = bf16[2048,1376]{1,0:T(8,128)(2,1)} async-done(((bf16[512,1376]{1,0:T(8,128)(2,1)}), bf16[2048,1376]{1,0:T(8,128)(2,1)}) %all-gather.23.cloned.1.call-update) | async-done | bytes 5636112 | tf_op jit(solution)/shard_map/all_gather | solution.py:333
  475.1 48.2 %all-gather.21.cloned.1.call-done = bf16[1024,2048]{1,0:T(8,128)(2,1)} async-done(((bf16[128,2048]{1,0:T(8,128)(2,1)}), bf16[1024,2048]{1,0:T(8,128)(2,1)}) %all-gather.21.cloned.1.call-update) | async-done | bytes 4194320 | tf_op jit(solution)/shard_map/all_gather | solution.py:410
  523.4 11.2 fusion.64
  534.6 36.3 %all-gather.27.cloned.1.call-done = bf16[1,1024,2048]{2,1,0:T(8,128)(2,1)} async-done(((bf16[1,128,2048]{2,1,0:T(8,128)(2,1)}), bf16[1,1024,2048]{2,1,0:T(8,128)(2,1)}) %all-gather.27.cloned.1.call-update) | async-done | bytes 4194320 | tf_op jit(solution)/shard_map/all_gather | solution.py:376
  570.9 10.0 multiply_convert_fusion.1
  582.4 8.9 fusion.9
  591.4 88.0 %reduce-scatter.17.cloned.1.call-done = f32[128,2048]{1,0:T(8,128)} async-done(((f32[1024,2048]{1,0:T(8,128)}), f32[128,2048]{1,0:T(8,128)}) %reduce-scatter.17.cloned.1.call-update) | async-done | bytes 1048592 | tf_op jit(solution)/shard_map/reduce_scatter | solution.py:425
  684.4 11.1 fusion.8
  695.6 34.7 %all-gather.25.cloned.1.call-done = bf16[1024,2048]{1,0:T(8,128)(2,1)} async-done(((bf16[128,2048]{1,0:T(8,128)(2,1)}), bf16[1024,2048]{1,0:T(8,128)(2,1)}) %all-gather.25.cloned.1.call-update) | async-done | bytes 4194320 | tf_op jit(solution)/shard_map/all_gather | solution.py:433
  736.4 11.4 psum.7
  749.8 35.7 %inner_backward.1 = (bf16[1024,768]{1,0:T(8,128)(2,1)S(1)}, f32[64,1,64]{2,1,0:T(1,128)S(1)}, f32[64,256]{1,0:T(8,128)S(1)}, f32[64,64]{1,0:T(8,128)S(1)}, f32[64,64]{1,0:T(8,128)S(1)}, /*index=5*/f32[64,64]{1,0:T(8,128)S(1)}) custom-call(s32[64]{0:T(128)S(1)} %add_convert_fusion.1.fresh_ref, f32[1024,768]{1,0:T(8,128)} %fusion.5.qkv_ref, ...), custom_call_target="tpu_custom_call" | custom-call | tf_op jit(solution)/shard_map/inner_backward/pallas_call | solution.py:239
  800.1 9.1 fusion.14
  811.0 7.5 fusion.65
  818.6 24.7 %reduce-scatter.25.cloned.1.call-done = f32[512,1376]{0,1:T(8,128)} async-done(((f32[2048,1376]{0,1:T(8,128)}), f32[512,1376]{0,1:T(8,128)}) %reduce-scatter.25.cloned.1.call-update) | async-done | bytes 2818064 | tf_op jit(solution)/shard_map/reduce_scatter | solution.py:336
  861.3 134.2 %reduce-scatter.19.cloned.1.call-done = f32[128,2048]{1,0:T(8,128)} async-done(((f32[1024,2048]{1,0:T(8,128)}), f32[128,2048]{1,0:T(8,128)}) %reduce-scatter.19.cloned.1.call-update) | async-done | bytes 1048592 | tf_op jit(solution)/shard_map/reduce_scatter | solution.py:454
  1006.3 7.2 fusion.1
  1016.2 67.4 %reduce-scatter.21.cloned.1.call-done = f32[512,1024]{1,0:T(8,128)} async-done(((f32[2048,1024]{1,0:T(8,128)}), f32[512,1024]{1,0:T(8,128)}) %reduce-scatter.21.cloned.1.call-update) | async-done | bytes 2097168 | tf_op jit(solution)/shard_map/reduce_scatter | solution.py:336
  1089.1 67.9 %fusion = f32[176,2048]{1,0:T(8,128)S(1)} fusion(f32[688,2048]{1,0:T(8,128)} %fusion.1), kind=kCustom, calls=%all-reduce-scatter | all-reduce-scatter fusion | flops 1441793 | bytes 7078400
  1169.2 8.4 reshape.300
  1189.7 26.7 %reduce-scatter.15.cloned.1.call-done = f32[128,2048]{1,0:T(8,128)} async-done(((f32[1024,2048]{1,0:T(8,128)}), f32[128,2048]{1,0:T(8,128)}) %reduce-scatter.15.cloned.1.call-update) | async-done | bytes 1048592 | tf_op jit(solution)/shard_map/reduce_scatter | solution.py:417
  1219.4 95.1 %reduce-scatter.27.cloned.1.call-done = f32[1,72,103]{2,1,0:T(8,128)} async-done(((f32[32,72,103]{2,1,0:T(8,128)}), f32[1,72,103]{2,1,0:T(8,128)}) %reduce-scatter.27.cloned.1.call-update) | async-done | bytes 29680
  1336.2 18.1 %reduce-scatter.23.cloned.1.call-done = f32[64,2048]{1,0:T(8,128)} async-done(((f32[256,2048]{1,0:T(8,128)}), f32[64,2048]{1,0:T(8,128)}) %reduce-scatter.23.cloned.1.call-update) | async-done | bytes 524304 | tf_op jit(solution)/shard_map/reduce_scatter | solution.py:436
  (241 shorter events, 167.7 us)
Async XLA Ops:
  7.2 49.8 %copy-start.11 = (bf16[64,2048]{1,0:T(8,128)(2,1)S(1)}, bf16[64,2048]{1,0:T(8,128)(2,1)}, u32[]{:S(2)}) copy-start(bf16[64,2048]{1,0:T(8,128)(2,1)} %param.24) | copy-start | bytes 786436
  7.2 116.1 %all-gather.15.cloned.1.call-start = ((), (), s32[]{:S(2)}) async-start(), calls=%async_computation.12 | async-start | bytes 4718592 | tf_op jit(solution)/shard_map/all_gather | solution.py:380
  56.9 123.9 %all-gather.17.cloned.1.call-start = ((), (), s32[]{:S(2)}) async-start(), calls=%async_computation.13 | async-start | bytes 5242880 | tf_op jit(solution)/shard_map/all_gather | solution.py:333
  62.2 58.1 %copy-start.9 = (bf16[32,200,64]{1,2,0:T(8,128)(2,1)S(1)}, bf16[32,200,64]{1,2,0:T(8,128)(2,1)}, u32[]{:S(2)}) copy-start(bf16[32,200,64]{1,2,0:T(8,128)(2,1)} %copy-done.8) | copy-start | bytes 2457604
  62.3 58.3 %copy-start.19 = (bf16[32]{0:T(256)(128)(2,1)S(1)}, bf16[32]{0:T(256)(128)(2,1)}, u32[]{:S(2)}) copy-start(bf16[32]{0:T(256)(128)(2,1)} %param.23) | copy-start | bytes 196
  62.3 60.1 %slice-start = ((bf16[32,200,64]{1,2,0:T(8,128)(2,1)}), bf16[32,64,64]{1,2,0:T(8,128)(2,1)S(1)}, s32[]{:S(2)}) async-start(bf16[32,200,64]{1,2,0:T(8,128)(2,1)} %copy-done.8), calls=%async_computation.28 | async-start | bytes 1048576 | tf_op jit(solution)/shard_map/slice | solution.py:352
  119.5 121.0 %all-gather.19.cloned.1.call-start = ((), (), s32[]{:S(2)}) async-start(), calls=%async_computation.14 | async-start | bytes 1310720 | tf_op jit(solution)/shard_map/all_gather | solution.py:372
  120.2 245.2 %reduce-scatter.13.cloned.1.call-start = ((), (), s32[]{:S(2)}) async-start(), calls=%async_computation.15 | async-start | bytes 9437184 | tf_op jit(solution)/shard_map/reduce_scatter | solution.py:406
  189.1 46.2 %copy-start.14 = (f32[256,1]{0,1:T(1,128)S(1)}, f32[256,1]{0,1:T(1,128)}, u32[]{:S(2)}) copy-start(f32[256,1]{0,1:T(1,128)} %get-tuple-element.131) | copy-start | bytes 3076
  246.5 161.1 %all-gather.29.cloned.1.call-start = ((), (), s32[]{:S(2)}) async-start(), calls=%async_computation.26 | async-start | bytes 3604480 | tf_op jit(solution)/shard_map/all_gather | solution.py:375
  247.1 228.1 %all-gather.23.cloned.1.call-start = ((), (), s32[]{:S(2)}) async-start(), calls=%async_computation.17 | async-start | bytes 7208960 | tf_op jit(solution)/shard_map/all_gather | solution.py:333
  324.1 199.3 %all-gather.21.cloned.1.call-start = ((), (), s32[]{:S(2)}) async-start(), calls=%async_computation.16 | async-start | bytes 4718592 | tf_op jit(solution)/shard_map/all_gather | solution.py:410
  369.0 201.9 %all-gather.27.cloned.1.call-start = ((), (), s32[]{:S(2)}) async-start(), calls=%async_computation.25 | async-start | bytes 4718592 | tf_op jit(solution)/shard_map/all_gather | solution.py:376
  369.7 309.7 %reduce-scatter.17.cloned.1.call-start = ((), (), s32[]{:S(2)}) async-start(), calls=%async_computation.19 | async-start | bytes 9437184 | tf_op jit(solution)/shard_map/reduce_scatter | solution.py:425
  591.3 138.9 %all-gather.25.cloned.1.call-start = ((), (), s32[]{:S(2)}) async-start(), calls=%async_computation.20 | async-start | bytes 4718592 | tf_op jit(solution)/shard_map/all_gather | solution.py:433
  684.2 159.1 %reduce-scatter.25.cloned.1.call-start = ((), (), s32[]{:S(2)}) async-start(), calls=%async_computation.24 | async-start | bytes 14090240 | tf_op jit(solution)/shard_map/reduce_scatter | solution.py:336
  695.5 34.7 %copy-start.15 = (f32[256,1]{0,1:T(1,128)S(1)}, f32[256,1]{0,1:T(1,128)}, u32[]{:S(2)}) copy-start(f32[256,1]{0,1:T(1,128)} %get-tuple-element.131) | copy-start | bytes 3076
  695.5 300.1 %reduce-scatter.19.cloned.1.call-start = ((), (), s32[]{:S(2)}) async-start(), calls=%async_computation.21 | async-start | bytes 9437184 | tf_op jit(solution)/shard_map/reduce_scatter | solution.py:454
  749.8 37.3 %copy-start.22 = (bf16[1024,256]{1,0:T(8,128)(2,1)S(1)}, bf16[1024,256]{1,0:T(8,128)(2,1)}, u32[]{:S(2)}) copy-start(bf16[1024,256]{1,0:T(8,128)(2,1)} %get-tuple-element.122) | copy-start | bytes 1572868
  798.7 284.9 %reduce-scatter.21.cloned.1.call-start = ((), (), s32[]{:S(2)}) async-start(), calls=%async_computation.22 | async-start | bytes 10485760 | tf_op jit(solution)/shard_map/reduce_scatter | solution.py:336
  809.3 407.2 %reduce-scatter.15.cloned.1.call-start = ((), (), s32[]{:S(2)}) async-start(), calls=%async_computation.18 | async-start | bytes 9437184 | tf_op jit(solution)/shard_map/reduce_scatter | solution.py:417
  846.6 169.6 %all-to-all-start.3 = ((f32[8,64,1376]{2,1,0:T(8,128)}), f32[8,64,1376]{2,1,0:T(8,128)}, u32[]{:S(2)}, u32[]{:S(2)}) async-start(f32[8,64,1376]{2,1,0:T(8,128)} %bitcast.188), calls=%async_computation.10 | async-start | bytes 5767168 | tf_op jit(solution)/shard_map/all_to_all | solution.py:338
  852.0 462.5 %reduce-scatter.27.cloned.1.call-start = ((), (), s32[]{:S(2)}) async-start(), calls=%async_computation.27 | async-start | bytes 1216512
  856.7 138.9 %copy-start.5 = (bf16[1,128,2048]{2,1,0:T(8,128)(2,1)S(1)}, bf16[1,128,2048]{2,1,0:T(8,128)(2,1)}, u32[]{:S(2)}) copy-start(bf16[1,128,2048]{2,1,0:T(8,128)(2,1)} %param.18) | copy-start | bytes 1572868
  1006.2 348.1 %reduce-scatter.23.cloned.1.call-start = ((), (), s32[]{:S(2)}) async-start(), calls=%async_computation.23 | async-start | bytes 2621440 | tf_op jit(solution)/shard_map/reduce_scatter | solution.py:436
  1083.6 236.9 %all-to-all-start.2 = ((f32[8,64,1024]{2,1,0:T(8,128)}), f32[8,64,1024]{2,1,0:T(8,128)}, u32[]{:S(2)}, u32[]{:S(2)}) async-start(f32[8,64,1024]{2,1,0:T(8,128)} %bitcast.199), calls=%async_computation.7 | async-start | bytes 4194304 | tf_op jit(solution)/shard_map/all_to_all | solution.py:338
  1089.1 70.6 %copy-start.16 = (u32[32]{0:T(128)S(1)}, u32[32]{0:T(128)}, u32[]{:S(2)}) copy-start(u32[32]{0:T(128)} %constant.102) | copy-start | bytes 388
  1157.0 4.4 collective-permute-start
  1184.3 32.1 %copy-start.4 = (f32[128,2048]{1,0:T(8,128)S(1)}, f32[128,2048]{1,0:T(8,128)}, u32[]{:S(2)}) copy-start(f32[128,2048]{1,0:T(8,128)} %copy-done.3) | copy-start | bytes 3145732
  1184.3 32.1 %copy-start.6 = (f32[128,2048]{1,0:T(8,128)S(1)}, f32[128,2048]{1,0:T(8,128)}, u32[]{:S(2)}) copy-start(f32[128,2048]{1,0:T(8,128)} %reduce-scatter.17.cloned.1.call-done) | copy-start | bytes 3145732
  1184.3 32.1 %copy-start.7 = (bf16[1,128,2048]{2,1,0:T(8,128)(2,1)S(1)}, bf16[1,128,2048]{2,1,0:T(8,128)(2,1)}, u32[]{:S(2)}) copy-start(bf16[1,128,2048]{2,1,0:T(8,128)(2,1)} %param.35) | copy-start | bytes 1572868
  1184.3 32.1 %copy-start.13 = (f32[128]{0:T(128)S(1)}, f32[128]{0:T(128)}, u32[]{:S(2)}) copy-start(f32[128]{0:T(128)} %copy-done.12) | copy-start | bytes 1540
  (13 other events, 53.5 us)
Sparse Core Ops, SparseCore 0:
  57.1 65.8 all-gather.14
  124.8 56.0 all-gather.16
  182.7 26.6 all-gather.18
  246.6 118.7 reduce-scatter.12
  367.1 40.4 all-gather.28
  409.3 65.7 all-gather.22
  477.3 46.0 all-gather.20
  525.0 45.8 all-gather.26
  591.5 87.9 reduce-scatter.16
  684.3 45.8 all-gather.24
  733.4 109.7 reduce-scatter.24
  845.4 150.1 reduce-scatter.18
  998.6 84.9 reduce-scatter.20
  1085.9 130.5 reduce-scatter.14
  1222.2 92.3 reduce-scatter.26
  1318.2 36.0 reduce-scatter.22

commit v2 on v1

--- a/solution.py
+++ b/solution.py
@@ -259,6 +259,500 @@
         name="inner_backward",
     )(fresh, qkv, e_rows, dmix, *saved, gain, shift)
 
+MESH = pl.DeviceIdType.MESH
+
+
+class Wires:
+    def __init__(self, send_sems, recv_sems):
+        self.send_sems, self.recv_sems, self.used = send_sems, recv_sems, 0
+
+    def copy(self, source, target, device):
+        at = self.number()
+        return self.numbered(at, source, target, device)
+
+    def number(self):
+        self.used += 1
+        return self.used - 1
+
+    def numbered(self, at, source, target, device):
+        return pltpu.make_async_remote_copy(
+            src_ref=source,
+            dst_ref=target,
+            send_sem=self.send_sems.at[at],
+            recv_sem=self.recv_sems.at[at],
+            device_id=device,
+            device_id_type=MESH,
+        )
+
+    def keep(self, source, target):
+        at = self.number()
+        return pltpu.make_async_copy(source, target, self.send_sems.at[at])
+
+
+def on_line(step):
+    return {"seq": lax.axis_index("seq") + step}
+
+
+def sibling():
+    me = lax.axis_index("seq")
+    return {"seq": me + 1 - 2 * lax.rem(me, 2)}
+
+
+def pack_peer(step):
+    packs = lax.axis_size("dp")
+    return {"dp": lax.rem(lax.axis_index("dp") + step, packs)}
+
+
+def seq_peer(step):
+    count = lax.axis_size("seq")
+    return {"seq": lax.rem(lax.axis_index("seq") + step, count)}
+
+
+def meet(groups):
+    barrier = pltpu.get_barrier_semaphore()
+    me, count = lax.axis_index("seq"), lax.axis_size("seq")
+
+    def greet(device):
+        pl.semaphore_signal(barrier, inc=1, device_id=device, device_id_type=MESH)
+
+    peers = 0
+    if "dp" in groups:
+        for step in range(1, lax.axis_size("dp")):
+            greet(pack_peer(step))
+        peers += lax.axis_size("dp") - 1
+    if "seq" in groups:
+        for step in range(1, count):
+            greet(seq_peer(step))
+        peers += count - 1
+    elif "line" in groups:
+        greet(sibling())
+
+        @pl.when(me >= 2)
+        def _():
+            greet(on_line(-2))
+
+        @pl.when(me < count - 2)
+        def _():
+            greet(on_line(2))
+
+        peers += 1 + jnp.minimum(me // 2, 1) + jnp.minimum((count - 1 - me) // 2, 1)
+    pl.semaphore_wait(barrier, peers)
+
+
+def gather_line(wires, source, out, cut):
+    me, count = lax.axis_index("seq"), lax.axis_size("seq")
+    chips, chip = count // 2, me // 2
+    step = source.shape[0] // cut
+    other = me + 1 - 2 * lax.rem(me, 2)
+
+    def piece(slot, part):
+        return out.at[slot, pl.ds(part * step, step)]
+
+    own = wires.keep(source, out.at[me])
+    own.start()
+    numbers = {(way, i, part): wires.number() for way in "rlRL" for i in range(chips) for part in range(cut)}
+
+    def copy(way, i, part):
+        slot = me - 2 * i if way in "rR" else me + 2 * i
+        start = source.at[pl.ds(part * step, step)] if i == 0 else piece(slot, part)
+        device = {"r": on_line(2), "l": on_line(-2), "R": sibling(), "L": sibling()}[way]
+        return wires.numbered(numbers[way, i, part], start, piece(slot, part), device)
+
+    def arrived(way, i, part):
+        if way in "rl":
+            slot = me - 2 * (i + 1) if way == "r" else me + 2 * (i + 1)
+        else:
+            slot = other - 2 * i if way == "R" else other + 2 * i
+        there = piece(slot, part)
+        wires.numbered(numbers[way, i, part], there, there, sibling()).wait_recv()
+
+    @pl.when(chip < chips - 1)
+    def _():
+        for part in range(cut):
+            copy("r", 0, part).start()
+
+    @pl.when(chip > 0)
+    def _():
+        for part in range(cut):
+            copy("l", 0, part).start()
+
+    for part in range(cut):
+        copy("R", 0, part).start()
+    for i in range(1, chips):
+        for part in range(cut):
+            yield
+
+            @pl.when(chip >= i)
+            def _():
+                arrived("r", i - 1, part)
+
+                @pl.when(chip < chips - 1)
+                def _():
+                    copy("r", i, part).start()
+
+                copy("R", i, part).start()
+
+            @pl.when(chip + i <= chips - 1)
+            def _():
+                arrived("l", i - 1, part)
+
+                @pl.when(chip > 0)
+                def _():
+                    copy("l", i, part).start()
+
+                copy("L", i, part).start()
+
+    yield
+    own.wait()
+    for i in range(chips):
+        for part in range(cut):
+            if i == 0:
+                arrived("R", 0, part)
+                copy("R", 0, part).wait_send()
+            else:
+
+                @pl.when(chip >= i)
+                def _():
+                    arrived("R", i, part)
+                    copy("R", i, part).wait_send()
+
+                @pl.when(chip + i <= chips - 1)
+                def _():
+                    arrived("L", i, part)
+                    copy("L", i, part).wait_send()
+
+            @pl.when((chip >= i) & (chip < chips - 1))
+            def _():
+                copy("r", i, part).wait_send()
+
+            @pl.when((chip + i <= chips - 1) & (chip > 0))
+            def _():
+                copy("l", i, part).wait_send()
+
+
+def add_into(out, parts, rows=16):
+    def body(i, _):
+        lines = pl.ds(pl.multiple_of(i * rows, rows), rows)
+        total = parts[0][lines, :].astype(jnp.float32)
+        for part in parts[1:]:
+            total = total + part[lines, :].astype(jnp.float32)
+        out[lines, :] = total.astype(out.dtype)
+        return 0
+
+    lax.fori_loop(0, out.shape[0] // rows, body, 0)
+
+
+def scatter_line(wires, source, out, near, from_left, from_right, to_right, to_left, cut):
+    me, count = lax.axis_index("seq"), lax.axis_size("seq")
+    chips, chip, core = count // 2, me // 2, lax.rem(me, 2)
+    step = source.shape[1] // cut
+
+    def lines(part):
+        return pl.ds(part * step, step)
+
+    order = []
+    for i in range(chips // 2):
+        order += [chips - 1 - i, i]
+    order += [chips // 2] if chips % 2 else []
+    across = {}
+    for dest in order:
+        for part in range(cut):
+            across[dest, part] = wires.copy(
+                source.at[2 * dest + 1 - core, lines(part)], near.at[dest, lines(part)], sibling()
+            )
+            across[dest, part].start()
+    right, left = {}, {}
+    for dest in range(chips):
+        for part in range(cut):
+            right[dest, part] = wires.copy(to_right.at[dest, lines(part)], from_left.at[dest, lines(part)], on_line(2))
+            left[dest, part] = wires.copy(to_left.at[dest, lines(part)], from_right.at[dest, lines(part)], on_line(-2))
+    for i in range(chips - 1):
+        for part in range(cut):
+            yield
+            for dest, table, inbox, outbox, ahead, first in (
+                (chips - 1 - i, right, from_left, to_right, chip < chips - 1 - i, chip == 0),
+                (i, left, from_right, to_left, chip > i, chip == chips - 1),
+            ):
+                terms = [source.at[2 * dest + core, lines(part)], near.at[dest, lines(part)]]
+
+                @pl.when(ahead)
+                def _():
+                    across[dest, part].wait_recv()
+
+                    @pl.when(first)
+                    def _():
+                        add_into(outbox.at[dest, lines(part)], terms)
+
+                    @pl.when(jnp.logical_not(first))
+                    def _():
+                        table[dest, part].wait_recv()
+                        add_into(outbox.at[dest, lines(part)], terms + [inbox.at[dest, lines(part)]])
+
+                    table[dest, part].start()
+
+    for part in range(cut):
+        yield
+        for dest in range(chips):
+
+            @pl.when(chip == dest)
+            def _():
+                across[dest, part].wait_recv()
+                terms = [source.at[2 * dest + core, lines(part)], near.at[dest, lines(part)]]
+                if dest > 0:
+                    right[dest, part].wait_recv()
+                    terms = terms + [from_left.at[dest, lines(part)]]
+                if dest < chips - 1:
+                    left[dest, part].wait_recv()
+                    terms = terms + [from_right.at[dest, lines(part)]]
+                add_into(out.at[lines(part)], terms)
+
+    for dest in range(chips):
+        for part in range(cut):
+            across[dest, part].wait_send()
+
+            @pl.when(chip < dest)
+            def _():
+                right[dest, part].wait_send()
+
+            @pl.when(chip > dest)
+            def _():
+                left[dest, part].wait_send()
+
+
+def swap_seq(wires, source, out):
+    me, count = lax.axis_index("seq"), lax.axis_size("seq")
+    own = wires.keep(source.at[me], out.at[me])
+    own.start()
+    sent = []
+    for step in range(1, count):
+        peer = lax.rem(me + step, count)
+        sent.append(wires.copy(source.at[peer], out.at[me], seq_peer(step)))
+        sent[-1].start()
+    yield
+    own.wait()
+    for copy in sent:
+        copy.wait()
+
+
+def spread_seq(wires, source, out):
+    me, count = lax.axis_index("seq"), lax.axis_size("seq")
+    own = wires.keep(source, out.at[me])
+    own.start()
+    sent = []
+    for step in range(1, count):
+        sent.append(wires.copy(source, out.at[me], seq_peer(step)))
+        sent[-1].start()
+    yield
+    own.wait()
+    for copy in sent:
+        copy.wait()
+
+
+def swap_dp(wires, source, out):
+    me, count = lax.axis_index("dp"), lax.axis_size("dp")
+    own = wires.keep(source.at[me], out.at[me])
+    own.start()
+    sent = []
+    for step in range(1, count):
+        sent.append(wires.copy(source.at[lax.rem(me + step, count)], out.at[me], pack_peer(step)))
+        sent[-1].start()
+    yield
+    own.wait()
+    for copy in sent:
+        copy.wait()
+
+
+def spread_dp(wires, source, out):
+    me, count = lax.axis_index("dp"), lax.axis_size("dp")
+    own = wires.keep(source, out.at[me])
+    own.start()
+    sent = []
+    for step in range(1, count):
+        sent.append(wires.copy(source, out.at[me], pack_peer(step)))
+        sent[-1].start()
+    yield
+    own.wait()
+    for copy in sent:
+        copy.wait()
+
+
+def run_all(jobs):
+    jobs = list(jobs)
+    while jobs:
+        for job in list(jobs):
+            try:
+                next(job)
+            except StopIteration:
+                jobs.remove(job)
+
+
+def talk(name, cid, groups, operands, outs, plan, copies, in_vmem=(), out_vmem=(), scratch=()):
+    n_in, n_out = len(operands), len(outs)
+
+    def kernel(*refs):
+        ins, results = refs[:n_in], refs[n_in : n_in + n_out]
+        buffers, (send_sems, recv_sems) = refs[n_in + n_out : -2], refs[-2:]
+        meet(groups)
+        wires = Wires(send_sems, recv_sems)
+        run_all(plan(wires, ins, results, buffers))
+        assert wires.used <= copies, wires.used
+
+    def where(i, chosen):
+        return pl.BlockSpec(memory_space=pltpu.VMEM if i in chosen else pl.ANY)
+
+    return pl.pallas_call(
+        kernel,
+        out_shape=outs,
+        in_specs=[where(i, in_vmem) for i in range(n_in)],
+        out_specs=[where(i, out_vmem) for i in range(n_out)],
+        scratch_shapes=list(scratch) + [pltpu.SemaphoreType.DMA((copies,)), pltpu.SemaphoreType.DMA((copies,))],
+        compiler_params=pltpu.CompilerParams(
+            collective_id=cid, has_side_effects=True, vmem_limit_bytes=48 * 1024 * 1024
+        ),
+        name=name,
+    )(*operands)
+
+
+def all_gather_line(name, cid, block, cut=2):
+    count = lax.axis_size("seq")
+    out = jax.ShapeDtypeStruct((count,) + block.shape, block.dtype)
+    (got,) = talk(
+        name, cid, ("line",), (block,), [out],
+        lambda wires, ins, outs, _: [gather_line(wires, ins[0], outs[0], cut)],
+        1 + 4 * (count // 2) * cut,
+    )
+    return got.reshape((-1,) + block.shape[1:])
+
+
+def reduce_scatter_line(name, cid, terms, cut=2):
+    count = lax.axis_size("seq")
+    rows, width = terms.shape[0] // count, terms.shape[1]
+    box = pltpu.VMEM((count // 2, rows, width), terms.dtype)
+    (got,) = talk(
+        name, cid, ("line",), (terms.reshape(count, rows, width),), [jax.ShapeDtypeStruct((rows, width), jnp.float32)],
+        lambda wires, ins, outs, boxes: [scatter_line(wires, ins[0], outs[0], *boxes, cut)],
+        3 * (count // 2) * cut, in_vmem=(0,), out_vmem=(0,), scratch=(box,) * 5,
+    )
+    return got
+
+
+def columns_out(wires, source, out):
+    mine, me, count, packs = lax.axis_index("dp"), lax.axis_index("seq"), lax.axis_size("seq"), lax.axis_size("dp")
+    own = wires.keep(source.at[me], out.at[mine, me])
+    own.start()
+    sent, onward = [], []
+    for step in range(1, count):
+        sent.append(wires.copy(source.at[lax.rem(me + step, count)], out.at[mine, me], seq_peer(step)))
+        sent[-1].start()
+    for step in range(1, packs):
+        onward.append(wires.copy(source.at[me], out.at[mine, me], pack_peer(step)))
+        onward[-1].start()
+    for step in range(1, count):
+        yield
+        sent[step - 1].wait_recv()
+        came = out.at[mine, lax.rem(me + count - step, count)]
+        for other in range(1, packs):
+            onward.append(wires.copy(came, came, pack_peer(other)))
+            onward[-1].start()
+    yield
+    own.wait()
+    for copy in sent:
+        copy.wait_send()
+    for copy in onward:
+        copy.wait()
+
+
+def spread_all(wires, source, out):
+    mine, me, count, packs = lax.axis_index("dp"), lax.axis_index("seq"), lax.axis_size("seq"), lax.axis_size("dp")
+    own = wires.keep(source, out.at[mine, me])
+    own.start()
+    sent, onward = [], []
+    for step in range(1, packs):
+        sent.append(wires.copy(source, out.at[mine, me], pack_peer(step)))
+        sent[-1].start()
+    for step in range(1, count):
+        onward.append(wires.copy(source, out.at[mine, me], seq_peer(step)))
+        onward[-1].start()
+    for other in range(1, packs):
+        yield
+        sent[other - 1].wait_recv()
+        came = out.at[lax.rem(mine + packs - other, packs), me]
+        for step in range(1, count):
+            onward.append(wires.copy(came, came, seq_peer(step)))
+            onward[-1].start()
+    yield
+    own.wait()
+    for copy in sent:
+        copy.wait_send()
+    for copy in onward:
+        copy.wait()
+
+
+def shape_of(shape, dtype):
+    return jax.ShapeDtypeStruct(tuple(shape), dtype)
+
+
+def first_exchange(small, mix, wide, block):
+    packs, count = lax.axis_size("dp"), lax.axis_size("seq")
+    outs = [
+        shape_of((packs, count) + small.shape, small.dtype),
+        shape_of((packs,) + mix.shape, mix.dtype),
+        shape_of(wide.shape, wide.dtype),
+        shape_of((count,) + block.shape, block.dtype),
+    ]
+    cut = 2
+
+    def plan(wires, ins, results, _):
+        return [
+            columns_out(wires, ins[1], results[1]),
+            spread_all(wires, ins[0], results[0]),
+            gather_line(wires, ins[3], results[3], cut),
+            swap_seq(wires, ins[2], results[2]),
+        ]
+
+    copies = 3 * (count * packs + count) + 4 * (count // 2) * cut
+    small, mix, wide, block = talk("first_exchange", 1, ("dp", "seq"), (small, mix, wide, block), outs, plan, copies)
+    return small, mix.reshape(-1, mix.shape[-1]), wide, block.reshape(-1, block.shape[-1])
+
+
+def gather_seq(name, cid, block):
+    count = lax.axis_size("seq")
+    (got,) = talk(
+        name, cid, ("seq",), (block,), [shape_of((count,) + block.shape, block.dtype)],
+        lambda wires, ins, outs, _: [spread_seq(wires, ins[0], outs[0])], count,
+    )
+    return got
+
+
+def scatter_with(name, cid, terms, over_dp, cut=2):
+    count, packs = lax.axis_size("seq"), lax.axis_size("dp")
+    rows, width = terms.shape[0] // count, terms.shape[1]
+    box = pltpu.VMEM((count // 2, rows, width), terms.dtype)
+    blocks = [array.reshape((packs, -1) + array.shape[1:]) for array in over_dp]
+    outs = [shape_of((rows, width), jnp.float32)] + [shape_of(b.shape, b.dtype) for b in blocks]
+
+    def plan(wires, ins, results, boxes):
+        jobs = [swap_dp(wires, source, result) for source, result in zip(ins[1:], results[1:])]
+        return jobs + [scatter_line(wires, ins[0], results[0], *boxes, cut)]
+
+    got = talk(
+        name, cid, ("line", "dp") if blocks else ("line",), (terms.reshape(count, rows, width), *blocks), outs, plan,
+        3 * (count // 2) * cut + packs * len(blocks), in_vmem=(0,), out_vmem=(0,), scratch=(box,) * 5,
+    )
+    return got
+
+
+def swap_places(name, cid, arrays):
+    count = lax.axis_size("seq")
+    return talk(
+        name, cid, ("seq",), arrays, [shape_of(a.shape, a.dtype) for a in arrays],
+        lambda wires, ins, outs, _: [swap_seq(wires, i, o) for i, o in zip(ins, outs)], count * len(arrays),
+    )
+
+
+def add_packs(array):
+    return jnp.sum(array.astype(jnp.float32), axis=0)
+
 
 def cross_rows(left_side, right_side):
     return lax.dot_general(left_side, right_side, (((0,), (0,)), ((), ())), preferred_element_type=jnp.float32)
@@ -327,28 +821,23 @@
         cut = cut.reshape(per_seq, depth, parts * out * last)
         return cut
 
-    def gather_columns(cut):
-        got = lax.all_to_all(cut, "seq", 0, 0, tiled=True)
-        got = got.reshape(-1, cut.shape[-1])
-        return lax.all_gather(got, "dp", axis=0, tiled=True)
-
-    def return_columns(grad):
-        got = lax.psum_scatter(grad, "dp", scatter_dimension=0, tiled=True)
-        got = got.reshape(per_seq, -1, grad.shape[1])
-        return lax.all_to_all(got, "seq", 0, 0, tiled=True)
-
     def columns_back(got, parts, out, last):
         depth = got.shape[1]
         got = got.reshape(per_seq, depth, parts, out, last).transpose(1, 2, 3, 0, 4)
         return got.reshape(depth, parts * out * per_seq * last)
 
-    inputs = tokens[0].astype(floats)
     lanes = max(HD, heads_all)
     pad = lambda array: jnp.pad(array, ((0, 0), (0, lanes - array.shape[1])))
     tags = segments[0].reshape(span // MB, MB)[:, 0].astype(bf16)
     vectors = jnp.stack([norm_one, norm_two, b_init, tnorm_w, tnorm_b, post_w, post_b], axis=1)
     small = jnp.concatenate([pad(w_init), pad(w_lr), pad(vectors), pad(jnp.broadcast_to(tags[None], (8, span // MB)))], axis=0)
-    small = lax.all_gather(small, both, axis=0)
+    small, w_mix, gu_part, rows_all = first_exchange(
+        small,
+        jnp.concatenate([by_place(w_qkv, 3, outer, inner), by_place(w_gate, 1, outer, inner)], axis=2),
+        by_place(w_gate_up, 2, packs, units),
+        tokens[0],
+    )
+    small = small.reshape((devices,) + small.shape[2:])
     init_all = small[:, :rows, :HD].reshape(width, HD)
     lr_all = small[:, rows : 2 * rows, :heads_all].reshape(width, heads_all)
     vec_all = small[:, 2 * rows : 3 * rows, :7].reshape(width, 7)
@@ -364,10 +853,7 @@
     bias_own = lax.dynamic_index_in_dim(lr_bias.reshape(outer, per_seq, heads // outer), place, 1, keepdims=False)
     bias_own = bias_own.reshape(heads).astype(floats)
 
-    w_mix = gather_columns(
-        jnp.concatenate([by_place(w_qkv, 3, outer, inner), by_place(w_gate, 1, outer, inner)], axis=2)
-    )
-    w_gu = gather_columns(by_place(w_gate_up, 2, packs, units))
+    w_gu = lax.all_gather(gu_part.reshape(-1, gu_part.shape[-1]), "dp", axis=0, tiled=True)
     if aligned:
         w_o = lax.all_gather(w_out, "dp", axis=0, tiled=True)
     else:
@@ -375,9 +861,10 @@
     w_d = lax.all_gather(w_down, "dp", axis=0, tiled=True)
     d_top = lax.all_gather(grad_out[0], "seq", axis=0, tiled=True)
 
+    inputs = rows_all.astype(floats)
     scale_one = lax.rsqrt(jnp.mean(inputs * inputs, -1, keepdims=True) + EPSILON)
     normed_in = inputs * scale_one
-    x_one = lax.all_gather((normed_in * gain_one).astype(bf16), "seq", axis=0, tiled=True)
+    x_one = (normed_in * gain_one).astype(bf16)
     qkv = dot(x_one, w_mix[:, : 3 * mine])
     gate_pre = dot(x_one, w_mix[:, 3 * mine :])
     lr_sigm = jax.nn.sigmoid(dot(x_one, lr_own) + bias_own)
@@ -395,7 +882,7 @@
 
     mean_own = jnp.mean(mixed, -1)
     spread_own = jnp.sum((mixed - mean_own[:, None]) ** 2, -1)
-    stats = lax.all_gather(jnp.stack([mean_own, spread_own]), "seq", axis=0)
+    stats = gather_seq("share_moments", 2, jnp.stack([mean_own, spread_own]))
     mean_all = jnp.mean(stats[:, 0], 0)
     var_all = (jnp.sum(stats[:, 1], 0) + mine * jnp.sum((stats[:, 0] - mean_all) ** 2, 0)) * (1.0 / width)
     out_scale = lax.rsqrt(var_all + EPSILON)[:, None]
@@ -403,63 +890,57 @@
     normed_out = out_hat * post_gain + post_shift
     gelu_gate, gelu_pull = jax.vjp(jax.nn.gelu, gate_pre)
     gated_unit = (gelu_gate * normed_out).astype(bf16)
-    branch = lax.psum_scatter(dot(gated_unit, w_o), "seq", scatter_dimension=0, tiled=True)
+    (branch,) = scatter_with("scatter_branch", 3, dot(gated_unit, w_o).astype(bf16), ())
+    inputs = tokens[0].astype(floats)
     residual = inputs + branch
     scale_two = lax.rsqrt(jnp.mean(residual * residual, -1, keepdims=True) + EPSILON)
     normed_mid = residual * scale_two
-    x_two = lax.all_gather((normed_mid * gain_two).astype(bf16), "seq", axis=0, tiled=True)
+    x_two = all_gather_line("gather_mid", 4, (normed_mid * gain_two).astype(bf16))
     hidden_units = packs * units
     gate_up = dot(x_two, w_gu)
     gate_part, up_part = gate_up[:, :hidden_units], gate_up[:, hidden_units:]
     silu_sig = jax.nn.sigmoid(gate_part)
     silu_val = gate_part * silu_sig
     hidden = (silu_val * up_part).astype(bf16)
-    down = lax.psum_scatter(dot(hidden, w_d), "seq", scatter_dimension=0, tiled=True)
-    result = residual + down
-
-    g_down = lax.psum_scatter(cross_rows(hidden, d_top), "dp", scatter_dimension=0, tiled=True)
+    down = lax.psum_scatter(dot(hidden, w_d).astype(bf16), "seq", scatter_dimension=0, tiled=True)
+    result = residual + down.astype(floats)
+
+    g_down = cross_rows(hidden, d_top).astype(bf16)
     d_hidden = cross_cols(d_top, w_d)
     d_gate = d_hidden * up_part * silu_sig * (1.0 + gate_part * (1.0 - silu_sig))
     d_up = d_hidden * silu_val
     d_gate_up = jnp.concatenate([d_gate, d_up], axis=1).astype(bf16)
-    d_xtwo = lax.psum_scatter(cross_cols(d_gate_up, w_gu), "seq", scatter_dimension=0, tiled=True)
-    g_gate_up = return_columns(cross_rows(x_two, d_gate_up))
-    g_gate_up = columns_back(g_gate_up, 2, packs, units)
+    d_xtwo, g_down = scatter_with("scatter_mid", 5, cross_cols(d_gate_up, w_gu).astype(bf16), (g_down,))
+    g_down = add_packs(g_down)
+    g_gate_up = lax.psum_scatter(cross_rows(x_two, d_gate_up).astype(bf16), "dp", scatter_dimension=0, tiled=True)
     g_two = jnp.sum(d_xtwo * normed_mid, axis=0)
     d_mid = d_xtwo * gain_two
     d_residual = grad_out[0].astype(floats) + scale_two * (
         d_mid - normed_mid * jnp.mean(d_mid * normed_mid, -1, keepdims=True)
     )
-    d_branch = lax.all_gather(d_residual.astype(bf16), "seq", axis=0, tiled=True)
-    g_out = cross_rows(gated_unit, d_branch)
+    d_branch = all_gather_line("gather_branch", 6, d_residual.astype(bf16))
+    g_out = cross_rows(gated_unit, d_branch).astype(bf16)
     if aligned:
         g_out = lax.psum_scatter(g_out, "dp", scatter_dimension=0, tiled=True)
     else:
         g_out = lax.psum_scatter(put_rows(g_out), both, scatter_dimension=0, tiled=True)
+    g_out = g_out.astype(floats)
     d_unit = cross_cols(d_branch, w_o)
     d_normed = d_unit * gelu_gate
     g_post_w = jnp.sum(d_normed * out_hat, axis=0)
     g_post_b = jnp.sum(d_normed, axis=0)
     d_hat = d_normed * post_gain
-    sums = lax.psum(jnp.stack([jnp.sum(d_hat, -1), jnp.sum(d_hat * out_hat, -1)]), "seq") * (1.0 / width)
+    sums = gather_seq("share_sums", 7, jnp.stack([jnp.sum(d_hat, -1), jnp.sum(d_hat * out_hat, -1)]))
+    sums = jnp.sum(sums, 0) * (1.0 / width)
     d_mixed = out_scale * (d_hat - sums[0][:, None] - out_hat * sums[1][:, None])
     d_gate_pre = gelu_pull(d_unit * normed_out)[0].astype(bf16)
     d_qkv, d_rate, d_w0, d_c0, d_gain, d_shift = inner_backward(fresh, qkv, e_rows, d_mixed, saved, gain_t, shift_t)
     d_rate = d_rate.reshape(blocks, heads, MB).transpose(0, 2, 1).reshape(length, heads)
     d_logit = (d_rate * (1.0 / HD) * lr_sigm * (1.0 - lr_sigm)).astype(bf16)
     d_mix = jnp.concatenate([d_qkv, d_gate_pre], axis=1)
-    g_mix = return_columns(cross_rows(x_one, d_mix))
-    g_qkv = columns_back(g_mix[:, :, : 3 * mine], 3, outer, inner)
-    g_gate = columns_back(g_mix[:, :, 3 * mine :], 1, outer, inner)
-    d_xone = lax.psum_scatter(
-        cross_cols(d_mix, w_mix) + cross_cols(d_logit, lr_own), "seq", scatter_dimension=0, tiled=True
-    )
+    g_mix = cross_rows(x_one, d_mix).astype(bf16)
+    d_xone = cross_cols(d_mix, w_mix) + cross_cols(d_logit, lr_own)
     g_one = jnp.sum(d_xone * normed_in, axis=0)
-    d_inner = d_xone * gain_one
-    d_tokens = d_residual + scale_one * (
-        d_inner - normed_in * jnp.mean(d_inner * normed_in, -1, keepdims=True)
-    )
-
     def from_token(array):
         return jnp.sum(array.reshape(HD, heads, MB), -1).T.reshape(mine)
 
@@ -481,7 +962,24 @@
     g_small = jnp.concatenate([g_init, g_lr, g_vec], axis=1).reshape(devices, rows, wide)
     g_last = jnp.broadcast_to(jnp.pad(g_bias, (0, wide - heads_all)), (devices, 8, wide))
     g_small = jnp.concatenate([g_small, g_last], axis=1)
-    g_small = lax.psum_scatter(g_small, both, scatter_dimension=0, tiled=True)[0]
+    d_xone, g_mix, g_small = scatter_with("scatter_first", 8, d_xone.astype(bf16), (g_mix, g_small))
+    place_rows = lambda array: array.reshape((per_seq, -1) + array.shape[1:])
+    g_gate_up, g_mix, g_small = swap_places(
+        "return_columns",
+        9,
+        (place_rows(g_gate_up), place_rows(add_packs(g_mix).astype(bf16)), place_rows(add_packs(g_small))),
+    )
+    g_gate_up = columns_back(g_gate_up.astype(floats), 2, packs, units)
+    g_mix = g_mix.astype(floats)
+    g_qkv = columns_back(g_mix[:, :, : 3 * mine], 3, outer, inner)
+    g_gate = columns_back(g_mix[:, :, 3 * mine :], 1, outer, inner)
+    g_small = jnp.sum(g_small, 0).reshape(-1, wide)
+    scale_one = lax.rsqrt(jnp.mean(inputs * inputs, -1, keepdims=True) + EPSILON)
+    normed_in = inputs * scale_one
+    d_inner = d_xone * gain_one
+    d_tokens = d_residual + scale_one * (
+        d_inner - normed_in * jnp.mean(d_inner * normed_in, -1, keepdims=True)
+    )
     g_vec = g_small[:rows, HD + heads_all :]
     return (
         result.astype(bf16)[None],

time: 1370 us -> 911 us (0.66)
  waiting for transfers between devices: 773 us -> 1.98 us
  Pallas kernels: 65 us -> 632 us
  blocking collectives: 253 us -> 0 us
  starting transfers between devices: 15.1 us -> 0.49 us
    pallas_call x0 -> x9, Pallas kernels: none -> 567 us  [talk(): pl.pallas_call(kernel, out_shape=outs, in_specs=[where(i, in_vmem) for i...]
    reduce_scatter x6 -> x2, waiting for transfers between devices: 382 us -> 0.01 us  [the longest x1 0.01 us: on_device(): lax.psum_scatter(dot(hidden, w_d).astype(bf16), 'seq', scatter_dimension=...]
    all_gather x5 -> x1, waiting for transfers between devices: 201 us -> 0.01 us  [on_device(): lax.all_gather(gu_part.reshape(-1, gu_part.shape[-1]), 'dp', axis=0, tile...]
    all_to_all x2 -> x0, blocking collectives: 117 us -> none  [gather_columns(): got = lax.all_to_all(cut, 'seq', 0, 0, tiled=True)]
    unnamed x18 -> x7, waiting for transfers between devices: 97.6 us -> 1.97 us
    unnamed x1 -> x0, blocking collectives: 67.9 us -> none
    all_gather x2 -> x0, blocking collectives: 56.6 us -> none  [the longest x1 41.9 us: on_device(): small = lax.all_gather(small, both, axis=0)]
    all_gather x1, waiting for transfers between devices: 37.4 us -> 0.01 us  [on_device(): w_d = lax.all_gather(w_down, 'dp', axis=0, tiled=True)]
  transfers between devices with their start and end apart: 19 -> 7, of which waited for: 15 -> 0; matrix products, arithmetic and copies ran while one was open for 19% -> 18% of each run, Pallas kernels for 5% -> 49%
where the time goes in v2:
time: 911 us; the launch traced here: 902 us
  Pallas kernels  632 us (69%)
  local copies, waits for them, and re-layouts  117 us (13%)
  matrix products  101 us (11%)
  other arithmetic  34.7 us (4%)
  between operations  15.1 us (2%)
    pallas_call x9, Pallas kernels, talk(): pl.pallas_call(kernel, out_shape=outs, in_specs=[where(i, in_vmem) for i...  567 us
    dot_general x5, matrix products, cross_cols(): lax.dot_general(left_side, right_side, (((1,), (1,)), ((), ())), preferre...  39.5 us
    pallas_call x1, Pallas kernels, inner_backward(): pl.pallas_call(functools.partial(backward_kernel, heads, per), grid=(bloc...  35.5 us
    dot_general x6, matrix products, dot(): return jnp.dot(left_side, right_side, preferred_element_type=jnp.float32)  32.6 us
    pallas_call x1, Pallas kernels, inner_forward(): pl.pallas_call(functools.partial(forward_kernel, heads, per), grid=(block...  29.5 us
    dot_general x5, matrix products, cross_rows(): lax.dot_general(left_side, right_side, (((0,), (0,)), ((), ())), preferre...  29 us
    reshape x5, local copies, waits for them, and re-layouts, columns_back(): return got.reshape(depth, parts * out * per_seq * last)  25.3 us
    unnamed x89, local copies, waits for them, and re-layouts  24.6 us
  transfers between devices with their start and end apart: 7, of which 0 were waited for; matrix products, arithmetic and copies ran while one was open for 18% of the time, Pallas kernels for 49%

profile of v2, /device:TPU:9, one launch (start us, length us, event | category | flops | bytes accessed | tf_op | source)
XLA Modules:
  0.0 902.0 jit_solution(3424035023718055035)
XLA Ops:
  19.4 7.5 reshape.340
  29.0 4.5 reshape.341.refs_2_
  34.8 138.0 %first_exchange.1 = (bf16[4,8,200,64]{3,2,1,0:T(8,128)(2,1)S(1)}, bf16[4,8,64,1024]{3,2,1,0:T(8,128)(2,1)}, bf16[8,64,1376]{2,1,0:T(8,128)(2,1)}, bf16[8,128,2048]{2,1,0:T(8,128)(2,1)}) custom-call(bf16[200,64]{1,0:T(8,128)(2,1)S(1)} %fusion.41.refs_0_, bf16[8,64,1024]{2,1,0:T(8,128)(2,1)S(1)} %pad_maximum_fusion.7.refs_1_, ...), custom_call_target="tpu_custom_call" | custom-call | tf_op jit(solution)/shard_map/first_exchange/pallas_call | solution.py:603
  196.4 5.0 fusion.7.qkv_ref
  201.4 29.5 %inner_forward.1 = (f32[1024,256]{1,0:T(8,128)S(1)}, bf16[64,64,256]{2,1,0:T(8,128)(2,1)S(1)}, f32[64,64,64]{2,1,0:T(8,128)S(1)}, f32[64,64,64]{2,1,0:T(8,128)},...) custom-call(s32[64]{0:T(128)S(1)} %add_convert_fusion.1.fresh_ref, ...), custom_call_target="tpu_custom_call" | custom-call | tf_op jit(solution)/shard_map/inner_forward/pallas_call | solution.py:127
  234.2 5.9 share_moments.1
  241.9 5.0 multiply_convert_fusion.6
  249.3 73.9 %scatter_branch.1 = f32[128,2048]{1,0:T(8,128)S(1)} custom-call(bf16[8,128,2048]{2,1,0:T(8,128)(2,1)S(1)} %bitcast.191), custom_call_target="tpu_custom_call" | custom-call | tf_op jit(solution)/shard_map/scatter_branch/pallas_call | solution.py:603
  324.7 35.5 %gather_mid.1 = bf16[8,128,2048]{2,1,0:T(8,128)(2,1)S(1)} custom-call(bf16[128,2048]{1,0:T(8,128)(2,1)S(1)} %multiply_convert_fusion.5.refs_0_), custom_call_target="tpu_custom_call" | custom-call | tf_op jit(solution)/shard_map/gather_mid/pallas_call | solution.py:603
  365.4 11.1 %fusion.57 = f32[1024,1376]{0,1:T(8,128)} fusion(bf16[1024,2048]{1,0:T(8,128)(2,1)} %bitcast.195, bf16[2048,1376]{1,0:T(8,128)(2,1)} %all-gather.9.cloned.1.call-done), kind=kOutput, calls=%fused_computation.159 | convolution fusion | flops 5771362304 | bytes 15466496 | tf_op jit(solution)/shard_map/dot_general | solution.py:766
  376.6 10.4 %multiply_convert_fusion.3 = (bf16[1024,688]{0,1:T(8,128)(2,1)}, bf16[1024,688]{0,1:T(8,128)(2,1)}, bf16[1024,688]{0,1:T(8,128)(2,1)S(1)}) fusion(f32[1024,1376]{0,1:T(8,128)} %fusion.57, bf16[688,2048]{1,0:T(8,128)(2,1)} %reshape.392, bf16[1,1024,2048]{2,1,0:T(8,128)(2,1)} %all-gather.11.cloned.1.call-done), kind=kOutput, calls=%fused_computation.21 | convolution fusion | flops 2896248832 | bytes 16875520 | tf_op jit(solution)/shard_map/dot_general | solution.py:762
  388.2 4.5 fusion.4
  395.9 11.2 %convolution_convert_fusion.1 = bf16[1024,2048]{1,0:T(8,128)(2,1)} fusion(bf16[2048,1376]{1,0:T(8,128)(2,1)} %all-gather.9.cloned.1.call-done, bf16[1024,688]{0,1:T(8,128)(2,1)} %get-tuple-element.176, bf16[1024,688]{0,1:T(8,128)(2,1)} %get-tuple-element.175), kind=kOutput, calls=%fused_computation.12 | convolution fusion | flops 5779095552 | bytes 12648448 | tf_op jit(solution)/shard_map/dot_general | solution.py:762
  407.1 80.5 %scatter_mid.1 = (f32[128,2048]{1,0:T(8,128)S(1)}, bf16[4,172,2048]{2,1,0:T(8,128)(2,1)S(1)}) custom-call(bf16[8,128,2048]{2,1,0:T(8,128)(2,1)} %bitcast.214, bf16[4,172,2048]{2,1,0:T(8,128)(2,1)} %reshape.357.refs_1_), custom_call_target="tpu_custom_call" | custom-call | tf_op jit(solution)/shard_map/scatter_mid/pallas_call | solution.py:603
  490.8 36.8 %gather_branch.1 = bf16[8,128,2048]{2,1,0:T(8,128)(2,1)S(1)} custom-call(bf16[128,2048]{1,0:T(8,128)(2,1)S(1)} %fusion.54.refs_0_), custom_call_target="tpu_custom_call" | custom-call | tf_op jit(solution)/shard_map/gather_branch/pallas_call | solution.py:603
  532.0 7.7 convolution_convert_fusion.2
  539.8 10.5 %convolution_convert_fusion = bf16[2048,1376]{0,1:T(8,128)(2,1)} fusion(bf16[1024,2048]{1,0:T(8,128)(2,1)} %bitcast.196, bf16[1024,688]{0,1:T(8,128)(2,1)} %get-tuple-element.176, bf16[1024,688]{0,1:T(8,128)(2,1)} %get-tuple-element.175), kind=kOutput, calls=%fused_computation.5 | convolution fusion | flops 5779816448 | bytes 12648448 | tf_op jit(solution)/shard_map/dot_general | solution.py:758
  550.2 6.8 multiply_reduce_fusion.2
  557.1 11.0 %share_sums.1 = f32[8,2,1024]{2,1,0:T(2,128)S(1)} custom-call(f32[2,1024]{1,0:T(2,128)S(1)} %pad_maximum_fusion.9.refs_0_), custom_call_target="tpu_custom_call" | custom-call | tf_op jit(solution)/shard_map/share_sums/pallas_call | solution.py:603
  570.2 35.5 %inner_backward.1 = (bf16[1024,768]{1,0:T(8,128)(2,1)S(1)}, f32[64,1,64]{2,1,0:T(1,128)S(1)}, f32[64,256]{1,0:T(8,128)S(1)}, f32[64,64]{1,0:T(8,128)S(1)}, f32[64,64]{1,0:T(8,128)S(1)}, /*index=5*/f32[64,64]{1,0:T(8,128)S(1)}) custom-call(s32[64]{0:T(128)S(1)} %add_convert_fusion.1.fresh_ref, f32[1024,768]{1,0:T(8,128)} %fusion.7.qkv_ref, ...), custom_call_target="tpu_custom_call" | custom-call | tf_op jit(solution)/shard_map/inner_backward/pallas_call | solution.py:239
  616.9 7.1 fusion.10
  624.1 4.0 multiply_reduce_fusion
  636.0 4.7 concatenate.47
  642.2 8.9 convolution_convert_fusion.4
  651.1 115.8 %scatter_first.1 = (f32[128,2048]{1,0:T(8,128)S(1)}, bf16[4,512,1024]{2,1,0:T(8,128)(2,1)}, f32[4,8,72,103]{3,2,1,0:T(8,128)S(1)}) custom-call(bf16[8,128,2048]{2,1,0:T(8,128)(2,1)} %bitcast.206, bf16[4,512,1024]{2,1,0:T(8,128)(2,1)} %bitcast.213, f32[4,8,72,103]{3,2,1,0:T(8,128)S(1)} %bitcast.194), custom_call_target="tpu_custom_call" | custom-call | tf_op jit(solution)/shard_map/scatter_first/pallas_call | solution.py:603
  767.9 4.4 reduce_sum.259
  774.0 3.6 convert_reduce_fusion
  785.6 69.3 %return_columns.1 = (bf16[8,64,1376]{2,1,0:T(8,128)(2,1)S(1)}, bf16[8,64,1024]{2,1,0:T(8,128)(2,1)S(1)}, f32[8,1,72,103]{3,2,1,0:T(8,128)S(1)}) custom-call(bf16[8,64,1376]{2,1,0:T(8,128)(2,1)S(1)} %bitcast.193, bf16[8,64,1024]{2,1,0:T(8,128)(2,1)S(1)} %bitcast.199, f32[8,1,72,103]{3,2,1,0:T(8,128)S(1)} %bitcast.204), custom_call_target="tpu_custom_call" | custom-call | tf_op jit(solution)/shard_map/return_columns/pallas_call | solution.py:603
  861.5 5.5 copy.239
  875.5 7.6 reshape.388
  883.2 6.6 copy.241
  889.8 5.2 reshape.385
  (243 shorter events, 113.3 us)
Async XLA Ops:
  7.2 6.7 copy-start.20
  7.2 239.6 %all-gather.7.cloned.1.call-start = ((), (), s32[]{:S(2)}) async-start(), calls=%async_computation.3 | async-start | bytes 1310720 | tf_op jit(solution)/shard_map/all_gather | solution.py:858
  7.9 354.3 %all-gather.13.cloned.1.call-start = ((), (), s32[]{:S(2)}) async-start(), calls=%async_computation.9 | async-start | bytes 3604480 | tf_op jit(solution)/shard_map/all_gather | solution.py:861
  8.7 356.7 %all-gather.9.cloned.1.call-start = ((), (), s32[]{:S(2)}) async-start(), calls=%async_computation.4 | async-start | bytes 7208960 | tf_op jit(solution)/shard_map/all_gather | solution.py:856
  26.9 6.8 copy-start.27
  26.9 7.9 copy-start
  174.0 202.6 %all-gather.11.cloned.1.call-start = ((), (), s32[]{:S(2)}) async-start(), calls=%async_computation.8 | async-start | bytes 4718592 | tf_op jit(solution)/shard_map/all_gather | solution.py:862
  174.6 603.0 %reduce-scatter.8.cloned.1.call-start = ((), (), s32[]{:S(2)}) async-start(), calls=%async_computation.7 | async-start | bytes 1310720 | tf_op jit(solution)/shard_map/reduce_scatter | solution.py:924
  178.1 4.6 copy-start.38
  181.2 9.8 %copy-start.24 = (f32[1024]{0:T(1024)}, f32[1024]{0:T(1024)S(1)}, u32[]{:S(2)}) copy-start(f32[1024]{0:T(1024)S(1)} %get-tuple-element.192) | copy-start | bytes 12292
  191.0 5.4 copy-start.36
  323.6 166.9 %copy-start.28 = (f32[128]{0:T(128)}, f32[128]{0:T(128)S(1)}, u32[]{:S(2)}) copy-start(f32[128]{0:T(128)S(1)} %add_rsqrt_fusion.3) | copy-start | bytes 1540
  376.6 11.6 %copy-start.37 = (bf16[1,1024,2048]{2,1,0:T(8,128)(2,1)S(1)}, bf16[1,1024,2048]{2,1,0:T(8,128)(2,1)}, u32[]{:S(2)}) copy-start(bf16[1,1024,2048]{2,1,0:T(8,128)(2,1)} %all-gather.11.cloned.1.call-done) | copy-start | bytes 12582916
  407.1 82.0 %copy-start.16 = (f32[128,2048]{1,0:T(8,128)S(1)}, f32[128,2048]{1,0:T(8,128)}, u32[]{:S(2)}) copy-start(f32[128,2048]{1,0:T(8,128)} %copy-done.15) | copy-start | bytes 3145732
  407.1 83.4 %copy-start.18 = (bf16[1,128,2048]{2,1,0:T(8,128)(2,1)S(1)}, bf16[1,128,2048]{2,1,0:T(8,128)(2,1)}, u32[]{:S(2)}) copy-start(bf16[1,128,2048]{2,1,0:T(8,128)(2,1)} %param.35) | copy-start | bytes 1572868
  490.5 41.4 %copy-start.31 = (f32[128]{0:T(128)}, f32[128]{0:T(128)S(1)}, u32[]{:S(2)}) copy-start(f32[128]{0:T(128)S(1)} %get-tuple-element.199) | copy-start | bytes 1540
  531.9 247.5 %reduce-scatter.4.cloned.1.call-start = ((), (), s32[]{:S(2)}) async-start(), calls=%async_computation.5 | async-start | bytes 4718592 | tf_op jit(solution)/shard_map/reduce_scatter | solution.py:905
  539.7 242.7 %reduce-scatter.6.cloned.1.call-start = ((), (), s32[]{:S(2)}) async-start(), calls=%async_computation.6 | async-start | bytes 7045120 | tf_op jit(solution)/shard_map/reduce_scatter | solution.py:915
  608.3 8.7 copy-start.13
  616.9 7.1 copy-start.14
  616.9 7.1 copy-start.23
  616.9 7.1 copy-start.25
  624.0 5.9 copy-start.26
  624.1 8.0 copy-start.34
  624.1 8.1 copy-start.33
  624.1 9.5 %copy-start.21 = (f32[4,1,64,64]{3,2,1,0:T(8,128)S(1)}, f32[4,1,64,64]{3,2,1,0:T(8,128)}, u32[]{:S(2)}) copy-start(f32[4,1,64,64]{3,2,1,0:T(8,128)} %copy.228) | copy-start | bytes 196612
  633.5 7.2 copy-start.35
  767.9 5.8 copy-start.30
  772.3 7.1 copy-start.29
  772.3 7.1 copy-start.32
  861.5 9.6 %copy-start.19 = (f32[8,64,256]{2,1,0:T(8,128)S(1)}, f32[8,64,256]{2,1,0:T(8,128)}, u32[]{:S(2)}) copy-start(f32[8,64,256]{2,1,0:T(8,128)} %slice.174) | copy-start | bytes 1572868
  867.0 8.5 copy-start.10
  (15 other events, 24.7 us)
Sparse Core Ops, SparseCore 0:
  9.9 27.7 all-gather.6
  39.5 43.8 all-gather.12
  174.1 65.7 all-gather.8
  241.3 75.8 all-gather.10
  532.0 33.5 reduce-scatter.7
  567.9 48.3 reduce-scatter.3
  619.7 94.0 reduce-scatter.5

commit v3 on v2

--- a/solution.py
+++ b/solution.py
@@ -66,8 +66,11 @@
     return jnp.sum(value, axis=0, keepdims=True) * (1.0 / HD)
 
 
-def forward_kernel(heads, per, fresh_ref, qkv_ref, e_ref, w0_ref, c0_ref, gain_ref, shift_ref,
-                   mixed_ref, wsave_ref, hat_ref, slope_ref, gap_ref, bar_ref, rows_ref, w_ref, c_ref):
+def forward_kernel(heads, per, moved, fresh_ref, qkv_ref, e_ref, w0_ref, c0_ref, gain_ref, shift_ref, *refs):
+    sources, refs = refs[:moved], refs[moved:]
+    mixed_ref, wsave_ref, hat_ref, slope_ref, gap_ref, bar_ref, rows_ref = refs[:7]
+    results, (w_ref, c_ref, send_sems, recv_sems) = refs[7 : 7 + moved], refs[7 + moved :]
+    beside(("seq",), send_sems, recv_sems, lambda wires: [swap_seq(wires, a, b) for a, b in zip(sources, results)])
     hi = heads * HD
     own, unit, same, later, _ = head_masks(heads)
     gain, shift, w0, c0 = gain_ref[...], shift_ref[...], w0_ref[...], c0_ref[...]
@@ -116,7 +119,7 @@
     c_ref[...] = c
 
 
-def inner_forward(fresh, qkv, e_rows, w0, c0, gain, shift):
+def inner_forward(cid, fresh, qkv, e_rows, w0, c0, gain, shift, arrays):
     tokens, heads = qkv.shape[0], qkv.shape[1] // (3 * HD)
     ht, hi = heads * MB, heads * HD
     blocks = tokens // MB
@@ -125,33 +128,44 @@
     whole = lambda shape: pl.BlockSpec(shape, lambda i: (0, 0))
     save = pl.BlockSpec((per, HD, ht), lambda i: (i, 0, 0))
     return pl.pallas_call(
-        functools.partial(forward_kernel, heads, per),
+        functools.partial(forward_kernel, heads, per, len(arrays)),
         grid=(blocks // per,),
         in_specs=[
             pl.BlockSpec(memory_space=pltpu.SMEM),
             pl.BlockSpec((per * MB, 3 * hi), lambda i: (i, 0)),
             pl.BlockSpec((per, 1, ht), lambda i: (i, 0, 0)),
             whole((HD, hi)), whole((HD, ht)), whole((HD, ht)), whole((HD, ht)),
-        ],
+        ] + [pl.BlockSpec(memory_space=pl.ANY)] * len(arrays),
         out_specs=[
             pl.BlockSpec((per * MB, hi), lambda i: (i, 0)),
             pl.BlockSpec((per, HD, hi), lambda i: (i, 0, 0)),
             save, save, save, save,
             pl.BlockSpec((per, 4, ht), lambda i: (i, 0, 0)),
-        ],
+        ] + [pl.BlockSpec(memory_space=pl.ANY)] * len(arrays),
         out_shape=[
             jax.ShapeDtypeStruct((tokens, hi), f32),
             jax.ShapeDtypeStruct((blocks, HD, hi), jnp.bfloat16),
-        ] + [jax.ShapeDtypeStruct((blocks, HD, ht), f32)] * 4 + [jax.ShapeDtypeStruct((blocks, 4, ht), f32)],
-        scratch_shapes=[pltpu.VMEM((HD, hi), f32), pltpu.VMEM((HD, ht), f32)],
-        compiler_params=pltpu.CompilerParams(vmem_limit_bytes=48 * 1024 * 1024),
+        ] + [jax.ShapeDtypeStruct((blocks, HD, ht), f32)] * 4 + [jax.ShapeDtypeStruct((blocks, 4, ht), f32)]
+        + [shape_of(a.shape, a.dtype) for a in arrays],
+        scratch_shapes=[pltpu.VMEM((HD, hi), f32), pltpu.VMEM((HD, ht), f32)] + wire_sems(len(arrays) * lax.axis_size("seq")),
+        compiler_params=pltpu.CompilerParams(
+            vmem_limit_bytes=48 * 1024 * 1024, collective_id=cid, has_side_effects=True
+        ),
         name="inner_forward",
-    )(fresh, qkv, e_rows, w0, c0, gain, shift)
-
-
-def backward_kernel(heads, per, fresh_ref, qkv_ref, e_ref, dmix_ref, wsave_ref, hat_ref, slope_ref, gap_ref,
-                    bar_ref, rows_ref, gain_ref, shift_ref,
-                    dqkv_ref, drate_ref, dw0_ref, dc0_ref, dgain_ref, dshift_ref, a_ref, ac_ref):
+    )(fresh, qkv, e_rows, w0, c0, gain, shift, *arrays)
+
+
+def backward_kernel(heads, per, over_seq, over_dp, fresh_ref, qkv_ref, e_ref, dmix_ref, wsave_ref, hat_ref, slope_ref,
+                    gap_ref, bar_ref, rows_ref, gain_ref, shift_ref, *refs):
+    moved = over_seq + over_dp
+    sources, refs = refs[:moved], refs[moved:]
+    dqkv_ref, drate_ref, dw0_ref, dc0_ref, dgain_ref, dshift_ref = refs[:6]
+    results, (a_ref, ac_ref, send_sems, recv_sems) = refs[6 : 6 + moved], refs[6 + moved :]
+    swaps = [swap_seq] * over_seq + [swap_dp] * over_dp
+    beside(
+        ("seq", "dp"), send_sems, recv_sems,
+        lambda wires: [swap(wires, a, b) for swap, a, b in zip(swaps, sources, results)],
+    )
     hi, ht = heads * HD, heads * MB
     own, unit, same, later, earlier = head_masks(heads)
     gain = gain_ref[...]
@@ -225,7 +239,8 @@
     dshift_ref[...] = dshift
 
 
-def inner_backward(fresh, qkv, e_rows, dmix, saved, gain, shift):
+def inner_backward(cid, fresh, qkv, e_rows, dmix, saved, gain, shift, seq_arrays, dp_arrays):
+    arrays = tuple(seq_arrays) + tuple(dp_arrays)
     tokens, heads = qkv.shape[0], qkv.shape[1] // (3 * HD)
     ht, hi = heads * MB, heads * HD
     blocks = tokens // MB
@@ -237,34 +252,42 @@
     two = lambda shape: pl.BlockSpec(shape, lambda i: (last - i, 0))
     save = three((per, HD, ht))
     return pl.pallas_call(
-        functools.partial(backward_kernel, heads, per),
+        functools.partial(backward_kernel, heads, per, len(seq_arrays), len(dp_arrays)),
         grid=(blocks // per,),
         in_specs=[
             pl.BlockSpec(memory_space=pltpu.SMEM),
             two((per * MB, 3 * hi)), three((per, 1, ht)), two((per * MB, hi)),
             three((per, HD, hi)), save, save, save, save, three((per, 4, ht)),
             whole((HD, ht)), whole((HD, ht)),
-        ],
+        ] + [pl.BlockSpec(memory_space=pl.ANY)] * len(arrays),
         out_specs=[
             two((per * MB, 3 * hi)), three((per, 1, ht)),
             whole((HD, hi)), whole((HD, ht)), whole((HD, ht)), whole((HD, ht)),
-        ],
+        ] + [pl.BlockSpec(memory_space=pl.ANY)] * len(arrays),
         out_shape=[
             jax.ShapeDtypeStruct((tokens, 3 * hi), jnp.bfloat16),
             jax.ShapeDtypeStruct((blocks, 1, ht), f32),
             jax.ShapeDtypeStruct((HD, hi), f32),
-        ] + [jax.ShapeDtypeStruct((HD, ht), f32)] * 3,
-        scratch_shapes=[pltpu.VMEM((HD, hi), f32), pltpu.VMEM((HD, ht), f32)],
-        compiler_params=pltpu.CompilerParams(vmem_limit_bytes=48 * 1024 * 1024),
+        ] + [jax.ShapeDtypeStruct((HD, ht), f32)] * 3 + [shape_of(a.shape, a.dtype) for a in arrays],
+        scratch_shapes=[pltpu.VMEM((HD, hi), f32), pltpu.VMEM((HD, ht), f32)]
+        + wire_sems(len(seq_arrays) * lax.axis_size("seq") + len(dp_arrays) * lax.axis_size("dp")),
+        compiler_params=pltpu.CompilerParams(
+            vmem_limit_bytes=48 * 1024 * 1024, collective_id=cid, has_side_effects=True
+        ),
         name="inner_backward",
-    )(fresh, qkv, e_rows, dmix, *saved, gain, shift)
+    )(fresh, qkv, e_rows, dmix, *saved, gain, shift, *arrays)
 
 MESH = pl.DeviceIdType.MESH
 
 
 class Wires:
-    def __init__(self, send_sems, recv_sems):
-        self.send_sems, self.recv_sems, self.used = send_sems, recv_sems, 0
+    def __init__(self, send_sems, recv_sems, started=False):
+        self.send_sems, self.recv_sems, self.used, self.started = send_sems, recv_sems, 0, started
+
+    def begin(self, copy):
+        if not self.started:
+            copy.start()
+        return copy
 
     def copy(self, source, target, device):
         at = self.number()
@@ -380,7 +403,7 @@
         copy("R", 0, part).start()
     for i in range(1, chips):
         for part in range(cut):
-            yield
+            yield True
 
             @pl.when(chip >= i)
             def _():
@@ -402,7 +425,7 @@
 
                 copy("L", i, part).start()
 
-    yield
+    yield True
     own.wait()
     for i in range(chips):
         for part in range(cut):
@@ -468,7 +491,7 @@
             left[dest, part] = wires.copy(to_left.at[dest, lines(part)], from_right.at[dest, lines(part)], on_line(-2))
     for i in range(chips - 1):
         for part in range(cut):
-            yield
+            yield True
             for dest, table, inbox, outbox, ahead, first in (
                 (chips - 1 - i, right, from_left, to_right, chip < chips - 1 - i, chip == 0),
                 (i, left, from_right, to_left, chip > i, chip == chips - 1),
@@ -491,7 +514,7 @@
                     table[dest, part].start()
 
     for part in range(cut):
-        yield
+        yield True
         for dest in range(chips):
 
             @pl.when(chip == dest)
@@ -522,13 +545,13 @@
 def swap_seq(wires, source, out):
     me, count = lax.axis_index("seq"), lax.axis_size("seq")
     own = wires.keep(source.at[me], out.at[me])
-    own.start()
+    wires.begin(own)
     sent = []
     for step in range(1, count):
         peer = lax.rem(me + step, count)
         sent.append(wires.copy(source.at[peer], out.at[me], seq_peer(step)))
-        sent[-1].start()
-    yield
+        wires.begin(sent[-1])
+    yield True
     own.wait()
     for copy in sent:
         copy.wait()
@@ -537,12 +560,12 @@
 def spread_seq(wires, source, out):
     me, count = lax.axis_index("seq"), lax.axis_size("seq")
     own = wires.keep(source, out.at[me])
-    own.start()
+    wires.begin(own)
     sent = []
     for step in range(1, count):
         sent.append(wires.copy(source, out.at[me], seq_peer(step)))
-        sent[-1].start()
-    yield
+        wires.begin(sent[-1])
+    yield True
     own.wait()
     for copy in sent:
         copy.wait()
@@ -551,39 +574,101 @@
 def swap_dp(wires, source, out):
     me, count = lax.axis_index("dp"), lax.axis_size("dp")
     own = wires.keep(source.at[me], out.at[me])
-    own.start()
+    wires.begin(own)
     sent = []
     for step in range(1, count):
         sent.append(wires.copy(source.at[lax.rem(me + step, count)], out.at[me], pack_peer(step)))
-        sent[-1].start()
-    yield
+        wires.begin(sent[-1])
+    yield True
     own.wait()
     for copy in sent:
         copy.wait()
 
 
+PIECES = 4
+HALVES = 8 + 4 * PIECES
+
+
+def halves_dp(wires, source, out):
+    me, count = lax.axis_index("dp"), lax.axis_size("dp")
+    rows, width = source.shape
+    by_rows = rows % (16 * PIECES) == 0
+    step = (rows if by_rows else width) // PIECES
+    own = wires.keep(source, out.at[me])
+    own.start()
+    bit = lax.rem(me, 2)
+    flip = {1: me + 1 - 2 * bit, 2: lax.rem(me + 2, 4)}
+    part = lambda ref, i: ref.at[pl.ds(i * step, step)] if by_rows else ref.at[:, pl.ds(i * step, step)]
+    first, then = {}, {}
+    for i in list(range(PIECES // 2)):
+        for way, j in ((1, i), (2, PIECES // 2 + i)):
+            first[way, j] = wires.copy(part(source, j), part(out.at[me], j), {"dp": flip[way]})
+            first[way, j].start()
+    for i in list(range(PIECES // 2)):
+        for way, j in ((2, i), (1, PIECES // 2 + i)):
+            first[way, j] = wires.copy(part(source, j), part(out.at[me], j), {"dp": flip[way]})
+            first[way, j].start()
+    for i in range(PIECES // 2):
+        for way, j in ((1, i), (2, PIECES // 2 + i)):
+            yield True
+            first[way, j].wait_recv()
+            came = part(out.at[flip[way]], j)
+            then[way, j] = wires.copy(came, came, {"dp": flip[3 - way]})
+            then[way, j].start()
+    yield True
+    own.wait()
+    for i in range(PIECES // 2):
+        for way, j in ((2, i), (1, PIECES // 2 + i)):
+            first[way, j].wait_recv()
+    for copy in first.values():
+        copy.wait_send()
+    for copy in then.values():
+        copy.wait()
+
+
 def spread_dp(wires, source, out):
     me, count = lax.axis_index("dp"), lax.axis_size("dp")
     own = wires.keep(source, out.at[me])
-    own.start()
+    wires.begin(own)
     sent = []
     for step in range(1, count):
         sent.append(wires.copy(source, out.at[me], pack_peer(step)))
-        sent[-1].start()
-    yield
+        wires.begin(sent[-1])
+    yield True
     own.wait()
     for copy in sent:
         copy.wait()
 
 
-def run_all(jobs):
-    jobs = list(jobs)
+def run_all(jobs, patient=()):
+    jobs, patient = list(jobs), list(patient)
+    for job in patient:
+        next(job)
     while jobs:
         for job in list(jobs):
-            try:
-                next(job)
-            except StopIteration:
+            if next(job, False) is False:
                 jobs.remove(job)
+    for job in patient:
+        for _ in job:
+            pass
+
+
+def beside(groups, send_sems, recv_sems, plan):
+    @pl.when(pl.program_id(0) == 0)
+    def _():
+        meet(groups)
+        for job in plan(Wires(send_sems, recv_sems)):
+            next(job)
+
+    @pl.when(pl.program_id(0) == pl.num_programs(0) - 1)
+    def _():
+        for job in plan(Wires(send_sems, recv_sems, started=True)):
+            for _ in job:
+                pass
+
+
+def wire_sems(copies):
+    return [pltpu.SemaphoreType.DMA((copies,)), pltpu.SemaphoreType.DMA((copies,))]
 
 
 def talk(name, cid, groups, operands, outs, plan, copies, in_vmem=(), out_vmem=(), scratch=()):
@@ -594,7 +679,7 @@
         buffers, (send_sems, recv_sems) = refs[n_in + n_out : -2], refs[-2:]
         meet(groups)
         wires = Wires(send_sems, recv_sems)
-        run_all(plan(wires, ins, results, buffers))
+        run_all(*plan(wires, ins, results, buffers))
         assert wires.used <= copies, wires.used
 
     def where(i, chosen):
@@ -613,27 +698,34 @@
     )(*operands)
 
 
-def all_gather_line(name, cid, block, cut=2):
-    count = lax.axis_size("seq")
-    out = jax.ShapeDtypeStruct((count,) + block.shape, block.dtype)
-    (got,) = talk(
-        name, cid, ("line",), (block,), [out],
-        lambda wires, ins, outs, _: [gather_line(wires, ins[0], outs[0], cut)],
-        1 + 4 * (count // 2) * cut,
-    )
-    return got.reshape((-1,) + block.shape[1:])
-
-
-def reduce_scatter_line(name, cid, terms, cut=2):
-    count = lax.axis_size("seq")
-    rows, width = terms.shape[0] // count, terms.shape[1]
-    box = pltpu.VMEM((count // 2, rows, width), terms.dtype)
-    (got,) = talk(
-        name, cid, ("line",), (terms.reshape(count, rows, width),), [jax.ShapeDtypeStruct((rows, width), jnp.float32)],
-        lambda wires, ins, outs, boxes: [scatter_line(wires, ins[0], outs[0], *boxes, cut)],
-        3 * (count // 2) * cut, in_vmem=(0,), out_vmem=(0,), scratch=(box,) * 5,
-    )
-    return got
+def can_halve(array):
+    rows, width = array.shape
+    return lax.axis_size("dp") == 4 and (rows % (16 * PIECES) == 0 or width % (128 * PIECES) == 0)
+
+
+def gather_jobs(wires, arrays, sources, results):
+    jobs, patient = [], []
+    for array, source, result in zip(arrays, sources, results):
+        if can_halve(array):
+            jobs.append(halves_dp(wires, source, result))
+        else:
+            patient.append(spread_dp(wires, source, result))
+    return jobs, patient
+
+
+def gather_with(name, cid, block, over_dp, cut=2):
+    count, packs = lax.axis_size("seq"), lax.axis_size("dp")
+    outs = [shape_of((count,) + block.shape, block.dtype)] + [shape_of((packs,) + a.shape, a.dtype) for a in over_dp]
+
+    def plan(wires, ins, results, _):
+        jobs, patient = gather_jobs(wires, over_dp, ins[1:], results[1:])
+        return [gather_line(wires, ins[0], results[0], cut)] + jobs, patient
+
+    got = talk(
+        name, cid, ("line", "dp") if over_dp else ("line",), (block, *over_dp), outs, plan,
+        1 + 4 * (count // 2) * cut + HALVES * len(over_dp),
+    )
+    return [g.reshape((-1,) + a.shape[1:]) for g, a in zip(got, (block, *over_dp))]
 
 
 def columns_out(wires, source, out):
@@ -648,13 +740,13 @@
         onward.append(wires.copy(source.at[me], out.at[mine, me], pack_peer(step)))
         onward[-1].start()
     for step in range(1, count):
-        yield
+        yield True
         sent[step - 1].wait_recv()
         came = out.at[mine, lax.rem(me + count - step, count)]
         for other in range(1, packs):
             onward.append(wires.copy(came, came, pack_peer(other)))
             onward[-1].start()
-    yield
+    yield True
     own.wait()
     for copy in sent:
         copy.wait_send()
@@ -674,13 +766,13 @@
         onward.append(wires.copy(source, out.at[mine, me], seq_peer(step)))
         onward[-1].start()
     for other in range(1, packs):
-        yield
+        yield True
         sent[other - 1].wait_recv()
         came = out.at[lax.rem(mine + packs - other, packs), me]
         for step in range(1, count):
             onward.append(wires.copy(came, came, seq_peer(step)))
             onward[-1].start()
-    yield
+    yield True
     own.wait()
     for copy in sent:
         copy.wait_send()
@@ -692,62 +784,116 @@
     return jax.ShapeDtypeStruct(tuple(shape), dtype)
 
 
-def first_exchange(small, mix, wide, block):
+def first_exchange(small, mix, block, over_dp):
     packs, count = lax.axis_size("dp"), lax.axis_size("seq")
     outs = [
         shape_of((packs, count) + small.shape, small.dtype),
         shape_of((packs,) + mix.shape, mix.dtype),
-        shape_of(wide.shape, wide.dtype),
         shape_of((count,) + block.shape, block.dtype),
+        shape_of((packs,) + over_dp.shape, over_dp.dtype),
     ]
     cut = 2
 
     def plan(wires, ins, results, _):
         return [
+            spread_all(wires, ins[0], results[0]),
             columns_out(wires, ins[1], results[1]),
-            spread_all(wires, ins[0], results[0]),
-            gather_line(wires, ins[3], results[3], cut),
-            swap_seq(wires, ins[2], results[2]),
-        ]
+            gather_line(wires, ins[2], results[2], cut),
+        ], [spread_dp(wires, ins[3], results[3])]
 
     copies = 3 * (count * packs + count) + 4 * (count // 2) * cut
-    small, mix, wide, block = talk("first_exchange", 1, ("dp", "seq"), (small, mix, wide, block), outs, plan, copies)
-    return small, mix.reshape(-1, mix.shape[-1]), wide, block.reshape(-1, block.shape[-1])
+    small, mix, block, over_dp = talk(
+        "first_exchange", 1, ("dp", "seq"), (small, mix, block, over_dp), outs, plan, copies
+    )
+    flat = lambda array: array.reshape(-1, array.shape[-1])
+    return small, flat(mix), flat(block), flat(over_dp)
 
 
 def gather_seq(name, cid, block):
     count = lax.axis_size("seq")
     (got,) = talk(
         name, cid, ("seq",), (block,), [shape_of((count,) + block.shape, block.dtype)],
-        lambda wires, ins, outs, _: [spread_seq(wires, ins[0], outs[0])], count,
+        lambda wires, ins, outs, _: ([spread_seq(wires, ins[0], outs[0])],), count,
     )
     return got
 
 
-def scatter_with(name, cid, terms, over_dp, cut=2):
+def scatter_with(name, cid, terms, swaps=(), gathers=(), cut=2):
     count, packs = lax.axis_size("seq"), lax.axis_size("dp")
     rows, width = terms.shape[0] // count, terms.shape[1]
     box = pltpu.VMEM((count // 2, rows, width), terms.dtype)
-    blocks = [array.reshape((packs, -1) + array.shape[1:]) for array in over_dp]
+    blocks = [array.reshape((packs, -1) + array.shape[1:]) for array in swaps]
     outs = [shape_of((rows, width), jnp.float32)] + [shape_of(b.shape, b.dtype) for b in blocks]
+    outs += [shape_of((packs,) + a.shape, a.dtype) for a in gathers]
+    n = 1 + len(blocks)
 
     def plan(wires, ins, results, boxes):
-        jobs = [swap_dp(wires, source, result) for source, result in zip(ins[1:], results[1:])]
-        return jobs + [scatter_line(wires, ins[0], results[0], *boxes, cut)]
+        jobs, patient = gather_jobs(wires, gathers, ins[n:], results[n:])
+        patient += [swap_dp(wires, a, b) for a, b in zip(ins[1:n], results[1:n])]
+        return [scatter_line(wires, ins[0], results[0], *boxes, cut)] + jobs, patient
 
     got = talk(
-        name, cid, ("line", "dp") if blocks else ("line",), (terms.reshape(count, rows, width), *blocks), outs, plan,
-        3 * (count // 2) * cut + packs * len(blocks), in_vmem=(0,), out_vmem=(0,), scratch=(box,) * 5,
-    )
-    return got
+        name, cid, ("line", "dp") if swaps or gathers else ("line",),
+        (terms.reshape(count, rows, width), *blocks, *gathers), outs, plan,
+        3 * (count // 2) * cut + packs * len(blocks) + HALVES * len(gathers),
+        in_vmem=(0,), out_vmem=(0,), scratch=(box,) * 5,
+    )
+    return list(got[:n]) + [g.reshape((-1,) + a.shape[1:]) for g, a in zip(got[n:], gathers)]
 
 
 def swap_places(name, cid, arrays):
     count = lax.axis_size("seq")
     return talk(
         name, cid, ("seq",), arrays, [shape_of(a.shape, a.dtype) for a in arrays],
-        lambda wires, ins, outs, _: [swap_seq(wires, i, o) for i, o in zip(ins, outs)], count * len(arrays),
-    )
+        lambda wires, ins, outs, _: ([], [swap_seq(wires, i, o) for i, o in zip(ins, outs)]), count * len(arrays),
+    )
+
+
+def split_columns(arrays, pieces):
+    rows = arrays[0].shape[0]
+    width = sum(p[2] for p in pieces[0])
+    tall = min(rows, 16)
+
+    def kernel(*refs):
+        for place, cuts in enumerate(pieces):
+            refs[-1][place] = jnp.concatenate([refs[a][:, at : at + n] for a, at, n in cuts], axis=1)
+
+    return pl.pallas_call(
+        kernel,
+        grid=(rows // tall,),
+        in_specs=[pl.BlockSpec((tall, a.shape[1]), lambda i: (i, 0)) for a in arrays],
+        out_specs=pl.BlockSpec((len(pieces), tall, width), lambda i: (0, i, 0)),
+        out_shape=shape_of((len(pieces), rows, width), arrays[0].dtype),
+        compiler_params=pltpu.CompilerParams(vmem_limit_bytes=48 * 1024 * 1024),
+        name="split_columns",
+    )(*arrays)
+
+
+def join_columns(array, widths, pieces):
+    places, rows, width = array.shape
+    tall = min(rows, 16)
+
+    def kernel(source, *outs):
+        whole = [source[place].astype(jnp.float32) for place in range(places)]
+        for which, out in enumerate(outs):
+            found = []
+            for place, cuts in enumerate(pieces):
+                start = 0
+                for a, at, n in cuts:
+                    if a == which:
+                        found.append((at, whole[place][:, start : start + n]))
+                    start += n
+            out[...] = jnp.concatenate([part for _, part in sorted(found, key=lambda f: f[0])], axis=1)
+
+    return pl.pallas_call(
+        kernel,
+        grid=(rows // tall,),
+        in_specs=[pl.BlockSpec((places, tall, width), lambda i: (0, i, 0))],
+        out_specs=[pl.BlockSpec((tall, w), lambda i: (i, 0)) for w in widths],
+        out_shape=[shape_of((rows, w), jnp.float32) for w in widths],
+        compiler_params=pltpu.CompilerParams(vmem_limit_bytes=48 * 1024 * 1024),
+        name="join_columns",
+    )(array)
 
 
 def add_packs(array):
@@ -815,27 +961,25 @@
         at = (0, place) + (0,) * (part.ndim - 2)
         return lax.dynamic_update_slice(full, part, at).reshape((width,) + array.shape[1:])
 
-    def by_place(weight, parts, out, last):
-        depth = weight.shape[0]
-        cut = weight.reshape(depth, parts, out, per_seq, last).transpose(3, 0, 1, 2, 4)
-        cut = cut.reshape(per_seq, depth, parts * out * last)
-        return cut
-
-    def columns_back(got, parts, out, last):
-        depth = got.shape[1]
-        got = got.reshape(per_seq, depth, parts, out, last).transpose(1, 2, 3, 0, 4)
-        return got.reshape(depth, parts * out * per_seq * last)
+    feature_cuts = [
+        [(0, (part * outer + o) * per_seq * inner + s * inner, inner) for part in range(3) for o in range(outer)]
+        + [(1, o * per_seq * inner + s * inner, inner) for o in range(outer)]
+        for s in range(per_seq)
+    ]
+    unit_cuts = [
+        [(0, (part * per_seq + s) * units, units) for part in range(2 * packs)] for s in range(per_seq)
+    ]
 
     lanes = max(HD, heads_all)
     pad = lambda array: jnp.pad(array, ((0, 0), (0, lanes - array.shape[1])))
     tags = segments[0].reshape(span // MB, MB)[:, 0].astype(bf16)
     vectors = jnp.stack([norm_one, norm_two, b_init, tnorm_w, tnorm_b, post_w, post_b], axis=1)
     small = jnp.concatenate([pad(w_init), pad(w_lr), pad(vectors), pad(jnp.broadcast_to(tags[None], (8, span // MB)))], axis=0)
-    small, w_mix, gu_part, rows_all = first_exchange(
+    small, w_mix, rows_all, w_o = first_exchange(
         small,
-        jnp.concatenate([by_place(w_qkv, 3, outer, inner), by_place(w_gate, 1, outer, inner)], axis=2),
-        by_place(w_gate_up, 2, packs, units),
+        split_columns((w_qkv, w_gate), feature_cuts),
         tokens[0],
+        w_out,
     )
     small = small.reshape((devices,) + small.shape[2:])
     init_all = small[:, :rows, :HD].reshape(width, HD)
@@ -853,13 +997,11 @@
     bias_own = lax.dynamic_index_in_dim(lr_bias.reshape(outer, per_seq, heads // outer), place, 1, keepdims=False)
     bias_own = bias_own.reshape(heads).astype(floats)
 
-    w_gu = lax.all_gather(gu_part.reshape(-1, gu_part.shape[-1]), "dp", axis=0, tiled=True)
-    if aligned:
-        w_o = lax.all_gather(w_out, "dp", axis=0, tiled=True)
-    else:
+    if not aligned:
         w_o = own_rows(lax.all_gather(w_out, both, axis=0, tiled=True))
-    w_d = lax.all_gather(w_down, "dp", axis=0, tiled=True)
-    d_top = lax.all_gather(grad_out[0], "seq", axis=0, tiled=True)
+    later_top, rows_all = lax.optimization_barrier((grad_out[0], rows_all))
+    d_top = lax.all_gather(later_top, "seq", axis=0, tiled=True)
+    gu_mine = split_columns((w_gate_up,), unit_cuts)
 
     inputs = rows_all.astype(floats)
     scale_one = lax.rsqrt(jnp.mean(inputs * inputs, -1, keepdims=True) + EPSILON)
@@ -878,7 +1020,10 @@
     init_b = vec_own[:, 2].reshape(heads, HD)
     init_b = (init_b - jnp.mean(init_b, -1, keepdims=True)).reshape(-1)
     gain_t, shift_t = by_token(vec_own[:, 3]), by_token(vec_own[:, 4])
-    mixed, *saved = inner_forward(fresh, qkv, e_rows, init_w, by_token(init_b), gain_t, shift_t)
+    *results, gu_part = inner_forward(
+        10, fresh, qkv, e_rows, init_w, by_token(init_b), gain_t, shift_t, (gu_mine,)
+    )
+    mixed, *saved = results
 
     mean_own = jnp.mean(mixed, -1)
     spread_own = jnp.sum((mixed - mean_own[:, None]) ** 2, -1)
@@ -890,12 +1035,13 @@
     normed_out = out_hat * post_gain + post_shift
     gelu_gate, gelu_pull = jax.vjp(jax.nn.gelu, gate_pre)
     gated_unit = (gelu_gate * normed_out).astype(bf16)
-    (branch,) = scatter_with("scatter_branch", 3, dot(gated_unit, w_o).astype(bf16), ())
+    branch_terms, d_top = lax.optimization_barrier((dot(gated_unit, w_o).astype(bf16), d_top))
+    branch, w_gu = scatter_with("scatter_branch", 3, branch_terms, (), (gu_part.reshape(-1, gu_part.shape[-1]),))
     inputs = tokens[0].astype(floats)
     residual = inputs + branch
     scale_two = lax.rsqrt(jnp.mean(residual * residual, -1, keepdims=True) + EPSILON)
     normed_mid = residual * scale_two
-    x_two = all_gather_line("gather_mid", 4, (normed_mid * gain_two).astype(bf16))
+    x_two, w_d = gather_with("gather_mid", 4, (normed_mid * gain_two).astype(bf16), (w_down,))
     hidden_units = packs * units
     gate_up = dot(x_two, w_gu)
     gate_part, up_part = gate_up[:, :hidden_units], gate_up[:, hidden_units:]
@@ -903,28 +1049,24 @@
     silu_val = gate_part * silu_sig
     hidden = (silu_val * up_part).astype(bf16)
     down = lax.psum_scatter(dot(hidden, w_d).astype(bf16), "seq", scatter_dimension=0, tiled=True)
-    result = residual + down.astype(floats)
 
     g_down = cross_rows(hidden, d_top).astype(bf16)
     d_hidden = cross_cols(d_top, w_d)
     d_gate = d_hidden * up_part * silu_sig * (1.0 + gate_part * (1.0 - silu_sig))
     d_up = d_hidden * silu_val
     d_gate_up = jnp.concatenate([d_gate, d_up], axis=1).astype(bf16)
-    d_xtwo, g_down = scatter_with("scatter_mid", 5, cross_cols(d_gate_up, w_gu).astype(bf16), (g_down,))
-    g_down = add_packs(g_down)
-    g_gate_up = lax.psum_scatter(cross_rows(x_two, d_gate_up).astype(bf16), "dp", scatter_dimension=0, tiled=True)
+    g_gate_up = cross_rows(x_two, d_gate_up).astype(bf16)
+    mid_terms, down = lax.optimization_barrier((cross_cols(d_gate_up, w_gu).astype(bf16), down))
+    d_xtwo, g_gate_up = scatter_with("scatter_mid", 5, mid_terms, (g_gate_up,))
+    g_gate_up = add_packs(g_gate_up).astype(bf16)
+    result = residual + down.astype(floats)
     g_two = jnp.sum(d_xtwo * normed_mid, axis=0)
     d_mid = d_xtwo * gain_two
     d_residual = grad_out[0].astype(floats) + scale_two * (
         d_mid - normed_mid * jnp.mean(d_mid * normed_mid, -1, keepdims=True)
     )
-    d_branch = all_gather_line("gather_branch", 6, d_residual.astype(bf16))
+    (d_branch,) = gather_with("gather_branch", 6, d_residual.astype(bf16), ())
     g_out = cross_rows(gated_unit, d_branch).astype(bf16)
-    if aligned:
-        g_out = lax.psum_scatter(g_out, "dp", scatter_dimension=0, tiled=True)
-    else:
-        g_out = lax.psum_scatter(put_rows(g_out), both, scatter_dimension=0, tiled=True)
-    g_out = g_out.astype(floats)
     d_unit = cross_cols(d_branch, w_o)
     d_normed = d_unit * gelu_gate
     g_post_w = jnp.sum(d_normed * out_hat, axis=0)
@@ -934,7 +1076,18 @@
     sums = jnp.sum(sums, 0) * (1.0 / width)
     d_mixed = out_scale * (d_hat - sums[0][:, None] - out_hat * sums[1][:, None])
     d_gate_pre = gelu_pull(d_unit * normed_out)[0].astype(bf16)
-    d_qkv, d_rate, d_w0, d_c0, d_gain, d_shift = inner_backward(fresh, qkv, e_rows, d_mixed, saved, gain_t, shift_t)
+    place_rows = lambda array: array.reshape((per_seq, -1) + array.shape[1:])
+    pack_rows = lambda array: array.reshape((packs, -1) + array.shape[1:])
+    d_qkv, d_rate, d_w0, d_c0, d_gain, d_shift, g_gate_up, g_down, *g_outs = inner_backward(
+        11, fresh, qkv, e_rows, d_mixed, saved, gain_t, shift_t, (place_rows(g_gate_up),),
+        (pack_rows(g_down), pack_rows(g_out)) if aligned else (pack_rows(g_down),),
+    )
+    (g_gate_up,) = join_columns(g_gate_up, (w_gate_up.shape[1],), unit_cuts)
+    g_down = add_packs(g_down)
+    if aligned:
+        g_out = add_packs(g_outs[0])
+    else:
+        g_out = lax.psum_scatter(put_rows(g_out), both, scatter_dimension=0, tiled=True).astype(floats)
     d_rate = d_rate.reshape(blocks, heads, MB).transpose(0, 2, 1).reshape(length, heads)
     d_logit = (d_rate * (1.0 / HD) * lr_sigm * (1.0 - lr_sigm)).astype(bf16)
     d_mix = jnp.concatenate([d_qkv, d_gate_pre], axis=1)
@@ -963,16 +1116,10 @@
     g_last = jnp.broadcast_to(jnp.pad(g_bias, (0, wide - heads_all)), (devices, 8, wide))
     g_small = jnp.concatenate([g_small, g_last], axis=1)
     d_xone, g_mix, g_small = scatter_with("scatter_first", 8, d_xone.astype(bf16), (g_mix, g_small))
-    place_rows = lambda array: array.reshape((per_seq, -1) + array.shape[1:])
-    g_gate_up, g_mix, g_small = swap_places(
-        "return_columns",
-        9,
-        (place_rows(g_gate_up), place_rows(add_packs(g_mix).astype(bf16)), place_rows(add_packs(g_small))),
-    )
-    g_gate_up = columns_back(g_gate_up.astype(floats), 2, packs, units)
-    g_mix = g_mix.astype(floats)
-    g_qkv = columns_back(g_mix[:, :, : 3 * mine], 3, outer, inner)
-    g_gate = columns_back(g_mix[:, :, 3 * mine :], 1, outer, inner)
+    g_mix, g_small = swap_places(
+        "return_columns", 9, (place_rows(add_packs(g_mix).astype(bf16)), place_rows(add_packs(g_small)))
+    )
+    g_qkv, g_gate = join_columns(g_mix, (w_qkv.shape[1], w_gate.shape[1]), feature_cuts)
     g_small = jnp.sum(g_small, 0).reshape(-1, wide)
     scale_one = lax.rsqrt(jnp.mean(inputs * inputs, -1, keepdims=True) + EPSILON)
     normed_in = inputs * scale_one

time: 911 us -> 760 us (0.83)
  Pallas kernels: 632 us -> 525 us
  local copies, waits for them, and re-layouts: 117 us -> 63.9 us
  waiting for transfers between devices: 1.98 us -> 12.1 us
    pallas_call x9, Pallas kernels: 567 us -> 419 us  [talk(): pl.pallas_call(kernel, out_shape=outs, in_specs=[where(i, in_vmem) for i...]
    reshape x17 -> x2, local copies, waits for them, and re-layouts: 53.7 us -> 6.45 us  [the longest x1 3.26 us: on_device(): pack_rows = lambda array: array.reshape((packs, -1) + array.shape[1:])]
    pallas_call x2 -> x6, Pallas kernels: 65 us -> 106 us  [the longest x1 53.5 us: inner_backward(): pl.pallas_call(functools.partial(backward_kernel, heads, per, len(seq_arr...]
    reduce_scatter x1, waiting for transfers between devices: 0.01 us -> 12 us  [on_device(): lax.psum_scatter(dot(hidden, w_d).astype(bf16), 'seq', scatter_dimension=...]
    unnamed x89 -> x136, local copies, waits for them, and re-layouts: 24.6 us -> 26.6 us
  transfers between devices with their start and end apart: 7 -> 2, of which waited for: 0 -> 1; matrix products, arithmetic and copies ran while one was open for 18% -> 11% of each run, Pallas kernels for 49% -> 7%
where the time goes in v3:
time: 760 us; the launch traced here: 753 us
  Pallas kernels  525 us (69%)
  matrix products  102 us (13%)
  local copies, waits for them, and re-layouts  63.9 us (8%)
  other arithmetic  33.9 us (4%)
  between operations  15.5 us (2%)
  waiting for transfers between devices  12.1 us (2%)
    pallas_call x9, Pallas kernels, talk(): pl.pallas_call(kernel, out_shape=outs, in_specs=[where(i, in_vmem) for i...  419 us
    pallas_call x1, Pallas kernels, inner_backward(): pl.pallas_call(functools.partial(backward_kernel, heads, per, len(seq_arr...  53.5 us
    pallas_call x1, Pallas kernels, inner_forward(): pl.pallas_call(functools.partial(forward_kernel, heads, per, len(arrays))...  46.6 us
    dot_general x6, matrix products, dot(): return jnp.dot(left_side, right_side, preferred_element_type=jnp.float32)  35.9 us
    dot_general x5, matrix products, cross_cols(): lax.dot_general(left_side, right_side, (((1,), (1,)), ((), ())), preferre...  35.1 us
    dot_general x5, matrix products, cross_rows(): lax.dot_general(left_side, right_side, (((0,), (0,)), ((), ())), preferre...  31.4 us
    unnamed x136, local copies, waits for them, and re-layouts  26.6 us
    reduce_sum x5, other arithmetic, add_packs(): return jnp.sum(array.astype(jnp.float32), axis=0)  16.6 us
  transfers between devices with their start and end apart: 2, of which 1 were waited for; matrix products, arithmetic and copies ran while one was open for 11% of the time, Pallas kernels for 7%

profile of v3, /device:TPU:9, one launch (start us, length us, event | category | flops | bytes accessed | tf_op | source)
XLA Modules:
  0.0 752.8 jit_solution(17459883745931438958)
XLA Ops:
  15.3 112.4 %first_exchange.1 = (bf16[4,8,200,64]{3,2,1,0:T(8,128)(2,1)S(1)}, bf16[4,8,64,1024]{3,2,1,0:T(8,128)(2,1)}, bf16[8,128,2048]{2,1,0:T(8,128)(2,1)}, bf16[4,64,2048]{2,1,0:T(8,128)(2,1)S(1)}) custom-call(bf16[200,64]{1,0:T(8,128)(2,1)S(1)} %fusion.39.refs_0_, bf16[8,64,1024]{2,1,0:T(8,128)(2,1)S(1)} %split_columns.2.refs_1_, bf16[128,2048]{1,0:T(8,128)(2,1)S(1)} %bitcast.156, ...), custom_call_target="tpu_custom_call" | custom-call | tf_op jit(solution)/shard_map/first_exchange/pallas_call | solution.py:688
  132.9 3.3 fusion.4
  139.4 4.0 broadcast_multiply_fusion.1
  153.0 8.3 %fusion.5.qkv_ref = f32[1024,768]{1,0:T(8,128)} fusion(bf16[1024,2048]{1,0:T(8,128)(2,1)} %fusion.2, bf16[2048,1024]{1,0:T(8,128)(2,1)} %bitcast.227), kind=kOutput, calls=%fused_computation.15 | convolution fusion | flops 3221225472 | bytes 10485760 | tf_op jit(solution)/shard_map/dot_general | solution.py:912
  161.3 46.6 %inner_forward.1 = (f32[1024,256]{1,0:T(8,128)S(1)}, bf16[64,64,256]{2,1,0:T(8,128)(2,1)}, f32[64,64,64]{2,1,0:T(8,128)}, f32[64,64,64]{2,1,0:T(8,128)}, f32[64,...) custom-call(s32[64]{0:T(128)S(1)} %add_convert_fusion.1.fresh_ref, ...), custom_call_target="tpu_custom_call" | custom-call | tf_op jit(solution)/shard_map/inner_forward/pallas_call | solution.py:130
  210.3 4.7 share_moments.1
  216.7 5.1 multiply_convert_fusion.4
  221.7 3.3 convolution_convert_fusion.3
  226.4 59.0 %scatter_branch.1 = (f32[128,2048]{1,0:T(8,128)S(1)}, bf16[4,512,1376]{2,1,0:T(8,128)(2,1)}) custom-call(bf16[8,128,2048]{2,1,0:T(8,128)(2,1)} %bitcast.174, bf16[512,1376]{1,0:T(8,128)(2,1)S(1)} %bitcast.166), custom_call_target="tpu_custom_call" | custom-call | tf_op jit(solution)/shard_map/scatter_branch/pallas_call | solution.py:688
  286.9 35.5 %gather_mid.1 = (bf16[8,128,2048]{2,1,0:T(8,128)(2,1)}, bf16[4,172,2048]{2,1,0:T(8,128)(2,1)S(1)}) custom-call(bf16[128,2048]{1,0:T(8,128)(2,1)S(1)} %multiply_convert_fusion.3.refs_0_, bf16[172,2048]{1,0:T(8,128)(2,1)S(1)} %copy-done.18), custom_call_target="tpu_custom_call" | custom-call | tf_op jit(solution)/shard_map/gather_mid/pallas_call | solution.py:688
  327.2 10.2 %fusion.54 = f32[1024,1376]{0,1:T(8,128)S(1)} fusion(bf16[1024,2048]{1,0:T(8,128)(2,1)} %bitcast.230, bf16[2048,1376]{1,0:T(8,128)(2,1)} %bitcast.225), kind=kOutput, calls=%fused_computation.153 | convolution fusion | flops 5771362304 | bytes 15466496 | tf_op jit(solution)/shard_map/dot_general | solution.py:912
  337.4 5.3 multiply_convert_fusion.2
  343.9 5.1 convolution_convert_fusion.1
  349.0 10.2 %convolution_convert_fusion = bf16[2048,1376]{0,1:T(8,128)(2,1)} fusion(bf16[1024,2048]{1,0:T(8,128)(2,1)} %bitcast.231, bf16[1024,688]{0,1:T(8,128)(2,1)} %get-tuple-element.206, bf16[1024,688]{0,1:T(8,128)(2,1)} %get-tuple-element.205), kind=kOutput, calls=%fused_computation.7 | convolution fusion | flops 5779816448 | bytes 12648448 | tf_op jit(solution)/shard_map/dot_general | solution.py:904
  359.2 8.6 %copy.193 = bf16[2048,1376]{1,0:T(8,128)(2,1)} copy(bf16[2048,1376]{0,1:T(8,128)(2,1)} %convolution_convert_fusion) | data formatting | bytes 11272192 | tf_op jit(solution)/shard_map/convert_element_type | solution.py:1058
  367.8 7.3 convolution_convert_fusion.5
  378.4 11.1 %convolution_convert_fusion.2 = bf16[1024,2048]{1,0:T(8,128)(2,1)} fusion(bf16[2048,1376]{1,0:T(8,128)(2,1)} %bitcast.226, bf16[1024,688]{0,1:T(8,128)(2,1)} %get-tuple-element.206, bf16[1024,688]{0,1:T(8,128)(2,1)} %get-tuple-element.205), kind=kOutput, calls=%fused_computation.11 | convolution fusion | flops 5779095552 | bytes 12648448 | tf_op jit(solution)/shard_map/dot_general | solution.py:908
  389.5 12.0 %reduce-scatter.2.cloned.1.call-done = bf16[128,2048]{1,0:T(8,128)(2,1)} async-done(((bf16[1024,2048]{1,0:T(8,128)(2,1)}), bf16[128,2048]{1,0:T(8,128)(2,1)}) %reduce-scatter.2.cloned.1.call-update) | async-done | bytes 524304 | tf_op jit(solution)/shard_map/reduce_scatter | solution.py:1051
  403.7 65.3 %scatter_mid.1 = (f32[128,2048]{1,0:T(8,128)S(1)}, bf16[4,512,1376]{2,1,0:T(8,128)(2,1)}) custom-call(bf16[8,128,2048]{2,1,0:T(8,128)(2,1)S(1)} %bitcast.160, bf16[4,512,1376]{2,1,0:T(8,128)(2,1)} %bitcast.175), custom_call_target="tpu_custom_call" | custom-call | tf_op jit(solution)/shard_map/scatter_mid/pallas_call | solution.py:688
  469.7 34.7 %gather_branch.1 = bf16[8,128,2048]{2,1,0:T(8,128)(2,1)S(1)} custom-call(bf16[128,2048]{1,0:T(8,128)(2,1)S(1)} %fusion.51.refs_0_), custom_call_target="tpu_custom_call" | custom-call | tf_op jit(solution)/shard_map/gather_branch/pallas_call | solution.py:688
  506.7 3.7 multiply_reduce_fusion
  510.4 9.9 %share_sums.1 = f32[8,2,1024]{2,1,0:T(2,128)S(1)} custom-call(f32[2,1024]{1,0:T(2,128)S(1)} %pad_maximum_fusion.8.refs_0_), custom_call_target="tpu_custom_call" | custom-call | tf_op jit(solution)/shard_map/share_sums/pallas_call | solution.py:688
  520.4 5.0 reduce_sum.272
  528.6 53.5 %inner_backward.1 = (bf16[1024,768]{1,0:T(8,128)(2,1)}, f32[64,1,64]{2,1,0:T(1,128)S(1)}, f32[64,256]{1,0:T(8,128)S(1)}, f32[64,64]{1,0:T(8,128)S(1)}, f32[64,64...) custom-call(s32[64]{0:T(128)S(1)} %add_convert_fusion.1.fresh_ref, ...), custom_call_target="tpu_custom_call" | custom-call | tf_op jit(solution)/shard_map/inner_backward/pallas_call | solution.py:254
  582.1 9.0 %fusion.8 = f32[1024,2048]{1,0:T(8,128)} fusion(bf16[2048,1024]{1,0:T(8,128)(2,1)S(1)} %bitcast.229, bf16[1024,256]{1,0:T(8,128)(2,1)S(1)} %copy-done.63, bf16[1024,768]{1,0:T(8,128)(2,1)} %get-tuple-element.81), kind=kOutput, calls=%fused_computation.32 | convolution fusion | flops 4299161600 | bytes 14680064 | tf_op jit(solution)/shard_map/dot_general | solution.py:908
  591.2 8.7 %convolution_convert_fusion.4 = bf16[2048,1024]{1,0:T(8,128)(2,1)} fusion(bf16[1024,2048]{1,0:T(8,128)(2,1)} %fusion.2, bf16[1024,256]{1,0:T(8,128)(2,1)S(1)} %copy-done.63, bf16[1024,768]{1,0:T(8,128)(2,1)S(1)} %copy-done.59), kind=kOutput, calls=%fused_computation.13 | convolution fusion | flops 4301258752 | bytes 10485760 | tf_op jit(solution)/shard_map/dot_general | solution.py:904
  603.7 6.0 fusion.3
  618.0 3.8 concatenate.43
  621.9 64.1 %scatter_first.1 = (f32[128,2048]{1,0:T(8,128)S(1)}, bf16[4,512,1024]{2,1,0:T(8,128)(2,1)}, f32[4,8,72,103]{3,2,1,0:T(8,128)S(1)}) custom-call(bf16[8,128,2048]{2,1,0:T(8,128)(2,1)} %bitcast.176, bf16[4,512,1024]{2,1,0:T(8,128)(2,1)} %bitcast.181, f32[4,8,72,103]{3,2,1,0:T(8,128)S(1)} %bitcast.157), custom_call_target="tpu_custom_call" | custom-call | tf_op jit(solution)/shard_map/scatter_first/pallas_call | solution.py:688
  687.0 4.4 reduce_sum.281
  694.0 33.0 %return_columns.1 = (bf16[8,64,1024]{2,1,0:T(8,128)(2,1)S(1)}, f32[8,1,72,103]{3,2,1,0:T(8,128)S(1)}) custom-call(bf16[8,64,1024]{2,1,0:T(8,128)(2,1)S(1)} %bitcast.161, f32[8,1,72,103]{3,2,1,0:T(8,128)S(1)} %bitcast.167), custom_call_target="tpu_custom_call" | custom-call | tf_op jit(solution)/shard_map/return_columns/pallas_call | solution.py:688
  740.4 3.6 convert_reduce_fusion
  (259 shorter events, 80.8 us)
Async XLA Ops:
  7.2 217.8 %all-gather.2.cloned.1.call-start = ((), (), s32[]{:S(2)}) async-start(), calls=%async_computation.1 | async-start | bytes 4718592 | tf_op jit(solution)/shard_map/all_gather | solution.py:1003
  127.7 94.1 %copy-start.15 = (bf16[4,64,2048]{2,1,0:T(8,128)(2,1)}, bf16[4,64,2048]{2,1,0:T(8,128)(2,1)S(1)}, u32[]{:S(2)}) copy-start(bf16[4,64,2048]{2,1,0:T(8,128)(2,1)S(1)} %get-tuple-element.62) | copy-start | bytes 3145732
  127.7 273.8 %reduce-scatter.2.cloned.1.call-start = ((), (), s32[]{:S(2)}) async-start(), calls=%async_computation.2 | async-start | bytes 4718592 | tf_op jit(solution)/shard_map/reduce_scatter | solution.py:1051
  131.9 7.5 copy-start.45
  139.4 13.4 %copy-start.56 = (bf16[4,64]{1,0:T(4,128)(2,1)S(1)}, bf16[4,64]{1,0:T(4,128)(2,1)}, u32[]{:S(2)}) copy-start(bf16[4,64]{1,0:T(4,128)(2,1)} %reshape_squeeze.17) | copy-start | bytes 1540
  153.0 8.3 %copy-start.19 = (f32[64,1,64]{2,1,0:T(1,128)S(1)}, f32[64,1,64]{2,1,0:T(1,128)}, u32[]{:S(2)}) copy-start(f32[64,1,64]{2,1,0:T(1,128)} %copy.188.e_ref) | copy-start | bytes 49156
  153.0 8.3 %copy-start.21 = (f32[64,64]{1,0:T(8,128)S(1)}, f32[64,64]{1,0:T(8,128)}, u32[]{:S(2)}) copy-start(f32[64,64]{1,0:T(8,128)} %copy.190.gain_ref) | copy-start | bytes 49156
  153.0 8.3 %copy-start.23 = (f32[64,64]{1,0:T(8,128)S(1)}, f32[64,64]{1,0:T(8,128)}, u32[]{:S(2)}) copy-start(f32[64,64]{1,0:T(8,128)} %copy.191.shift_ref) | copy-start | bytes 49156
  153.0 8.3 %copy-start.25 = (f32[64,256]{1,0:T(8,128)S(1)}, f32[64,256]{1,0:T(8,128)}, u32[]{:S(2)}) copy-start(f32[64,256]{1,0:T(8,128)} %copy.215.w0_ref) | copy-start | bytes 196612
  153.0 8.3 %copy-start.30 = (f32[64,64]{1,0:T(8,128)S(1)}, f32[64,64]{1,0:T(8,128)}, u32[]{:S(2)}) copy-start(f32[64,64]{1,0:T(8,128)} %copy.189.c0_ref) | copy-start | bytes 49156
  216.6 5.1 copy-start.50
  225.0 60.5 %copy-start.1 = (bf16[1,128,2048]{2,1,0:T(8,128)(2,1)S(1)}, bf16[1,128,2048]{2,1,0:T(8,128)(2,1)}, u32[]{:S(2)}) copy-start(bf16[1,128,2048]{2,1,0:T(8,128)(2,1)} %param.18) | copy-start | bytes 1572868
  226.4 60.5 %copy-start.18 = (bf16[172,2048]{1,0:T(8,128)(2,1)S(1)}, bf16[172,2048]{1,0:T(8,128)(2,1)}, u32[]{:S(2)}) copy-start(bf16[172,2048]{1,0:T(8,128)(2,1)} %refs_1_.3) | copy-start | bytes 2113540
  327.2 10.2 %copy-start.40 = (bf16[688,2048]{1,0:T(8,128)(2,1)S(1)}, bf16[688,2048]{1,0:T(8,128)(2,1)}, u32[]{:S(2)}) copy-start(bf16[688,2048]{1,0:T(8,128)(2,1)} %reshape.306) | copy-start | bytes 8454148
  327.2 10.2 %copy-start.58 = (bf16[1024,2048]{1,0:T(8,128)(2,1)S(1)}, bf16[1024,2048]{1,0:T(8,128)(2,1)}, u32[]{:S(2)}) copy-start(bf16[1024,2048]{1,0:T(8,128)(2,1)} %all-gather.2.cloned.1.call-done) | copy-start | bytes 12582916
  403.7 65.3 %copy-start.34 = (f32[128,2048]{1,0:T(8,128)S(1)}, f32[128,2048]{1,0:T(8,128)}, u32[]{:S(2)}) copy-start(f32[128,2048]{1,0:T(8,128)} %copy-done.33) | copy-start | bytes 3145732
  403.7 65.7 %copy-start.36 = (bf16[1,128,2048]{2,1,0:T(8,128)(2,1)S(1)}, bf16[1,128,2048]{2,1,0:T(8,128)(2,1)}, u32[]{:S(2)}) copy-start(bf16[1,128,2048]{2,1,0:T(8,128)(2,1)} %param.35) | copy-start | bytes 1572868
  469.3 35.1 %copy-start.43 = (bf16[1024,256]{1,0:T(8,128)(2,1)S(1)}, bf16[1024,256]{1,0:T(8,128)(2,1)}, u32[]{:S(2)}) copy-start(bf16[1024,256]{1,0:T(8,128)(2,1)} %copy-done.42) | copy-start | bytes 1572868
  520.3 7.0 copy-start.20
  520.4 7.0 copy-start.22
  520.4 7.0 copy-start.24
  520.4 7.0 copy-start.29
  528.6 53.5 %copy-start.57 = (bf16[4,8,64,1024]{3,2,1,0:T(8,128)(2,1)S(1)}, bf16[4,8,64,1024]{3,2,1,0:T(8,128)(2,1)}, u32[]{:S(2)}) copy-start(bf16[4,8,64,1024]{3,2,1,0:T(8,128)(2,1)} %get-tuple-element.60) | copy-start | bytes 12582916
  528.6 53.5 %copy-start.63 = (bf16[1024,256]{1,0:T(8,128)(2,1)S(1)}, bf16[1024,256]{1,0:T(8,128)(2,1)}, u32[]{:S(2)}) copy-start(bf16[1024,256]{1,0:T(8,128)(2,1)} %get-tuple-element.210) | copy-start | bytes 1572868
  582.1 9.1 %copy-start.5 = (bf16[8,64,1376]{2,1,0:T(8,128)(2,1)}, bf16[8,64,1376]{2,1,0:T(8,128)(2,1)S(1)}, u32[]{:S(2)}) copy-start(bf16[8,64,1376]{2,1,0:T(8,128)(2,1)S(1)} %get-tuple-element.95.source) | copy-start | bytes 4227076
  582.1 9.1 %copy-start.12 = (bf16[4,64,2048]{2,1,0:T(8,128)(2,1)}, bf16[4,64,2048]{2,1,0:T(8,128)(2,1)S(1)}, u32[]{:S(2)}) copy-start(bf16[4,64,2048]{2,1,0:T(8,128)(2,1)S(1)} %get-tuple-element.94) | copy-start | bytes 3145732
  582.1 9.0 %copy-start.59 = (bf16[1024,768]{1,0:T(8,128)(2,1)S(1)}, bf16[1024,768]{1,0:T(8,128)(2,1)}, u32[]{:S(2)}) copy-start(bf16[1024,768]{1,0:T(8,128)(2,1)} %get-tuple-element.81) | copy-start | bytes 4718596
  591.2 9.1 %copy-start.49 = (f32[1024,4]{0,1:T(4,128)S(1)}, f32[1024,4]{0,1:T(4,128)}, u32[]{:S(2)}) copy-start(f32[1024,4]{0,1:T(4,128)} %get-tuple-element.222) | copy-start | bytes 49156
  687.0 43.1 %copy-start.46 = (f32[2048,1]{0,1:T(1,128)S(1)}, f32[2048,1]{0,1:T(1,128)}, u32[]{:S(2)}) copy-start(f32[2048,1]{0,1:T(1,128)} %copy-done.45) | copy-start | bytes 24580
  737.9 6.1 copy-start.35
  737.9 6.1 copy-start.37
  737.9 6.1 copy-start.44
  (34 other events, 66.2 us)
Sparse Core Ops, SparseCore 0:
  127.8 51.0 all-gather.1
  349.1 52.3 reduce-scatter.1

commit v4 on v3

--- a/solution.py
+++ b/solution.py
@@ -66,11 +66,16 @@
     return jnp.sum(value, axis=0, keepdims=True) * (1.0 / HD)
 
 
-def forward_kernel(heads, per, moved, fresh_ref, qkv_ref, e_ref, w0_ref, c0_ref, gain_ref, shift_ref, *refs):
+def forward_kernel(heads, per, over_seq, over_dp, fresh_ref, qkv_ref, e_ref, w0_ref, c0_ref, gain_ref, shift_ref, *refs):
+    moved = over_seq + over_dp
     sources, refs = refs[:moved], refs[moved:]
     mixed_ref, wsave_ref, hat_ref, slope_ref, gap_ref, bar_ref, rows_ref = refs[:7]
     results, (w_ref, c_ref, send_sems, recv_sems) = refs[7 : 7 + moved], refs[7 + moved :]
-    beside(("seq",), send_sems, recv_sems, lambda wires: [swap_seq(wires, a, b) for a, b in zip(sources, results)])
+    jobs = [swap_seq] * over_seq + [spread_dp] * over_dp
+    beside(
+        ("seq", "dp"), send_sems, recv_sems,
+        lambda wires: [job(wires, a, b) for job, a, b in zip(jobs, sources, results)],
+    )
     hi = heads * HD
     own, unit, same, later, _ = head_masks(heads)
     gain, shift, w0, c0 = gain_ref[...], shift_ref[...], w0_ref[...], c0_ref[...]
@@ -119,7 +124,9 @@
     c_ref[...] = c
 
 
-def inner_forward(cid, fresh, qkv, e_rows, w0, c0, gain, shift, arrays):
+def inner_forward(cid, fresh, qkv, e_rows, w0, c0, gain, shift, seq_arrays, dp_arrays):
+    arrays = tuple(seq_arrays) + tuple(dp_arrays)
+    packs = lax.axis_size("dp")
     tokens, heads = qkv.shape[0], qkv.shape[1] // (3 * HD)
     ht, hi = heads * MB, heads * HD
     blocks = tokens // MB
@@ -128,7 +135,7 @@
     whole = lambda shape: pl.BlockSpec(shape, lambda i: (0, 0))
     save = pl.BlockSpec((per, HD, ht), lambda i: (i, 0, 0))
     return pl.pallas_call(
-        functools.partial(forward_kernel, heads, per, len(arrays)),
+        functools.partial(forward_kernel, heads, per, len(seq_arrays), len(dp_arrays)),
         grid=(blocks // per,),
         in_specs=[
             pl.BlockSpec(memory_space=pltpu.SMEM),
@@ -146,8 +153,10 @@
             jax.ShapeDtypeStruct((tokens, hi), f32),
             jax.ShapeDtypeStruct((blocks, HD, hi), jnp.bfloat16),
         ] + [jax.ShapeDtypeStruct((blocks, HD, ht), f32)] * 4 + [jax.ShapeDtypeStruct((blocks, 4, ht), f32)]
-        + [shape_of(a.shape, a.dtype) for a in arrays],
-        scratch_shapes=[pltpu.VMEM((HD, hi), f32), pltpu.VMEM((HD, ht), f32)] + wire_sems(len(arrays) * lax.axis_size("seq")),
+        + [shape_of(a.shape, a.dtype) for a in seq_arrays]
+        + [shape_of((packs,) + a.shape, a.dtype) for a in dp_arrays],
+        scratch_shapes=[pltpu.VMEM((HD, hi), f32), pltpu.VMEM((HD, ht), f32)]
+        + wire_sems(len(seq_arrays) * lax.axis_size("seq") + len(dp_arrays) * packs),
         compiler_params=pltpu.CompilerParams(
             vmem_limit_bytes=48 * 1024 * 1024, collective_id=cid, has_side_effects=True
         ),
@@ -155,13 +164,14 @@
     )(fresh, qkv, e_rows, w0, c0, gain, shift, *arrays)
 
 
-def backward_kernel(heads, per, over_seq, over_dp, fresh_ref, qkv_ref, e_ref, dmix_ref, wsave_ref, hat_ref, slope_ref,
+def backward_kernel(heads, per, over_seq, items, fresh_ref, qkv_ref, e_ref, dmix_ref, wsave_ref, hat_ref, slope_ref,
                     gap_ref, bar_ref, rows_ref, gain_ref, shift_ref, *refs):
-    moved = over_seq + over_dp
+    moved = over_seq + len(items)
     sources, refs = refs[:moved], refs[moved:]
+    sources = list(sources[:over_seq]) + [window(ref, item) for ref, item in zip(sources[over_seq:], items)]
     dqkv_ref, drate_ref, dw0_ref, dc0_ref, dgain_ref, dshift_ref = refs[:6]
     results, (a_ref, ac_ref, send_sems, recv_sems) = refs[6 : 6 + moved], refs[6 + moved :]
-    swaps = [swap_seq] * over_seq + [swap_dp] * over_dp
+    swaps = [swap_seq] * over_seq + [swap_dp] * len(items)
     beside(
         ("seq", "dp"), send_sems, recv_sems,
         lambda wires: [swap(wires, a, b) for swap, a, b in zip(swaps, sources, results)],
@@ -239,8 +249,8 @@
     dshift_ref[...] = dshift
 
 
-def inner_backward(cid, fresh, qkv, e_rows, dmix, saved, gain, shift, seq_arrays, dp_arrays):
-    arrays = tuple(seq_arrays) + tuple(dp_arrays)
+def inner_backward(cid, fresh, qkv, e_rows, dmix, saved, gain, shift, seq_arrays, items):
+    arrays = tuple(seq_arrays) + tuple(item[0] for item in items)
     tokens, heads = qkv.shape[0], qkv.shape[1] // (3 * HD)
     ht, hi = heads * MB, heads * HD
     blocks = tokens // MB
@@ -252,7 +262,7 @@
     two = lambda shape: pl.BlockSpec(shape, lambda i: (last - i, 0))
     save = three((per, HD, ht))
     return pl.pallas_call(
-        functools.partial(backward_kernel, heads, per, len(seq_arrays), len(dp_arrays)),
+        functools.partial(backward_kernel, heads, per, len(seq_arrays), items),
         grid=(blocks // per,),
         in_specs=[
             pl.BlockSpec(memory_space=pltpu.SMEM),
@@ -268,9 +278,10 @@
             jax.ShapeDtypeStruct((tokens, 3 * hi), jnp.bfloat16),
             jax.ShapeDtypeStruct((blocks, 1, ht), f32),
             jax.ShapeDtypeStruct((HD, hi), f32),
-        ] + [jax.ShapeDtypeStruct((HD, ht), f32)] * 3 + [shape_of(a.shape, a.dtype) for a in arrays],
+        ] + [jax.ShapeDtypeStruct((HD, ht), f32)] * 3 + [shape_of(a.shape, a.dtype) for a in seq_arrays]
+        + [window_shape(item) for item in items],
         scratch_shapes=[pltpu.VMEM((HD, hi), f32), pltpu.VMEM((HD, ht), f32)]
-        + wire_sems(len(seq_arrays) * lax.axis_size("seq") + len(dp_arrays) * lax.axis_size("dp")),
+        + wire_sems(len(seq_arrays) * lax.axis_size("seq") + len(items) * lax.axis_size("dp")),
         compiler_params=pltpu.CompilerParams(
             vmem_limit_bytes=48 * 1024 * 1024, collective_id=cid, has_side_effects=True
         ),
@@ -600,25 +611,27 @@
     flip = {1: me + 1 - 2 * bit, 2: lax.rem(me + 2, 4)}
     part = lambda ref, i: ref.at[pl.ds(i * step, step)] if by_rows else ref.at[:, pl.ds(i * step, step)]
     first, then = {}, {}
-    for i in list(range(PIECES // 2)):
-        for way, j in ((1, i), (2, PIECES // 2 + i)):
-            first[way, j] = wires.copy(part(source, j), part(out.at[me], j), {"dp": flip[way]})
-            first[way, j].start()
-    for i in list(range(PIECES // 2)):
-        for way, j in ((2, i), (1, PIECES // 2 + i)):
-            first[way, j] = wires.copy(part(source, j), part(out.at[me], j), {"dp": flip[way]})
-            first[way, j].start()
-    for i in range(PIECES // 2):
-        for way, j in ((1, i), (2, PIECES // 2 + i)):
+
+    def send(way, j):
+        first[way, j] = wires.copy(part(source, j), part(out.at[me], j), {"dp": flip[way]})
+        first[way, j].start()
+
+    half = PIECES // 2
+    for i in range(half):
+        send(1, i)
+        send(2, half + i)
+    for i in range(half):
+        for way, j in ((1, i), (2, half + i)):
             yield True
             first[way, j].wait_recv()
             came = part(out.at[flip[way]], j)
             then[way, j] = wires.copy(came, came, {"dp": flip[3 - way]})
             then[way, j].start()
+            send(3 - way, j)
     yield True
     own.wait()
-    for i in range(PIECES // 2):
-        for way, j in ((2, i), (1, PIECES // 2 + i)):
+    for i in range(half):
+        for way, j in ((2, i), (1, half + i)):
             first[way, j].wait_recv()
     for copy in first.values():
         copy.wait_send()
@@ -713,19 +726,41 @@
     return jobs, patient
 
 
-def gather_with(name, cid, block, over_dp, cut=2):
+def window(ref, item):
+    _, rows, columns = item
+    if rows is None and columns is None:
+        return ref
+    lines = slice(None) if rows is None else pl.ds(rows[0], rows[1] - rows[0])
+    lanes = slice(None) if columns is None else pl.ds(columns[0], columns[1] - columns[0])
+    return ref.at[:, lines, lanes]
+
+
+def window_shape(item):
+    array, rows, columns = item
+    shape = list(array.shape)
+    if rows is not None:
+        shape[1] = rows[1] - rows[0]
+    if columns is not None:
+        shape[2] = columns[1] - columns[0]
+    return shape_of(shape, array.dtype)
+
+
+def gather_with(name, cid, block, over_dp, swaps=(), cut=2):
     count, packs = lax.axis_size("seq"), lax.axis_size("dp")
     outs = [shape_of((count,) + block.shape, block.dtype)] + [shape_of((packs,) + a.shape, a.dtype) for a in over_dp]
+    outs += [window_shape(item) for item in swaps]
+    n = 1 + len(over_dp)
 
     def plan(wires, ins, results, _):
-        jobs, patient = gather_jobs(wires, over_dp, ins[1:], results[1:])
+        jobs, patient = gather_jobs(wires, over_dp, ins[1:n], results[1:n])
+        patient += [swap_dp(wires, window(a, item), b) for a, b, item in zip(ins[n:], results[n:], swaps)]
         return [gather_line(wires, ins[0], results[0], cut)] + jobs, patient
 
     got = talk(
-        name, cid, ("line", "dp") if over_dp else ("line",), (block, *over_dp), outs, plan,
-        1 + 4 * (count // 2) * cut + HALVES * len(over_dp),
-    )
-    return [g.reshape((-1,) + a.shape[1:]) for g, a in zip(got, (block, *over_dp))]
+        name, cid, ("line", "dp") if over_dp or swaps else ("line",), (block, *over_dp, *(i[0] for i in swaps)), outs, plan,
+        1 + 4 * (count // 2) * cut + HALVES * len(over_dp) + packs * len(swaps),
+    )
+    return [g.reshape((-1,) + a.shape[1:]) for g, a in zip(got, (block, *over_dp))] + list(got[n:])
 
 
 def columns_out(wires, source, out):
@@ -784,29 +819,21 @@
     return jax.ShapeDtypeStruct(tuple(shape), dtype)
 
 
-def first_exchange(small, mix, block, over_dp):
+def first_exchange(mix, block, over_dp):
     packs, count = lax.axis_size("dp"), lax.axis_size("seq")
-    outs = [
-        shape_of((packs, count) + small.shape, small.dtype),
-        shape_of((packs,) + mix.shape, mix.dtype),
-        shape_of((count,) + block.shape, block.dtype),
-        shape_of((packs,) + over_dp.shape, over_dp.dtype),
-    ]
+    outs = [shape_of((packs,) + mix.shape, mix.dtype), shape_of((count,) + block.shape, block.dtype)]
+    outs += [shape_of((packs,) + a.shape, a.dtype) for a in over_dp]
     cut = 2
 
     def plan(wires, ins, results, _):
         return [
-            spread_all(wires, ins[0], results[0]),
-            columns_out(wires, ins[1], results[1]),
-            gather_line(wires, ins[2], results[2], cut),
-        ], [spread_dp(wires, ins[3], results[3])]
-
-    copies = 3 * (count * packs + count) + 4 * (count // 2) * cut
-    small, mix, block, over_dp = talk(
-        "first_exchange", 1, ("dp", "seq"), (small, mix, block, over_dp), outs, plan, copies
-    )
-    flat = lambda array: array.reshape(-1, array.shape[-1])
-    return small, flat(mix), flat(block), flat(over_dp)
+            columns_out(wires, ins[0], results[0]),
+            gather_line(wires, ins[1], results[1], cut),
+        ], [spread_dp(wires, a, b) for a, b in zip(ins[2:], results[2:])]
+
+    copies = count * packs + count + 4 * (count // 2) * cut + packs * len(over_dp) + 8
+    got = talk("first_exchange", 1, ("dp", "seq"), (mix, block, *over_dp), outs, plan, copies)
+    return [array.reshape(-1, array.shape[-1]) for array in got]
 
 
 def gather_seq(name, cid, block):
@@ -822,14 +849,14 @@
     count, packs = lax.axis_size("seq"), lax.axis_size("dp")
     rows, width = terms.shape[0] // count, terms.shape[1]
     box = pltpu.VMEM((count // 2, rows, width), terms.dtype)
-    blocks = [array.reshape((packs, -1) + array.shape[1:]) for array in swaps]
-    outs = [shape_of((rows, width), jnp.float32)] + [shape_of(b.shape, b.dtype) for b in blocks]
+    blocks = [item[0] for item in swaps]
+    outs = [shape_of((rows, width), jnp.float32)] + [window_shape(item) for item in swaps]
     outs += [shape_of((packs,) + a.shape, a.dtype) for a in gathers]
     n = 1 + len(blocks)
 
     def plan(wires, ins, results, boxes):
         jobs, patient = gather_jobs(wires, gathers, ins[n:], results[n:])
-        patient += [swap_dp(wires, a, b) for a, b in zip(ins[1:n], results[1:n])]
+        patient += [swap_dp(wires, window(a, item), b) for a, b, item in zip(ins[1:n], results[1:n], swaps)]
         return [scatter_line(wires, ins[0], results[0], *boxes, cut)] + jobs, patient
 
     got = talk(
@@ -856,7 +883,9 @@
 
     def kernel(*refs):
         for place, cuts in enumerate(pieces):
-            refs[-1][place] = jnp.concatenate([refs[a][:, at : at + n] for a, at, n in cuts], axis=1)
+            refs[-1][place] = jnp.concatenate(
+                [jnp.zeros((tall, n), refs[-1].dtype) if a is None else refs[a][:, at : at + n] for a, at, n in cuts], axis=1
+            )
 
     return pl.pallas_call(
         kernel,
@@ -898,6 +927,332 @@
 
 def add_packs(array):
     return jnp.sum(array.astype(jnp.float32), axis=0)
+
+
+def unit_groups(units):
+    return [(at, min(128, units - at)) for at in range(0, units, 128)]
+
+
+def feed_forward_kernel(
+    cut, block_ref, top_ref, wgu_hbm, wd_hbm,
+    x_out, hid_out, dgu_out, down_out, mid_out,
+    wgu_ref, wd_ref, xbuf, topbuf, hidbuf, dgubuf, downbuf, terms, near, from_left, from_right, outbox,
+    local_sems, line_send, line_recv, near_send, near_recv, sum_send, sum_recv, across_send, across_recv,
+):
+    me, count = lax.axis_index("seq"), lax.axis_size("seq")
+    chips, chip, core = count // 2, me // 2, lax.rem(me, 2)
+    other = me + 1 - 2 * core
+    tall = block_ref.shape[0]
+    step = tall // cut
+    units = wd_ref.shape[0]
+    width = wd_ref.shape[1]
+    meet(("line",))
+
+    def lines(part):
+        return pl.ds(part * step, step)
+
+    def along(sign, i, part, source=None):
+        at = ((1 - sign) // 2 * chips + i) * cut + part
+        slot = x_out.at[me + 2 * sign * i, lines(part)]
+        return pltpu.make_async_remote_copy(
+            slot if source is None else source.at[lines(part)], slot,
+            line_send.at[at], line_recv.at[at], on_line(-2 * sign), MESH,
+        )
+
+    def over(sign, i, part, source=None):
+        at = ((1 - sign) // 2 * chips + i) * cut + part
+        slot = x_out.at[me + 2 * sign * i, lines(part)]
+        return pltpu.make_async_remote_copy(
+            slot if source is None else source.at[lines(part)], slot,
+            near_send.at[at], near_recv.at[at], sibling(), MESH,
+        )
+
+    def along_came(sign, i, part):
+        at = ((1 - sign) // 2 * chips + i - 1) * cut + part
+        slot = x_out.at[me + 2 * sign * i, lines(part)]
+        pltpu.make_async_remote_copy(slot, slot, line_send.at[at], line_recv.at[at], sibling(), MESH).wait_recv()
+
+    def over_came(sign, i, part):
+        at = ((1 - sign) // 2 * chips + i) * cut + part
+        slot = x_out.at[other + 2 * sign * i, lines(part)]
+        pltpu.make_async_remote_copy(slot, slot, near_send.at[at], near_recv.at[at], sibling(), MESH).wait_recv()
+
+    def more(sign):
+        return jnp.where(sign > 0, chip > 0, chip < chips - 1)
+
+    def across(dest, part):
+        at = dest * cut + part
+        return pltpu.make_async_remote_copy(
+            terms.at[2 * dest + 1 - core, lines(part)], near.at[dest, lines(part)],
+            across_send.at[at], across_recv.at[at], sibling(), MESH,
+        )
+
+    def onward(right, dest, part):
+        at = ((0 if right else chips) + dest) * cut + part
+        inbox = from_left if right else from_right
+        return pltpu.make_async_remote_copy(
+            outbox.at[dest, lines(part)], inbox.at[dest, lines(part)],
+            sum_send.at[at], sum_recv.at[at], on_line(2 if right else -2), MESH,
+        )
+
+    own = pltpu.make_async_copy(block_ref, x_out.at[me], local_sems.at[0])
+    own.start()
+    for part in range(cut):
+        for sign in (1, -1):
+
+            @pl.when(more(sign))
+            def _():
+                along(sign, 0, part, block_ref).start()
+
+        over(1, 0, part, block_ref).start()
+    weights = [
+        pltpu.make_async_copy(wgu_hbm, wgu_ref, local_sems.at[1]),
+        pltpu.make_async_copy(wd_hbm, wd_ref, local_sems.at[2]),
+    ]
+    for copy in weights:
+        copy.start()
+    own.wait()
+    for copy in weights:
+        copy.wait()
+
+    def compute(dest):
+        x = xbuf[...].reshape(2 * tall, width)
+        top = topbuf[...].reshape(2 * tall, width)
+        for at, n in unit_groups(units):
+            both = nn(x, wgu_ref[:, 2 * at : 2 * at + 2 * n])
+            gate, up = both[:, :n], both[:, n:]
+            d_hidden = nt(top, wd_ref[at : at + n, :])
+            sig = 1.0 / (1.0 + jnp.exp(-gate))
+            silu = gate * sig
+            hidbuf[:, :, at : at + n] = (silu * up).astype(jnp.bfloat16).reshape(2, tall, n)
+            d_gate = d_hidden * up * sig * (1.0 + gate * (1.0 - sig))
+            d_both = jnp.concatenate([d_gate, d_hidden * silu], axis=1)
+            dgubuf[:, :, 2 * at : 2 * at + 2 * n] = d_both.astype(jnp.bfloat16).reshape(2, tall, 2 * n)
+        hid = hidbuf[...].reshape(2 * tall, units)
+        dgu = dgubuf[...].reshape(2 * tall, 2 * units)
+        wide = 512
+        for at in range(0, width, wide):
+            mid = nt(dgu, wgu_ref[at : at + wide, :]).astype(jnp.bfloat16)
+            terms[pl.ds(2 * dest, 2), :, at : at + wide] = mid.reshape(2, tall, wide)
+        for part in range(cut):
+            across(dest, part).start()
+        for at in range(0, width, wide):
+            downbuf[:, :, at : at + wide] = nn(hid, wd_ref[:, at : at + wide]).astype(jnp.bfloat16).reshape(2, tall, wide)
+
+    def send_sum(right, dest, part, first, in_turn=True):
+        mine = [terms.at[2 * dest + core, lines(part)], near.at[dest, lines(part)]]
+        across_came(dest, part)
+        if first:
+            add_into(outbox.at[dest, lines(part)], mine)
+        else:
+            inbox = from_left if right else from_right
+            sum_came(right, dest, part)
+            add_into(outbox.at[dest, lines(part)], mine + [inbox.at[dest, lines(part)]])
+        if in_turn and part > 0:
+            onward(right, dest, part - 1).wait_send()
+        onward(right, dest, part).start()
+
+    def across_came(dest, part):
+        at = dest * cut + part
+        there = near.at[dest, lines(part)]
+        pltpu.make_async_remote_copy(there, there, across_send.at[at], across_recv.at[at], sibling(), MESH).wait_recv()
+
+    def sum_came(right, dest, part):
+        at = ((0 if right else chips) + dest) * cut + part
+        there = (from_left if right else from_right).at[dest, lines(part)]
+        pltpu.make_async_remote_copy(there, there, sum_send.at[at], sum_recv.at[at], sibling(), MESH).wait_recv()
+
+    def inside(dest):
+        return (dest >= 0) & (dest < chips)
+
+    def visit(i, j):
+        sign = 1 - 2 * j
+        dest = chip + sign * i
+
+        @pl.when(inside(dest) & (i + 1 - j > 0))
+        def _():
+            top = pltpu.make_async_copy(top_ref.at[pl.ds(2 * dest, 2)], topbuf, local_sems.at[1])
+            top.start()
+            for part in range(cut):
+                over_came(sign, i, part)
+            x = pltpu.make_async_copy(x_out.at[pl.ds(2 * dest, 2)], xbuf, local_sems.at[0])
+            x.start()
+            top.wait()
+            x.wait()
+            compute(dest)
+            saved = [
+                pltpu.make_async_copy(hidbuf, hid_out.at[pl.ds(2 * dest, 2)], local_sems.at[0]),
+                pltpu.make_async_copy(dgubuf, dgu_out.at[pl.ds(2 * dest, 2)], local_sems.at[1]),
+                pltpu.make_async_copy(downbuf, down_out.at[pl.ds(2 * dest, 2)], local_sems.at[2]),
+            ]
+            for copy in saved:
+                copy.start()
+
+            @pl.when((chip == 0) & (dest > 0) & (dest < chips - 1))
+            def _():
+                for part in range(cut):
+                    send_sum(True, dest, part, True, False)
+
+            @pl.when((chip == chips - 1) & (dest < chips - 1) & (dest > 0))
+            def _():
+                for part in range(cut):
+                    send_sum(False, dest, part, True, False)
+
+            for copy in saved:
+                copy.wait()
+
+    def distance(i, _):
+        for sign in (1, -1):
+
+            @pl.when((i > 0) & inside(chip + sign * i))
+            def _():
+                for part in range(cut):
+                    along_came(sign, i, part)
+
+                    @pl.when(more(sign))
+                    def _():
+                        along(sign, i, part).start()
+
+                    over(sign, i, part).start()
+
+        def side(j, _):
+            visit(i, j)
+            return 0
+
+        lax.fori_loop(0, 2, side, 0)
+        return 0
+
+    lax.fori_loop(0, chips, distance, 0)
+
+    @pl.when(chip == 0)
+    def _():
+        for part in range(cut):
+            send_sum(True, chips - 1, part, True)
+
+    @pl.when(chip == chips - 1)
+    def _():
+        for part in range(cut):
+            send_sum(False, 0, part, True)
+
+    def rightward():
+        for i in range(1, chips - 1):
+
+            @pl.when((chip > 0) & (chip + i < chips))
+            def _():
+                for part in range(cut):
+                    send_sum(True, chip + i, part, False)
+
+    def leftward():
+        for i in range(1, chips - 1):
+
+            @pl.when((chip < chips - 1) & (chip - i >= 0))
+            def _():
+                for part in range(cut):
+                    send_sum(False, chip - i, part, False)
+
+    @pl.when(chip < chips // 2)
+    def _():
+        rightward()
+        leftward()
+
+    @pl.when(chip >= chips // 2)
+    def _():
+        leftward()
+        rightward()
+
+    for part in range(cut):
+        across_came(chip, part)
+        mine = [terms.at[2 * chip + core, lines(part)], near.at[chip, lines(part)]]
+        left_in, right_in = from_left.at[chip, lines(part)], from_right.at[chip, lines(part)]
+
+        @pl.when(chip == 0)
+        def _():
+            sum_came(False, chip, part)
+            add_into(mid_out.at[lines(part)], mine + [right_in])
+
+        @pl.when(chip == chips - 1)
+        def _():
+            sum_came(True, chip, part)
+            add_into(mid_out.at[lines(part)], mine + [left_in])
+
+        @pl.when((chip > 0) & (chip < chips - 1))
+        def _():
+            sum_came(True, chip, part)
+            sum_came(False, chip, part)
+            add_into(mid_out.at[lines(part)], mine + [left_in, right_in])
+
+    for part in range(cut):
+        for dest in range(chips):
+            across(dest, part).wait_send()
+
+            early_right = (chip == 0) & (dest < chips - 1) | (part == cut - 1)
+            early_left = (chip == chips - 1) & (dest > 0) | (part == cut - 1)
+
+            @pl.when((chip < dest) & early_right)
+            def _():
+                onward(True, dest, part).wait_send()
+
+            @pl.when((chip > dest) & early_left)
+            def _():
+                onward(False, dest, part).wait_send()
+
+        for i in range(chips):
+            for sign in (1, -1):
+                there = (chip + sign * i >= 0) & (chip + sign * i < chips)
+
+                @pl.when(there & more(sign))
+                def _():
+                    along(sign, i, part).wait_send()
+
+                if i > 0 or sign > 0:
+
+                    @pl.when(there)
+                    def _():
+                        over(sign, i, part).wait_send()
+
+
+def feed_forward(cid, block, top, w_gu, w_d, cut=2):
+    count = lax.axis_size("seq")
+    chips = count // 2
+    tall, width = block.shape
+    units = w_d.shape[0]
+    bf16 = jnp.bfloat16
+    outs = [
+        shape_of((count, tall, width), bf16),
+        shape_of((count, tall, units), bf16),
+        shape_of((count, tall, 2 * units), bf16),
+        shape_of((count, tall, width), bf16),
+        shape_of((tall, width), jnp.float32),
+    ]
+    box = pltpu.VMEM((chips, tall, width), bf16)
+    dma = lambda n: pltpu.SemaphoreType.DMA((n,))
+    anywhere, vmem = pl.BlockSpec(memory_space=pl.ANY), pl.BlockSpec(memory_space=pltpu.VMEM)
+    flops = 2 * 2 * count * tall * width * 3 * units
+    got = pl.pallas_call(
+        functools.partial(feed_forward_kernel, cut),
+        out_shape=outs,
+        in_specs=[anywhere] * 4,
+        out_specs=[anywhere] * 4 + [vmem],
+        scratch_shapes=[
+            pltpu.VMEM(w_gu.shape, bf16),
+            pltpu.VMEM(w_d.shape, bf16),
+            pltpu.VMEM((2, tall, width), bf16),
+            pltpu.VMEM((2, tall, width), bf16),
+            pltpu.VMEM((2, tall, units), bf16),
+            pltpu.VMEM((2, tall, 2 * units), bf16),
+            pltpu.VMEM((2, tall, width), bf16),
+            pltpu.VMEM((count, tall, width), bf16),
+            box, box, box, box,
+            dma(3),
+        ] + [dma(2 * chips * cut)] * 6 + [dma(chips * cut)] * 2,
+        compiler_params=pltpu.CompilerParams(
+            collective_id=cid, has_side_effects=True, vmem_limit_bytes=56 * 1024 * 1024
+        ),
+        cost_estimate=pl.CostEstimate(flops=flops, bytes_accessed=20 << 20, transcendentals=0),
+        name="feed_forward",
+    )(block, top.reshape(count, tall, width), w_gu, w_d)
+    flat = [g.reshape(-1, g.shape[-1]) for g in got]
+    return flat
 
 
 def cross_rows(left_side, right_side):
@@ -961,44 +1316,60 @@
         at = (0, place) + (0,) * (part.ndim - 2)
         return lax.dynamic_update_slice(full, part, at).reshape((width,) + array.shape[1:])
 
+    extra = 128
     feature_cuts = [
         [(0, (part * outer + o) * per_seq * inner + s * inner, inner) for part in range(3) for o in range(outer)]
         + [(1, o * per_seq * inner + s * inner, inner) for o in range(outer)]
         for s in range(per_seq)
     ]
-    unit_cuts = [
-        [(0, (part * per_seq + s) * units, units) for part in range(2 * packs)] for s in range(per_seq)
-    ]
-
-    lanes = max(HD, heads_all)
-    pad = lambda array: jnp.pad(array, ((0, 0), (0, lanes - array.shape[1])))
-    tags = segments[0].reshape(span // MB, MB)[:, 0].astype(bf16)
-    vectors = jnp.stack([norm_one, norm_two, b_init, tnorm_w, tnorm_b, post_w, post_b], axis=1)
-    small = jnp.concatenate([pad(w_init), pad(w_lr), pad(vectors), pad(jnp.broadcast_to(tags[None], (8, span // MB)))], axis=0)
-    small, w_mix, rows_all, w_o = first_exchange(
-        small,
-        split_columns((w_qkv, w_gate), feature_cuts),
-        tokens[0],
-        w_out,
-    )
-    small = small.reshape((devices,) + small.shape[2:])
-    init_all = small[:, :rows, :HD].reshape(width, HD)
-    lr_all = small[:, rows : 2 * rows, :heads_all].reshape(width, heads_all)
-    vec_all = small[:, 2 * rows : 3 * rows, :7].reshape(width, 7)
-    pack_tags = lax.dynamic_index_in_dim(
-        small[:, 3 * rows, : span // MB].reshape(packs, blocks), lax.axis_index("dp"), 0, keepdims=False
-    )
+    filled = -(-units // 16) * 16
+    unit_cuts = []
+    for s in range(per_seq):
+        cuts = []
+        for at, n in unit_groups(packs * filled):
+            for part in range(2):
+                u = at
+                while u < at + n:
+                    pack, i = divmod(u, filled)
+                    run = min((units if i < units else filled) - i, at + n - u)
+                    first = (part * packs * per_seq + pack * per_seq + s) * units + i
+                    cuts.append((0, first, run) if i < units else (None, 0, run))
+                    u += run
+        unit_cuts.append(cuts)
+
+    spans = span // MB
+    lr_places = w_lr.reshape(rows, outer, per_seq, heads // outer).transpose(0, 2, 1, 3).reshape(rows, per_seq, heads)
+    tags = segments[0].reshape(1, 1, spans, MB)[:, :, :, 0].astype(bf16)
+    beside_cols = jnp.concatenate(
+        [
+            lr_places,
+            jnp.broadcast_to(jnp.stack([norm_one, norm_two], axis=1)[:, None], (rows, per_seq, 2)),
+            jnp.broadcast_to(tags, (rows, per_seq, spans)),
+            jnp.zeros((rows, per_seq, extra - heads - 2 - spans), bf16),
+        ],
+        axis=2,
+    ).reshape(rows, per_seq * extra)
+    mix_cuts = [cuts + [(2, s * extra, extra)] for s, cuts in enumerate(feature_cuts)]
+    vectors = jnp.stack([b_init, tnorm_w, tnorm_b, post_w, post_b], axis=1)
+    head_rows = jnp.concatenate([w_init, vectors, jnp.zeros((rows, extra - HD - 5), bf16)], axis=1)
+    over_dp = (w_out, head_rows) if aligned else ()
+    w_mix, rows_all, *got = first_exchange(
+        split_columns((w_qkv, w_gate, beside_cols), mix_cuts), tokens[0], over_dp
+    )
+    if aligned:
+        w_o, head_rows = got
+    else:
+        w_o, head_rows = (own_rows(lax.all_gather(a, both, axis=0, tiled=True)) for a in (w_out, head_rows))
+    w_extra = w_mix[:, 4 * mine :]
+    gain_one, gain_two = w_extra[:, heads].astype(floats), w_extra[:, heads + 1].astype(floats)
+    pack_tags = w_extra.reshape(packs, per_seq, rows, extra)[:, :, 0, heads + 2 : heads + 2 + spans]
+    pack_tags = lax.dynamic_index_in_dim(pack_tags.reshape(packs, blocks), lax.axis_index("dp"), 0, keepdims=False)
     fresh = jnp.concatenate([jnp.ones((1,), jnp.int32), (pack_tags[1:] != pack_tags[:-1]).astype(jnp.int32)])
-    gain_one, gain_two = vec_all[:, 0].astype(floats), vec_all[:, 1].astype(floats)
-    vec_own = own_rows(vec_all).astype(floats)
-    post_gain, post_shift = vec_own[:, 5], vec_own[:, 6]
-    lr_cols = lr_all.reshape(width, outer, per_seq, heads // outer)
-    lr_own = lax.dynamic_index_in_dim(lr_cols, place, 2, keepdims=False).reshape(width, heads)
+    vec_own = head_rows[:, HD : HD + 5].astype(floats)
+    post_gain, post_shift = vec_own[:, 3], vec_own[:, 4]
     bias_own = lax.dynamic_index_in_dim(lr_bias.reshape(outer, per_seq, heads // outer), place, 1, keepdims=False)
     bias_own = bias_own.reshape(heads).astype(floats)
 
-    if not aligned:
-        w_o = own_rows(lax.all_gather(w_out, both, axis=0, tiled=True))
     later_top, rows_all = lax.optimization_barrier((grad_out[0], rows_all))
     d_top = lax.all_gather(later_top, "seq", axis=0, tiled=True)
     gu_mine = split_columns((w_gate_up,), unit_cuts)
@@ -1008,21 +1379,23 @@
     normed_in = inputs * scale_one
     x_one = (normed_in * gain_one).astype(bf16)
     qkv = dot(x_one, w_mix[:, : 3 * mine])
-    gate_pre = dot(x_one, w_mix[:, 3 * mine :])
-    lr_sigm = jax.nn.sigmoid(dot(x_one, lr_own) + bias_own)
+    gate_pre = dot(x_one, w_mix[:, 3 * mine : 4 * mine])
+    lr_sigm = jax.nn.sigmoid(dot(x_one, w_extra)[:, :heads] + bias_own)
     e_rows = (lr_sigm * (1.0 / (HD * MB))).reshape(blocks, MB, heads).transpose(0, 2, 1).reshape(blocks, 1, heads * MB)
 
     def by_token(vector):
         return jnp.repeat(vector.reshape(heads, HD).T, MB, axis=1)
 
-    init_w = own_rows(init_all).astype(floats).reshape(heads, HD, HD)
+    init_w = head_rows[:, :HD].astype(floats).reshape(heads, HD, HD)
     init_w = (init_w - jnp.mean(init_w, -1, keepdims=True)).transpose(2, 0, 1).reshape(HD, heads * HD)
-    init_b = vec_own[:, 2].reshape(heads, HD)
+    init_b = vec_own[:, 0].reshape(heads, HD)
     init_b = (init_b - jnp.mean(init_b, -1, keepdims=True)).reshape(-1)
-    gain_t, shift_t = by_token(vec_own[:, 3]), by_token(vec_own[:, 4])
-    *results, gu_part = inner_forward(
-        10, fresh, qkv, e_rows, init_w, by_token(init_b), gain_t, shift_t, (gu_mine,)
-    )
+    gain_t, shift_t = by_token(vec_own[:, 1]), by_token(vec_own[:, 2])
+    *results, gu_part, w_d = inner_forward(
+        10, fresh, qkv, e_rows, init_w, by_token(init_b), gain_t, shift_t, (gu_mine,),
+        (jnp.pad(w_down, ((0, filled - units), (0, 0))),),
+    )
+    w_d = w_d.reshape(-1, w_d.shape[-1])
     mixed, *saved = results
 
     mean_own = jnp.mean(mixed, -1)
@@ -1041,31 +1414,22 @@
     residual = inputs + branch
     scale_two = lax.rsqrt(jnp.mean(residual * residual, -1, keepdims=True) + EPSILON)
     normed_mid = residual * scale_two
-    x_two, w_d = gather_with("gather_mid", 4, (normed_mid * gain_two).astype(bf16), (w_down,))
-    hidden_units = packs * units
-    gate_up = dot(x_two, w_gu)
-    gate_part, up_part = gate_up[:, :hidden_units], gate_up[:, hidden_units:]
-    silu_sig = jax.nn.sigmoid(gate_part)
-    silu_val = gate_part * silu_sig
-    hidden = (silu_val * up_part).astype(bf16)
-    down = lax.psum_scatter(dot(hidden, w_d).astype(bf16), "seq", scatter_dimension=0, tiled=True)
-
-    g_down = cross_rows(hidden, d_top).astype(bf16)
-    d_hidden = cross_cols(d_top, w_d)
-    d_gate = d_hidden * up_part * silu_sig * (1.0 + gate_part * (1.0 - silu_sig))
-    d_up = d_hidden * silu_val
-    d_gate_up = jnp.concatenate([d_gate, d_up], axis=1).astype(bf16)
-    g_gate_up = cross_rows(x_two, d_gate_up).astype(bf16)
-    mid_terms, down = lax.optimization_barrier((cross_cols(d_gate_up, w_gu).astype(bf16), down))
-    d_xtwo, g_gate_up = scatter_with("scatter_mid", 5, mid_terms, (g_gate_up,))
-    g_gate_up = add_packs(g_gate_up).astype(bf16)
-    result = residual + down.astype(floats)
+    x_two, hidden, d_gate_up, down, d_xtwo = feed_forward(5, (normed_mid * gain_two).astype(bf16), d_top, w_gu, w_d)
+    pack_rows = lambda array: array.reshape((packs, -1) + array.shape[1:])
+    g_gate_up = pack_rows(cross_rows(x_two, d_gate_up).astype(bf16))
+    g_down = pack_rows(cross_rows(hidden, d_top).astype(bf16))
     g_two = jnp.sum(d_xtwo * normed_mid, axis=0)
     d_mid = d_xtwo * gain_two
     d_residual = grad_out[0].astype(floats) + scale_two * (
         d_mid - normed_mid * jnp.mean(d_mid * normed_mid, -1, keepdims=True)
     )
-    (d_branch,) = gather_with("gather_branch", 6, d_residual.astype(bf16), ())
+    d_branch, g_gate_up = gather_with(
+        "gather_branch", 6, d_residual.astype(bf16), (), [(g_gate_up, None, None)]
+    )
+    g_gate_up = add_packs(g_gate_up).astype(bf16)
+    down, d_branch = lax.optimization_barrier((down, d_branch))
+    down = lax.psum_scatter(down, "seq", scatter_dimension=0, tiled=True)
+    result = residual + down.astype(floats)
     g_out = cross_rows(gated_unit, d_branch).astype(bf16)
     d_unit = cross_cols(d_branch, w_o)
     d_normed = d_unit * gelu_gate
@@ -1077,23 +1441,29 @@
     d_mixed = out_scale * (d_hat - sums[0][:, None] - out_hat * sums[1][:, None])
     d_gate_pre = gelu_pull(d_unit * normed_out)[0].astype(bf16)
     place_rows = lambda array: array.reshape((per_seq, -1) + array.shape[1:])
-    pack_rows = lambda array: array.reshape((packs, -1) + array.shape[1:])
-    d_qkv, d_rate, d_w0, d_c0, d_gain, d_shift, g_gate_up, g_down, *g_outs = inner_backward(
+    g_gate = pack_rows(cross_rows(x_one, d_gate_pre).astype(bf16))
+    d_qkv, d_rate, d_w0, d_c0, d_gain, d_shift, g_gate_up, g_down, g_gate, *g_outs = inner_backward(
         11, fresh, qkv, e_rows, d_mixed, saved, gain_t, shift_t, (place_rows(g_gate_up),),
-        (pack_rows(g_down), pack_rows(g_out)) if aligned else (pack_rows(g_down),),
+        [(g_down, None, None), (g_gate, None, None)] + [(pack_rows(g_out), None, None)] * aligned,
     )
     (g_gate_up,) = join_columns(g_gate_up, (w_gate_up.shape[1],), unit_cuts)
-    g_down = add_packs(g_down)
+    g_down = add_packs(g_down)[:units]
     if aligned:
         g_out = add_packs(g_outs[0])
     else:
         g_out = lax.psum_scatter(put_rows(g_out), both, scatter_dimension=0, tiled=True).astype(floats)
     d_rate = d_rate.reshape(blocks, heads, MB).transpose(0, 2, 1).reshape(length, heads)
     d_logit = (d_rate * (1.0 / HD) * lr_sigm * (1.0 - lr_sigm)).astype(bf16)
-    d_mix = jnp.concatenate([d_qkv, d_gate_pre], axis=1)
-    g_mix = cross_rows(x_one, d_mix).astype(bf16)
-    d_xone = cross_cols(d_mix, w_mix) + cross_cols(d_logit, lr_own)
-    g_one = jnp.sum(d_xone * normed_in, axis=0)
+    g_qkv = cross_rows(x_one, d_qkv).astype(bf16)
+    d_logit_wide = jnp.pad(d_logit, ((0, 0), (0, extra - heads)))
+    d_xone = cross_cols(jnp.concatenate([d_qkv, d_gate_pre, d_logit_wide], axis=1), w_mix)
+    g_one = jnp.sum(d_xone * (lax.optimization_barrier(rows_all).astype(floats) * scale_one), axis=0)
+
+    lane = jnp.arange(extra)[None, :]
+    g_bias = jnp.pad(jnp.sum(d_logit.astype(floats), axis=0), (heads + 2, extra - 2 * heads - 2))
+    g_beside = cross_rows(x_one, d_logit_wide) + jnp.where(lane == heads, g_one[:, None], 0.0)
+    g_beside = (g_beside + jnp.where(lane == heads + 1, g_two[:, None], 0.0) + g_bias[None, :]).astype(bf16)
+
     def from_token(array):
         return jnp.sum(array.reshape(HD, heads, MB), -1).T.reshape(mine)
 
@@ -1101,49 +1471,50 @@
         [d_c0.reshape(HD, heads, MB)[:, :, 0].T.reshape(mine), from_token(d_gain), from_token(d_shift), g_post_w, g_post_b],
         axis=1,
     )
-    g_vec = jnp.concatenate([jnp.stack([g_one, g_two], axis=1), put_rows(g_vec)], axis=1)
-    g_init = put_rows(d_w0.reshape(HD, heads, HD).transpose(1, 2, 0).reshape(mine, HD))
-    g_lr = cross_rows(x_one, d_logit).reshape(width, outer, 1, heads // outer)
-    g_lr = lax.dynamic_update_slice(
-        jnp.zeros((width, outer, per_seq, heads // outer), floats), g_lr, (0, 0, place, 0)
-    ).reshape(width, heads_all)
-    g_bias = jnp.sum(d_logit.astype(floats), axis=0).reshape(outer, 1, heads // outer)
-    g_bias = lax.dynamic_update_slice(
-        jnp.zeros((outer, per_seq, heads // outer), floats), g_bias, (0, place, 0)
-    ).reshape(heads_all)
-    wide = HD + heads_all + 7
-    g_small = jnp.concatenate([g_init, g_lr, g_vec], axis=1).reshape(devices, rows, wide)
-    g_last = jnp.broadcast_to(jnp.pad(g_bias, (0, wide - heads_all)), (devices, 8, wide))
-    g_small = jnp.concatenate([g_small, g_last], axis=1)
-    d_xone, g_mix, g_small = scatter_with("scatter_first", 8, d_xone.astype(bf16), (g_mix, g_small))
-    g_mix, g_small = swap_places(
-        "return_columns", 9, (place_rows(add_packs(g_mix).astype(bf16)), place_rows(add_packs(g_small)))
-    )
+    g_heads = jnp.concatenate(
+        [d_w0.reshape(HD, heads, HD).transpose(1, 2, 0).reshape(mine, HD), g_vec, jnp.zeros((mine, extra - HD - 5), floats)],
+        axis=1,
+    )
+    swaps = [(pack_rows(g_beside), None, None), (pack_rows(g_qkv), None, None)]
+    d_xone, *got = scatter_with(
+        "scatter_first", 8, d_xone.astype(bf16), [(pack_rows(g_heads), None, None)] * aligned + swaps
+    )
+    if aligned:
+        g_heads = add_packs(got[0])
+    else:
+        g_heads = lax.psum_scatter(put_rows(g_heads), both, scatter_dimension=0, tiled=True)
+    g_mix = jnp.concatenate([add_packs(got[-1]), add_packs(g_gate), add_packs(got[-2])], axis=1).astype(bf16)
+    (g_mix,) = swap_places("return_columns", 9, (place_rows(g_mix),))
     g_qkv, g_gate = join_columns(g_mix, (w_qkv.shape[1], w_gate.shape[1]), feature_cuts)
-    g_small = jnp.sum(g_small, 0).reshape(-1, wide)
+    g_beside = g_mix[:, :, 4 * mine :].astype(floats)
+    g_norms = jnp.sum(g_beside[:, :, heads : heads + 2], 0)
+
+    def by_head(part):
+        part = part.reshape(part.shape[:-1] + (outer, heads // outer))
+        return jnp.moveaxis(part, 0, -2).reshape(part.shape[1:-2] + (heads_all,))
+
     scale_one = lax.rsqrt(jnp.mean(inputs * inputs, -1, keepdims=True) + EPSILON)
     normed_in = inputs * scale_one
     d_inner = d_xone * gain_one
     d_tokens = d_residual + scale_one * (
         d_inner - normed_in * jnp.mean(d_inner * normed_in, -1, keepdims=True)
     )
-    g_vec = g_small[:rows, HD + heads_all :]
     return (
         result.astype(bf16)[None],
         d_tokens.astype(bf16)[None],
-        g_vec[:, 0],
+        g_norms[:, 0],
         g_qkv,
-        g_small[:rows, HD : HD + heads_all],
-        g_small[rows, :heads_all],
+        by_head(g_beside[:, :, :heads]),
+        by_head(g_beside[:, 0, heads + 2 : 2 * heads + 2]),
         g_gate,
         g_out,
-        g_small[:rows, :HD],
-        g_vec[:, 2],
-        g_vec[:, 3],
-        g_vec[:, 4],
-        g_vec[:, 5],
-        g_vec[:, 6],
-        g_vec[:, 1],
+        g_heads[:, :HD],
+        g_heads[:, HD],
+        g_heads[:, HD + 1],
+        g_heads[:, HD + 2],
+        g_heads[:, HD + 3],
+        g_heads[:, HD + 4],
+        g_norms[:, 1],
         g_gate_up,
         g_down,
     )

time: 760 us -> 691 us (0.909)
  matrix products: 102 us -> 63.6 us
  local copies, waits for them, and re-layouts: 63.9 us -> 32.6 us
  Pallas kernels: 525 us -> 538 us
  waiting for transfers between devices: 12.1 us -> 0.04 us
    pallas_call x1 -> x2, Pallas kernels: 46.6 us -> 154 us  [the longest x1 101 us: feed_forward(): pl.pallas_call(functools.partial(feed_forward_kernel, cut), out_shape=out...]
    pallas_call x9 -> x7, Pallas kernels: 419 us -> 313 us  [talk(): pl.pallas_call(kernel, out_shape=outs, in_specs=[where(i, in_vmem) for i...]
    dot_general x5 -> x2, matrix products: 35.1 us -> 16.5 us  [cross_cols(): lax.dot_general(left_side, right_side, (((1,), (1,)), ((), ())), preferre...]
    dot_general x6 -> x4, matrix products: 35.9 us -> 20.3 us  [dot(): return jnp.dot(left_side, right_side, preferred_element_type=jnp.float32)]
    reduce_scatter x1, waiting for transfers between devices: 12 us -> 0.01 us  [on_device(): down = lax.psum_scatter(down, 'seq', scatter_dimension=0, tiled=True)]
    unnamed x136 -> x88, local copies, waits for them, and re-layouts: 26.6 us -> 15.3 us
    pallas_call x1, Pallas kernels: 53.5 us -> 64.7 us  [inner_backward(): pl.pallas_call(functools.partial(backward_kernel, heads, per, len(seq_arr...]
    convert_element_type x2 -> x0, local copies, waits for them, and re-layouts: 8.69 us -> none  [the longest x1 8.62 us: on_device(): g_gate_up = cross_rows(x_two, d_gate_up).astype(bf16)]
  transfers between devices with their start and end apart: 2 -> 2, of which waited for: 1 -> 0; matrix products, arithmetic and copies ran while one was open for 11% -> 13% of each run, Pallas kernels for 7% -> 33%
where the time goes in v4:
time: 691 us; the launch traced here: 685 us
  Pallas kernels  538 us (78%)
  matrix products  63.6 us (9%)
  other arithmetic  34.5 us (5%)
  local copies, waits for them, and re-layouts  32.6 us (5%)
  between operations  15.3 us (2%)
    pallas_call x7, Pallas kernels, talk(): pl.pallas_call(kernel, out_shape=outs, in_specs=[where(i, in_vmem) for i...  313 us
    pallas_call x1, Pallas kernels, feed_forward(): pl.pallas_call(functools.partial(feed_forward_kernel, cut), out_shape=out...  101 us
    pallas_call x1, Pallas kernels, inner_backward(): pl.pallas_call(functools.partial(backward_kernel, heads, per, len(seq_arr...  64.7 us
    pallas_call x1, Pallas kernels, inner_forward(): pl.pallas_call(functools.partial(forward_kernel, heads, per, len(seq_arra...  52.7 us
    dot_general x6, matrix products, cross_rows(): lax.dot_general(left_side, right_side, (((0,), (0,)), ((), ())), preferre...  26.8 us
    dot_general x4, matrix products, dot(): return jnp.dot(left_side, right_side, preferred_element_type=jnp.float32)  20.3 us
    dot_general x2, matrix products, cross_cols(): lax.dot_general(left_side, right_side, (((1,), (1,)), ((), ())), preferre...  16.5 us
    unnamed x88, local copies, waits for them, and re-layouts  15.3 us
  transfers between devices with their start and end apart: 2, of which 0 were waited for; matrix products, arithmetic and copies ran while one was open for 13% of the time, Pallas kernels for 33%

profile of v4, /device:TPU:9, one launch (start us, length us, event | category | flops | bytes accessed | tf_op | source)
XLA Modules:
  0.0 684.5 jit_solution(5177614872034300)
XLA Ops:
  19.5 77.1 %first_exchange.1 = (bf16[4,8,64,1152]{3,2,1,0:T(8,128)(2,1)}, bf16[8,128,2048]{2,1,0:T(8,128)(2,1)}, bf16[4,64,2048]{2,1,0:T(8,128)(2,1)S(1)}, bf16[4,64,128]{2,1,0:T(8,128)(2,1)S(1)}) custom-call(bf16[8,64,1152]{2,1,0:T(8,128)(2,1)S(1)} %split_columns.2.refs_0_, bf16[128,2048]{1,0:T(8,128)(2,1)S(1)} %bitcast.149, bf16[64,2048]{1,0:T(8,128)(2,1)S(1)} %copy-done.15, ...), custom_call_target="tpu_custom_call" | custom-call | tf_op jit(solution)/shard_map/first_exchange/pallas_call | solution.py:701
  98.9 2.6 slice_convert_fusion
  102.2 3.3 fusion
  106.8 3.7 broadcast_multiply_fusion
  112.4 1.8 split_columns.3.refs_0_
  114.1 2.0 pad.12.refs_1_
  116.4 8.3 %fusion.3.qkv_ref = f32[1024,768]{1,0:T(8,128)} fusion(bf16[1024,2048]{1,0:T(8,128)(2,1)} %copy-done.22, bf16[2048,1152]{1,0:T(8,128)(2,1)} %bitcast.181), kind=kOutput, calls=%fused_computation.11 | convolution fusion | flops 3221225472 | bytes 10485760 | tf_op jit(solution)/shard_map/dot_general | solution.py:1267
  124.6 52.7 %inner_forward.1 = (f32[1024,256]{1,0:T(8,128)S(1)}, bf16[64,64,256]{2,1,0:T(8,128)(2,1)}, f32[64,64,64]{2,1,0:T(8,128)}, f32[64,64,64]{2,1,0:T(8,128)}, f32[64,...) custom-call(s32[64]{0:T(128)S(1)} %add_convert_fusion.1.fresh_ref, ...), custom_call_target="tpu_custom_call" | custom-call | tf_op jit(solution)/shard_map/inner_forward/pallas_call | solution.py:137
  179.0 4.7 share_moments.1
  185.4 5.1 multiply_convert_fusion.1
  191.3 3.3 convolution_convert_fusion
  194.6 70.2 %scatter_branch.1 = (f32[128,2048]{1,0:T(8,128)S(1)}, bf16[4,512,1408]{2,1,0:T(8,128)(2,1)}) custom-call(bf16[8,128,2048]{2,1,0:T(8,128)(2,1)} %bitcast.162, bf16[512,1408]{1,0:T(8,128)(2,1)S(1)} %bitcast.150), custom_call_target="tpu_custom_call" | custom-call | tf_op jit(solution)/shard_map/scatter_branch/pallas_call | solution.py:701
  266.8 101.4 %feed_forward.1 = (bf16[8,128,2048]{2,1,0:T(8,128)(2,1)}, bf16[8,128,704]{2,1,0:T(8,128)(2,1)}, bf16[8,128,1408]{2,1,0:T(8,128)(2,1)}, bf16[8,128,2048]{2,1,0:T(8,128)(2,1)}, f32[128,2048]{1,0:T(8,128)}) custom-call(bf16[128,2048]{1,0:T(8,128)(2,1)} %multiply_convert_fusion.block_ref, bf16[8,128,2048]{2,1,0:T(8,128)(2,1)} %bitcast.228, ...), custom_call_target="tpu_custom_call" | custom-call | flops 17716740096 | bytes 20971520 | tf_op jit(solution)/shard_map/feed_forward/pallas_call | solution.py:1231
  371.5 10.5 %bitcast_convert_fusion = bf16[2048,1408]{1,0:T(8,128)(2,1)} fusion(bf16[8,128,2048]{2,1,0:T(8,128)(2,1)S(1)} %copy-done.41, bf16[8,128,1408]{2,1,0:T(8,128)(2,1)} %get-tuple-element.77), kind=kOutput, calls=%fused_computation | convolution fusion | flops 5908463616 | bytes 12845056 | tf_op jit(solution)/shard_map/dot_general | solution.py:1259
  382.0 66.0 %gather_branch.1 = (bf16[8,128,2048]{2,1,0:T(8,128)(2,1)S(1)}, bf16[4,512,1408]{2,1,0:T(8,128)(2,1)}) custom-call(bf16[128,2048]{1,0:T(8,128)(2,1)S(1)} %fusion.46.refs_0_, bf16[4,512,1408]{2,1,0:T(8,128)(2,1)} %bitcast.166), custom_call_target="tpu_custom_call" | custom-call | tf_op jit(solution)/shard_map/gather_branch/pallas_call | solution.py:701
  448.0 2.0 copy-done.16
  450.0 5.9 multiply_reduce_fusion.2
  455.9 9.7 %share_sums.1 = f32[8,2,1024]{2,1,0:T(2,128)S(1)} custom-call(f32[2,1024]{1,0:T(2,128)S(1)} %pad_maximum_fusion.2.refs_0_), custom_call_target="tpu_custom_call" | custom-call | tf_op jit(solution)/shard_map/share_sums/pallas_call | solution.py:701
  465.7 5.1 reduce_sum.287
  470.8 1.9 subtract_multiply_fusion.dmix_ref
  472.7 3.7 convolution_convert_fusion.3
  479.2 4.5 convolution_convert_fusion.2
  483.7 64.7 %inner_backward.1 = (bf16[1024,768]{1,0:T(8,128)(2,1)}, f32[64,1,64]{2,1,0:T(1,128)S(1)}, f32[64,256]{1,0:T(8,128)S(1)}, f32[64,64]{1,0:T(8,128)S(1)}, f32[64,64...) custom-call(s32[64]{0:T(128)S(1)} %add_convert_fusion.1.fresh_ref, ...), custom_call_target="tpu_custom_call" | custom-call | tf_op jit(solution)/shard_map/inner_backward/pallas_call | solution.py:264
  551.7 10.6 %multiply_reduce_fusion = (f32[2048]{0:T(1024)S(1)}, bf16[1024,2048]{1,0:T(8,128)(2,1)}) fusion(bf16[1024,2048]{1,0:T(8,128)(2,1)} %bitcast.164, f32[1024]{0:T(1024)S(1)} %add_rsqrt_fusion.1, bf16[2048,1152]{1,0:T(8,128)(2,1)} %bitcast.183, bf16[1024,128]{1,0:T(8,128)(2,1)S(1)} %pad.13, bf16[1024,256]{1,0:T(8,128)(2,1)} %get-tuple-element.132, ...), kind=kOutput, calls=%fused_computation.6 | convolution fusion | flops 4849399808 | bytes 15478784 | tf_op jit(solution)/shard_map/dot_general | solution.py:1263
  562.3 1.8 fusion.7
  564.1 4.9 convolution_convert_fusion.1
  569.1 55.0 %scatter_first.1 = (f32[128,2048]{1,0:T(8,128)S(1)}, f32[4,64,128]{2,1,0:T(8,128)S(1)}, bf16[4,512,128]{2,1,0:T(8,128)(2,1)S(1)}, bf16[4,512,768]{2,1,0:T(8,128)(2,1)S(1)}) custom-call(bf16[8,128,2048]{2,1,0:T(8,128)(2,1)} %bitcast.170, f32[4,64,128]{2,1,0:T(8,128)S(1)} %concatenate.49.refs_1_, bf16[4,512,128]{2,1,0:T(8,128)(2,1)S(1)} %bitcast.159, ...), custom_call_target="tpu_custom_call" | custom-call | tf_op jit(solution)/shard_map/scatter_first/pallas_call | solution.py:701
  626.1 3.4 reduce.4
  630.9 30.0 %return_columns.1.source = bf16[8,64,1152]{2,1,0:T(8,128)(2,1)S(1)} custom-call(bf16[8,64,1152]{2,1,0:T(8,128)(2,1)S(1)} %pad_maximum_fusion.refs_0_), custom_call_target="tpu_custom_call" | custom-call | tf_op jit(solution)/shard_map/return_columns/pallas_call | solution.py:701
  660.9 2.1 join_columns.2
  666.3 2.5 join_columns.3
  674.4 2.8 fusion.36
  (205 shorter events, 46.0 us)
Async XLA Ops:
  7.2 90.5 %copy-start.38 = (bf16[32]{0:T(256)(128)(2,1)S(1)}, bf16[32]{0:T(256)(128)(2,1)}, u32[]{:S(2)}) copy-start(bf16[32]{0:T(256)(128)(2,1)} %param.23) | copy-start | bytes 196
  7.2 187.4 %all-gather.2.cloned.1.call-start = ((), (), s32[]{:S(2)}) async-start(), calls=%async_computation.1 | async-start | bytes 4718592 | tf_op jit(solution)/shard_map/all_gather | solution.py:1374
  97.7 576.7 %reduce-scatter.2.cloned.1.call-start = ((), (), s32[]{:S(2)}) async-start(), calls=%async_computation.2 | async-start | bytes 4718592 | tf_op jit(solution)/shard_map/reduce_scatter | solution.py:1431
  102.1 3.7 copy-start.19
  106.8 3.7 copy-start.22
  106.8 5.5 copy-start.7
  116.4 8.3 %copy-start.3 = (bf16[176,2048]{1,0:T(8,128)(2,1)S(1)}, bf16[176,2048]{1,0:T(8,128)(2,1)}, u32[]{:S(2)}) copy-start(bf16[176,2048]{1,0:T(8,128)(2,1)} %pad.12.refs_1_) | copy-start | bytes 2162692
  185.4 5.9 copy-start.11
  190.5 4.1 copy-start.6
  194.6 70.2 %copy-start.1 = (bf16[1,128,2048]{2,1,0:T(8,128)(2,1)S(1)}, bf16[1,128,2048]{2,1,0:T(8,128)(2,1)}, u32[]{:S(2)}) copy-start(bf16[1,128,2048]{2,1,0:T(8,128)(2,1)} %param.18) | copy-start | bytes 1572868
  265.6 104.3 %copy-start.17 = (f32[128,2048]{1,0:T(8,128)}, f32[128,2048]{1,0:T(8,128)S(1)}, u32[]{:S(2)}) copy-start(f32[128,2048]{1,0:T(8,128)S(1)} %get-tuple-element.127) | copy-start | bytes 3145732
  265.6 104.3 %copy-start.31 = (f32[128]{0:T(128)}, f32[128]{0:T(128)S(1)}, u32[]{:S(2)}) copy-start(f32[128]{0:T(128)S(1)} %add_rsqrt_fusion.3) | copy-start | bytes 1540
  266.8 103.1 %copy-start.20 = (bf16[1,128,2048]{2,1,0:T(8,128)(2,1)S(1)}, bf16[1,128,2048]{2,1,0:T(8,128)(2,1)}, u32[]{:S(2)}) copy-start(bf16[1,128,2048]{2,1,0:T(8,128)(2,1)} %param.35) | copy-start | bytes 1572868
  368.2 3.3 copy-start.41
  369.9 12.0 %copy-start.33 = (f32[128]{0:T(128)}, f32[128]{0:T(128)S(1)}, u32[]{:S(2)}) copy-start(f32[128]{0:T(128)S(1)} %broadcast_multiply_fusion.7) | copy-start | bytes 1540
  382.0 68.1 %copy-start.12 = (bf16[4,64,2048]{2,1,0:T(8,128)(2,1)S(1)}, bf16[4,64,2048]{2,1,0:T(8,128)(2,1)}, u32[]{:S(2)}) copy-start(bf16[4,64,2048]{2,1,0:T(8,128)(2,1)} %copy-done.10) | copy-start | bytes 3145732
  465.7 7.0 %copy-start.29 = (bf16[1024,256]{1,0:T(8,128)(2,1)S(1)}, bf16[1024,256]{1,0:T(8,128)(2,1)}, u32[]{:S(2)}) copy-start(bf16[1024,256]{1,0:T(8,128)(2,1)} %copy-done.28) | copy-start | bytes 1572868
  472.7 3.7 copy-start.23
  472.7 3.7 copy-start.40
  476.4 2.7 copy-start.39
  483.7 66.2 %copy-start.30 = (f32[1024,4]{1,0:T(8,128)S(1)}, f32[1024,4]{1,0:T(8,128)}, u32[]{:S(2)}) copy-start(f32[1024,4]{1,0:T(8,128)} %get-tuple-element.142) | copy-start | bytes 49156
  551.6 10.6 %copy-start.24 = (bf16[1024,2048]{1,0:T(8,128)(2,1)S(1)}, bf16[1024,2048]{1,0:T(8,128)(2,1)}, u32[]{:S(2)}) copy-start(bf16[1024,2048]{1,0:T(8,128)(2,1)} %copy-done.22) | copy-start | bytes 12582916
  629.5 36.7 %copy-start.4 = (bf16[8,64,1408]{2,1,0:T(8,128)(2,1)S(1)}, bf16[8,64,1408]{2,1,0:T(8,128)(2,1)}, u32[]{:S(2)}) copy-start(bf16[8,64,1408]{2,1,0:T(8,128)(2,1)} %get-tuple-element.103.source) | copy-start | bytes 4325380
  660.9 11.5 %copy-start.35 = (f32[128]{0:T(128)S(1)}, f32[128]{0:T(128)}, u32[]{:S(2)}) copy-start(f32[128]{0:T(128)} %get-tuple-element.135) | copy-start | bytes 1540
  663.0 3.2 copy-start.26
  666.2 8.2 %copy-start.27 = (f32[64,128]{1,0:T(8,128)}, f32[64,128]{1,0:T(8,128)S(1)}, u32[]{:S(2)}) copy-start(f32[64,128]{1,0:T(8,128)S(1)} %reduce_sum.301) | copy-start | bytes 98308
  666.2 5.2 copy-start.9
  666.2 6.5 copy-start.25
  668.8 5.6 copy-start.18
  668.8 5.6 copy-start.21
  668.8 5.6 copy-start.32
  668.8 5.7 copy-start.34
  (12 other events, 15.7 us)
Sparse Core Ops, SparseCore 0:
  97.8 55.8 all-gather.1
  450.1 80.5 reduce-scatter.1

commit v5 on v4

--- a/solution.py
+++ b/solution.py
@@ -70,10 +70,10 @@
     moved = over_seq + over_dp
     sources, refs = refs[:moved], refs[moved:]
     mixed_ref, wsave_ref, hat_ref, slope_ref, gap_ref, bar_ref, rows_ref = refs[:7]
-    results, (w_ref, c_ref, send_sems, recv_sems) = refs[7 : 7 + moved], refs[7 + moved :]
+    results, (w_ref, c_ref, send_sems, recv_sems, *rooms) = refs[7 : 7 + moved], refs[7 + moved :]
     jobs = [swap_seq] * over_seq + [spread_dp] * over_dp
     beside(
-        ("seq", "dp"), send_sems, recv_sems,
+        ("seq", "dp"), send_sems, recv_sems, rooms,
         lambda wires: [job(wires, a, b) for job, a, b in zip(jobs, sources, results)],
     )
     hi = heads * HD
@@ -156,7 +156,8 @@
         + [shape_of(a.shape, a.dtype) for a in seq_arrays]
         + [shape_of((packs,) + a.shape, a.dtype) for a in dp_arrays],
         scratch_shapes=[pltpu.VMEM((HD, hi), f32), pltpu.VMEM((HD, ht), f32)]
-        + wire_sems(len(seq_arrays) * lax.axis_size("seq") + len(dp_arrays) * packs),
+        + wire_sems(len(seq_arrays) * lax.axis_size("seq") + len(dp_arrays) * packs)
+        + [room(a.shape[1:], a.dtype) for a in seq_arrays] + [room(a.shape, a.dtype) for a in dp_arrays],
         compiler_params=pltpu.CompilerParams(
             vmem_limit_bytes=48 * 1024 * 1024, collective_id=cid, has_side_effects=True
         ),
@@ -170,10 +171,10 @@
     sources, refs = refs[:moved], refs[moved:]
     sources = list(sources[:over_seq]) + [window(ref, item) for ref, item in zip(sources[over_seq:], items)]
     dqkv_ref, drate_ref, dw0_ref, dc0_ref, dgain_ref, dshift_ref = refs[:6]
-    results, (a_ref, ac_ref, send_sems, recv_sems) = refs[6 : 6 + moved], refs[6 + moved :]
+    results, (a_ref, ac_ref, send_sems, recv_sems, *rooms) = refs[6 : 6 + moved], refs[6 + moved :]
     swaps = [swap_seq] * over_seq + [swap_dp] * len(items)
     beside(
-        ("seq", "dp"), send_sems, recv_sems,
+        ("seq", "dp"), send_sems, recv_sems, rooms,
         lambda wires: [swap(wires, a, b) for swap, a, b in zip(swaps, sources, results)],
     )
     hi, ht = heads * HD, heads * MB
@@ -281,7 +282,9 @@
         ] + [jax.ShapeDtypeStruct((HD, ht), f32)] * 3 + [shape_of(a.shape, a.dtype) for a in seq_arrays]
         + [window_shape(item) for item in items],
         scratch_shapes=[pltpu.VMEM((HD, hi), f32), pltpu.VMEM((HD, ht), f32)]
-        + wire_sems(len(seq_arrays) * lax.axis_size("seq") + len(items) * lax.axis_size("dp")),
+        + wire_sems(len(seq_arrays) * lax.axis_size("seq") + len(items) * lax.axis_size("dp"))
+        + [room(a.shape[1:], a.dtype) for a in seq_arrays]
+        + [room(window_shape(item).shape[1:], item[0].dtype) for item in items],
         compiler_params=pltpu.CompilerParams(
             vmem_limit_bytes=48 * 1024 * 1024, collective_id=cid, has_side_effects=True
         ),
@@ -291,9 +294,24 @@
 MESH = pl.DeviceIdType.MESH
 
 
+class Kept:
+    def __init__(self, source, target, room, sem):
+        self.bring = pltpu.make_async_copy(source, room, sem)
+        self.leave = pltpu.make_async_copy(room, target, sem)
+
+    def start(self):
+        self.bring.start()
+        self.bring.wait()
+        self.leave.start()
+
+    def wait(self):
+        self.leave.wait()
+
+
 class Wires:
-    def __init__(self, send_sems, recv_sems, started=False):
+    def __init__(self, send_sems, recv_sems, rooms=(), started=False):
         self.send_sems, self.recv_sems, self.used, self.started = send_sems, recv_sems, 0, started
+        self.rooms = list(rooms)
 
     def begin(self, copy):
         if not self.started:
@@ -318,9 +336,11 @@
             device_id_type=MESH,
         )
 
+    def load(self, source, target):
+        return pltpu.make_async_copy(source, target, self.send_sems.at[self.number()])
+
     def keep(self, source, target):
-        at = self.number()
-        return pltpu.make_async_copy(source, target, self.send_sems.at[at])
+        return Kept(source, target, self.rooms.pop(0), self.send_sems.at[self.number()])
 
 
 def on_line(step):
@@ -383,7 +403,6 @@
         return out.at[slot, pl.ds(part * step, step)]
 
     own = wires.keep(source, out.at[me])
-    own.start()
     numbers = {(way, i, part): wires.number() for way in "rlRL" for i in range(chips) for part in range(cut)}
 
     def copy(way, i, part):
@@ -412,6 +431,7 @@
 
     for part in range(cut):
         copy("R", 0, part).start()
+    own.start()
     for i in range(1, chips):
         for part in range(cut):
             yield True
@@ -476,7 +496,7 @@
     lax.fori_loop(0, out.shape[0] // rows, body, 0)
 
 
-def scatter_line(wires, source, out, near, from_left, from_right, to_right, to_left, cut):
+def scatter_line(wires, produce, source, out, near, from_left, from_right, outbox, cut):
     me, count = lax.axis_index("seq"), lax.axis_size("seq")
     chips, chip, core = count // 2, me // 2, lax.rem(me, 2)
     step = source.shape[1] // cut
@@ -494,35 +514,44 @@
             across[dest, part] = wires.copy(
                 source.at[2 * dest + 1 - core, lines(part)], near.at[dest, lines(part)], sibling()
             )
-            across[dest, part].start()
+
+    def begin(dests):
+        for dest in dests:
+            produce(dest)
+            for part in range(cut):
+                across[dest, part].start()
+
     right, left = {}, {}
     for dest in range(chips):
         for part in range(cut):
-            right[dest, part] = wires.copy(to_right.at[dest, lines(part)], from_left.at[dest, lines(part)], on_line(2))
-            left[dest, part] = wires.copy(to_left.at[dest, lines(part)], from_right.at[dest, lines(part)], on_line(-2))
+            right[dest, part] = wires.copy(outbox.at[dest, lines(part)], from_left.at[dest, lines(part)], on_line(2))
+            left[dest, part] = wires.copy(outbox.at[dest, lines(part)], from_right.at[dest, lines(part)], on_line(-2))
+    def handle(part, ahead, turn, dest, table, inbox, first):
+        terms = [source.at[2 * dest + core, lines(part)], near.at[dest, lines(part)]]
+
+        @pl.when(ahead & turn)
+        def _():
+            across[dest, part].wait_recv()
+
+            @pl.when(first)
+            def _():
+                add_into(outbox.at[dest, lines(part)], terms)
+
+            @pl.when(jnp.logical_not(first))
+            def _():
+                table[dest, part].wait_recv()
+                add_into(outbox.at[dest, lines(part)], terms + [inbox.at[dest, lines(part)]])
+
+            table[dest, part].start()
+
     for i in range(chips - 1):
+        begin(order[2 * i : 2 * i + 2])
         for part in range(cut):
             yield True
-            for dest, table, inbox, outbox, ahead, first in (
-                (chips - 1 - i, right, from_left, to_right, chip < chips - 1 - i, chip == 0),
-                (i, left, from_right, to_left, chip > i, chip == chips - 1),
-            ):
-                terms = [source.at[2 * dest + core, lines(part)], near.at[dest, lines(part)]]
-
-                @pl.when(ahead)
-                def _():
-                    across[dest, part].wait_recv()
-
-                    @pl.when(first)
-                    def _():
-                        add_into(outbox.at[dest, lines(part)], terms)
-
-                    @pl.when(jnp.logical_not(first))
-                    def _():
-                        table[dest, part].wait_recv()
-                        add_into(outbox.at[dest, lines(part)], terms + [inbox.at[dest, lines(part)]])
-
-                    table[dest, part].start()
+            rightward, leftward = (chips - 1 - i, right, from_left, chip == 0), (i, left, from_right, chip == chips - 1)
+            handle(part, chip < chips - 1 - i, chip < chips // 2, *rightward)
+            handle(part, chip > i, True, *leftward)
+            handle(part, chip < chips - 1 - i, chip >= chips // 2, *rightward)
 
     for part in range(cut):
         yield True
@@ -556,12 +585,12 @@
 def swap_seq(wires, source, out):
     me, count = lax.axis_index("seq"), lax.axis_size("seq")
     own = wires.keep(source.at[me], out.at[me])
-    wires.begin(own)
     sent = []
     for step in range(1, count):
         peer = lax.rem(me + step, count)
         sent.append(wires.copy(source.at[peer], out.at[me], seq_peer(step)))
         wires.begin(sent[-1])
+    wires.begin(own)
     yield True
     own.wait()
     for copy in sent:
@@ -571,11 +600,11 @@
 def spread_seq(wires, source, out):
     me, count = lax.axis_index("seq"), lax.axis_size("seq")
     own = wires.keep(source, out.at[me])
-    wires.begin(own)
     sent = []
     for step in range(1, count):
         sent.append(wires.copy(source, out.at[me], seq_peer(step)))
         wires.begin(sent[-1])
+    wires.begin(own)
     yield True
     own.wait()
     for copy in sent:
@@ -585,11 +614,11 @@
 def swap_dp(wires, source, out):
     me, count = lax.axis_index("dp"), lax.axis_size("dp")
     own = wires.keep(source.at[me], out.at[me])
-    wires.begin(own)
     sent = []
     for step in range(1, count):
         sent.append(wires.copy(source.at[lax.rem(me + step, count)], out.at[me], pack_peer(step)))
         wires.begin(sent[-1])
+    wires.begin(own)
     yield True
     own.wait()
     for copy in sent:
@@ -600,13 +629,12 @@
 HALVES = 8 + 4 * PIECES
 
 
-def halves_dp(wires, source, out):
+def halves_dp(wires, source, out, idle=1):
     me, count = lax.axis_index("dp"), lax.axis_size("dp")
     rows, width = source.shape
     by_rows = rows % (16 * PIECES) == 0
     step = (rows if by_rows else width) // PIECES
     own = wires.keep(source, out.at[me])
-    own.start()
     bit = lax.rem(me, 2)
     flip = {1: me + 1 - 2 * bit, 2: lax.rem(me + 2, 4)}
     part = lambda ref, i: ref.at[pl.ds(i * step, step)] if by_rows else ref.at[:, pl.ds(i * step, step)]
@@ -620,6 +648,9 @@
     for i in range(half):
         send(1, i)
         send(2, half + i)
+    own.start()
+    for _ in range(idle):
+        yield True
     for i in range(half):
         for way, j in ((1, i), (2, half + i)):
             yield True
@@ -628,7 +659,7 @@
             then[way, j] = wires.copy(came, came, {"dp": flip[3 - way]})
             then[way, j].start()
             send(3 - way, j)
-    yield True
+    yield PATIENT
     own.wait()
     for i in range(half):
         for way, j in ((2, i), (1, half + i)):
@@ -642,15 +673,18 @@
 def spread_dp(wires, source, out):
     me, count = lax.axis_index("dp"), lax.axis_size("dp")
     own = wires.keep(source, out.at[me])
-    wires.begin(own)
     sent = []
     for step in range(1, count):
         sent.append(wires.copy(source, out.at[me], pack_peer(step)))
         wires.begin(sent[-1])
+    wires.begin(own)
     yield True
     own.wait()
     for copy in sent:
         copy.wait()
+
+
+PATIENT = None
 
 
 def run_all(jobs, patient=()):
@@ -659,23 +693,26 @@
         next(job)
     while jobs:
         for job in list(jobs):
-            if next(job, False) is False:
+            state = next(job, False)
+            if state is not True:
                 jobs.remove(job)
+            if state is PATIENT:
+                patient.append(job)
     for job in patient:
         for _ in job:
             pass
 
 
-def beside(groups, send_sems, recv_sems, plan):
+def beside(groups, send_sems, recv_sems, rooms, plan):
     @pl.when(pl.program_id(0) == 0)
     def _():
         meet(groups)
-        for job in plan(Wires(send_sems, recv_sems)):
+        for job in plan(Wires(send_sems, recv_sems, rooms)):
             next(job)
 
     @pl.when(pl.program_id(0) == pl.num_programs(0) - 1)
     def _():
-        for job in plan(Wires(send_sems, recv_sems, started=True)):
+        for job in plan(Wires(send_sems, recv_sems, rooms, started=True)):
             for _ in job:
                 pass
 
@@ -684,14 +721,19 @@
     return [pltpu.SemaphoreType.DMA((copies,)), pltpu.SemaphoreType.DMA((copies,))]
 
 
-def talk(name, cid, groups, operands, outs, plan, copies, in_vmem=(), out_vmem=(), scratch=()):
-    n_in, n_out = len(operands), len(outs)
+def room(shape, dtype):
+    return pltpu.VMEM(tuple(shape), dtype)
+
+
+def talk(name, cid, groups, operands, outs, plan, copies, in_vmem=(), out_vmem=(), scratch=(), rooms=()):
+    n_in, n_out, n_rooms = len(operands), len(outs), len(rooms)
 
     def kernel(*refs):
         ins, results = refs[:n_in], refs[n_in : n_in + n_out]
-        buffers, (send_sems, recv_sems) = refs[n_in + n_out : -2], refs[-2:]
+        held = refs[n_in + n_out : n_in + n_out + n_rooms]
+        buffers, (send_sems, recv_sems) = refs[n_in + n_out + n_rooms : -2], refs[-2:]
         meet(groups)
-        wires = Wires(send_sems, recv_sems)
+        wires = Wires(send_sems, recv_sems, held)
         run_all(*plan(wires, ins, results, buffers))
         assert wires.used <= copies, wires.used
 
@@ -703,9 +745,9 @@
         out_shape=outs,
         in_specs=[where(i, in_vmem) for i in range(n_in)],
         out_specs=[where(i, out_vmem) for i in range(n_out)],
-        scratch_shapes=list(scratch) + [pltpu.SemaphoreType.DMA((copies,)), pltpu.SemaphoreType.DMA((copies,))],
+        scratch_shapes=list(rooms) + list(scratch) + [pltpu.SemaphoreType.DMA((copies,)), pltpu.SemaphoreType.DMA((copies,))],
         compiler_params=pltpu.CompilerParams(
-            collective_id=cid, has_side_effects=True, vmem_limit_bytes=48 * 1024 * 1024
+            collective_id=cid, has_side_effects=True, vmem_limit_bytes=60 * 1024 * 1024
         ),
         name=name,
     )(*operands)
@@ -745,28 +787,25 @@
     return shape_of(shape, array.dtype)
 
 
-def gather_with(name, cid, block, over_dp, swaps=(), cut=2):
-    count, packs = lax.axis_size("seq"), lax.axis_size("dp")
-    outs = [shape_of((count,) + block.shape, block.dtype)] + [shape_of((packs,) + a.shape, a.dtype) for a in over_dp]
-    outs += [window_shape(item) for item in swaps]
-    n = 1 + len(over_dp)
-
-    def plan(wires, ins, results, _):
-        jobs, patient = gather_jobs(wires, over_dp, ins[1:n], results[1:n])
-        patient += [swap_dp(wires, window(a, item), b) for a, b, item in zip(ins[n:], results[n:], swaps)]
+def gather_with(name, cid, block, beside, cut=2):
+    count = lax.axis_size("seq")
+    outs = [shape_of((count,) + block.shape, block.dtype)] + beside.outs
+
+    def plan(wires, ins, results, scratch):
+        jobs, patient = beside.jobs(wires, ins[1:], results[1:], scratch)
         return [gather_line(wires, ins[0], results[0], cut)] + jobs, patient
 
     got = talk(
-        name, cid, ("line", "dp") if over_dp or swaps else ("line",), (block, *over_dp, *(i[0] for i in swaps)), outs, plan,
-        1 + 4 * (count // 2) * cut + HALVES * len(over_dp) + packs * len(swaps),
+        name, cid, ("line", "dp") if beside.arrays else ("line",), (block, *beside.arrays), outs, plan,
+        1 + 4 * (count // 2) * cut + beside.copies, out_vmem=[1 + i for i in beside.in_vmem_outs], scratch=beside.scratch,
+        rooms=beside.patient_rooms + [room(block.shape, block.dtype)] + beside.job_rooms,
     )
-    return [g.reshape((-1,) + a.shape[1:]) for g, a in zip(got, (block, *over_dp))] + list(got[n:])
+    return [got[0].reshape((-1,) + block.shape[1:])] + beside.finish(got[1:])
 
 
 def columns_out(wires, source, out):
     mine, me, count, packs = lax.axis_index("dp"), lax.axis_index("seq"), lax.axis_size("seq"), lax.axis_size("dp")
     own = wires.keep(source.at[me], out.at[mine, me])
-    own.start()
     sent, onward = [], []
     for step in range(1, count):
         sent.append(wires.copy(source.at[lax.rem(me + step, count)], out.at[mine, me], seq_peer(step)))
@@ -774,6 +813,7 @@
     for step in range(1, packs):
         onward.append(wires.copy(source.at[me], out.at[mine, me], pack_peer(step)))
         onward[-1].start()
+    own.start()
     for step in range(1, count):
         yield True
         sent[step - 1].wait_recv()
@@ -792,7 +832,6 @@
 def spread_all(wires, source, out):
     mine, me, count, packs = lax.axis_index("dp"), lax.axis_index("seq"), lax.axis_size("seq"), lax.axis_size("dp")
     own = wires.keep(source, out.at[mine, me])
-    own.start()
     sent, onward = [], []
     for step in range(1, packs):
         sent.append(wires.copy(source, out.at[mine, me], pack_peer(step)))
@@ -800,6 +839,7 @@
     for step in range(1, count):
         onward.append(wires.copy(source, out.at[mine, me], seq_peer(step)))
         onward[-1].start()
+    own.start()
     for other in range(1, packs):
         yield True
         sent[other - 1].wait_recv()
@@ -832,7 +872,8 @@
         ], [spread_dp(wires, a, b) for a, b in zip(ins[2:], results[2:])]
 
     copies = count * packs + count + 4 * (count // 2) * cut + packs * len(over_dp) + 8
-    got = talk("first_exchange", 1, ("dp", "seq"), (mix, block, *over_dp), outs, plan, copies)
+    rooms = [room(a.shape, a.dtype) for a in over_dp] + [room(mix.shape[1:], mix.dtype), room(block.shape, block.dtype)]
+    got = talk("first_exchange", 1, ("dp", "seq"), (mix, block, *over_dp), outs, plan, copies, rooms=rooms)
     return [array.reshape(-1, array.shape[-1]) for array in got]
 
 
@@ -841,31 +882,129 @@
     (got,) = talk(
         name, cid, ("seq",), (block,), [shape_of((count,) + block.shape, block.dtype)],
         lambda wires, ins, outs, _: ([spread_seq(wires, ins[0], outs[0])],), count,
+        rooms=[room(block.shape, block.dtype)],
     )
     return got
 
 
-def scatter_with(name, cid, terms, swaps=(), gathers=(), cut=2):
-    count, packs = lax.axis_size("seq"), lax.axis_size("dp")
-    rows, width = terms.shape[0] // count, terms.shape[1]
-    box = pltpu.VMEM((count // 2, rows, width), terms.dtype)
-    blocks = [item[0] for item in swaps]
-    outs = [shape_of((rows, width), jnp.float32)] + [window_shape(item) for item in swaps]
-    outs += [shape_of((packs,) + a.shape, a.dtype) for a in gathers]
-    n = 1 + len(blocks)
-
-    def plan(wires, ins, results, boxes):
-        jobs, patient = gather_jobs(wires, gathers, ins[n:], results[n:])
-        patient += [swap_dp(wires, window(a, item), b) for a, b, item in zip(ins[1:n], results[1:n], swaps)]
-        return [scatter_line(wires, ins[0], results[0], *boxes, cut)] + jobs, patient
+def fold_dp(wires, source, out, boxes, here, sums, idle=2):
+    me = lax.axis_index("dp")
+    half = source.shape[1] // 2
+    bit = lax.rem(me, 2)
+    flip = {1: me + 1 - 2 * bit, 2: lax.rem(me + 2, 4)}
+    corner = lax.rem(flip[1] + 2, 4)
+    rows = {1: pl.ds(0, half), 2: pl.ds(half, half)}
+    load = [wires.load(source.at[me], here.at[0])]
+    passing, direct, second = {}, {}, {}
+    for way in (1, 2):
+        passing[way] = wires.copy(source.at[corner, rows[way]], boxes.at[1 + way], {"dp": flip[way]})
+        passing[way].start()
+        load.append(wires.load(source.at[flip[3 - way], rows[way]], here.at[1, rows[way]]))
+    for copy in load:
+        copy.start()
+    for _ in range(idle):
+        yield True
+    for way in (1, 2):
+        yield True
+        load[way].wait()
+        passing[way].wait_recv()
+        add_into(sums.at[way - 1], [here.at[1, rows[way]], boxes.at[1 + way]])
+        second[way] = wires.copy(sums.at[way - 1], boxes.at[3 + way], {"dp": flip[3 - way]})
+        second[way].start()
+        direct[way] = wires.copy(source.at[flip[way], rows[way]], boxes.at[way - 1], {"dp": flip[way]})
+        direct[way].start()
+    load[0].wait()
+    yield PATIENT
+    for way in (1, 2):
+        direct[way].wait_recv()
+        second[way].wait_recv()
+        add_into(out.at[rows[way]], [here.at[0, rows[way]], boxes.at[way - 1], boxes.at[3 + way]])
+    for way in (1, 2):
+        passing[way].wait_send()
+        direct[way].wait_send()
+        second[way].wait_send()
+
+
+def can_fold(array):
+    return lax.axis_size("dp") == 4 and array.shape[1] % 32 == 0
+
+
+def fold_scratch(array):
+    _, rows, columns = array.shape
+    return [
+        pltpu.VMEM((6, rows // 2, columns), array.dtype),
+        pltpu.VMEM((2, rows, columns), array.dtype),
+        pltpu.VMEM((2, rows // 2, columns), array.dtype),
+    ]
+
+
+class Beside:
+    def __init__(self, gathers=(), swaps=(), sums=()):
+        self.gathers, self.swaps, self.sums = list(gathers), list(swaps), list(sums)
+        self.arrays = self.gathers + self.swaps + self.sums
+        packs = lax.axis_size("dp")
+        self.outs = [shape_of((packs,) + a.shape, a.dtype) for a in self.gathers]
+        self.outs += [shape_of(a.shape, a.dtype) for a in self.swaps]
+        self.scratch = []
+        for a in self.sums:
+            fold = can_fold(a)
+            self.outs.append(shape_of(a.shape[1:] if fold else a.shape, a.dtype))
+            self.scratch += fold_scratch(a) if fold else []
+        self.copies = HALVES * len(self.gathers) + packs * len(self.swaps) + 16 * len(self.sums)
+        self.job_rooms = [room(a.shape, a.dtype) for a in self.gathers if can_halve(a)]
+        self.patient_rooms = [room(a.shape, a.dtype) for a in self.gathers if not can_halve(a)]
+        self.patient_rooms += [room(a.shape[1:], a.dtype) for a in self.swaps]
+        self.patient_rooms += [room(a.shape[1:], a.dtype) for a in self.sums if not can_fold(a)]
+        self.in_vmem_outs = [len(self.gathers) + len(self.swaps) + i for i, a in enumerate(self.sums) if can_fold(a)]
+
+    def jobs(self, wires, ins, results, scratch):
+        g, s = len(self.gathers), len(self.gathers) + len(self.swaps)
+        jobs, patient = gather_jobs(wires, self.gathers, ins[:g], results[:g])
+        patient += [swap_dp(wires, a, b) for a, b in zip(ins[g:s], results[g:s])]
+        scratch = list(scratch)
+        for array, a, b in zip(self.sums, ins[s:], results[s:]):
+            if can_fold(array):
+                jobs.append(fold_dp(wires, a, b, *scratch[:3]))
+                scratch = scratch[3:]
+            else:
+                patient.append(swap_dp(wires, a, b))
+        return jobs, patient
+
+    def finish(self, got):
+        g, s = len(self.gathers), len(self.gathers) + len(self.swaps)
+        got = list(got)
+        done = [r.reshape((-1,) + a.shape[1:]) for r, a in zip(got[:g], self.gathers)] + got[g:s]
+        return done + [r if can_fold(a) else add_packs(r).astype(r.dtype) for r, a in zip(got[s:], self.sums)]
+
+
+def scatter_with(name, cid, out_shape, factors, product, beside, cut=2):
+    count = lax.axis_size("seq")
+    rows, width = out_shape
+    box = pltpu.VMEM((count // 2, rows, width), jnp.bfloat16)
+    made = [pltpu.VMEM((count, rows, width), jnp.bfloat16)] if product else []
+    if not product:
+        factors = (factors[0].reshape(count, rows, width),)
+    n_f, n_b = len(factors), len(beside.arrays)
+    outs = [shape_of((rows, width), jnp.float32)] + beside.outs
+
+    def plan(wires, ins, results, scratch):
+        terms = scratch[0] if product else ins[0]
+        boxes, rest = scratch[len(made) : len(made) + 4], scratch[len(made) + 4 :]
+        jobs, patient = beside.jobs(wires, ins[n_f:], results[1:], rest)
+
+        def produce(dest):
+            if product:
+                product(dest, ins[:n_f], terms)
+
+        return jobs + [scatter_line(wires, produce, terms, results[0], *boxes, cut)], patient
 
     got = talk(
-        name, cid, ("line", "dp") if swaps or gathers else ("line",),
-        (terms.reshape(count, rows, width), *blocks, *gathers), outs, plan,
-        3 * (count // 2) * cut + packs * len(blocks) + HALVES * len(gathers),
-        in_vmem=(0,), out_vmem=(0,), scratch=(box,) * 5,
+        name, cid, ("line", "dp") if n_b else ("line",), (*factors, *beside.arrays), outs, plan,
+        3 * (count // 2) * cut + beside.copies,
+        in_vmem=range(n_f), out_vmem=[0] + [1 + i for i in beside.in_vmem_outs], scratch=made + [box] * 4 + beside.scratch,
+        rooms=beside.patient_rooms + beside.job_rooms,
     )
-    return list(got[:n]) + [g.reshape((-1,) + a.shape[1:]) for g, a in zip(got[n:], gathers)]
+    return [got[0]] + beside.finish(got[1:])
 
 
 def swap_places(name, cid, arrays):
@@ -873,6 +1012,7 @@
     return talk(
         name, cid, ("seq",), arrays, [shape_of(a.shape, a.dtype) for a in arrays],
         lambda wires, ins, outs, _: ([], [swap_seq(wires, i, o) for i, o in zip(ins, outs)]), count * len(arrays),
+        rooms=[room(a.shape[1:], a.dtype) for a in arrays],
     )
 
 
@@ -934,10 +1074,11 @@
 
 
 def feed_forward_kernel(
-    cut, block_ref, top_ref, wgu_hbm, wd_hbm,
-    x_out, hid_out, dgu_out, down_out, mid_out,
-    wgu_ref, wd_ref, xbuf, topbuf, hidbuf, dgubuf, downbuf, terms, near, from_left, from_right, outbox,
-    local_sems, line_send, line_recv, near_send, near_recv, sum_send, sum_recv, across_send, across_recv,
+    cut, block_ref, top_first, top_second, wgu_hbm, wd_hbm,
+    x_out, down_out, g_gu_out, g_down_out, mid_out,
+    wgu_ref, wd_ref, xbuf, topbuf, hidbuf, dgubuf, downbuf, g_gu, g_down, g_gu_low, g_down_low,
+    terms, near, from_left, from_right, outbox,
+    local_sems, pack_send, pack_recv, line_send, line_recv, near_send, near_recv, sum_send, sum_recv, across_send, across_recv,
 ):
     me, count = lax.axis_index("seq"), lax.axis_size("seq")
     chips, chip, core = count // 2, me // 2, lax.rem(me, 2)
@@ -945,8 +1086,11 @@
     tall = block_ref.shape[0]
     step = tall // cut
     units = wd_ref.shape[0]
+    packs = lax.axis_size("dp")
+    pack = lax.axis_index("dp")
+    share = units // packs
     width = wd_ref.shape[1]
-    meet(("line",))
+    meet(("line", "dp"))
 
     def lines(part):
         return pl.ds(part * step, step)
@@ -995,8 +1139,7 @@
             sum_send.at[at], sum_recv.at[at], on_line(2 if right else -2), MESH,
         )
 
-    own = pltpu.make_async_copy(block_ref, x_out.at[me], local_sems.at[0])
-    own.start()
+    own = Kept(block_ref, x_out.at[me], xbuf.at[0], local_sems.at[0])
     for part in range(cut):
         for sign in (1, -1):
 
@@ -1009,6 +1152,7 @@
         pltpu.make_async_copy(wgu_hbm, wgu_ref, local_sems.at[1]),
         pltpu.make_async_copy(wd_hbm, wd_ref, local_sems.at[2]),
     ]
+    own.start()
     for copy in weights:
         copy.start()
     own.wait()
@@ -1036,8 +1180,20 @@
             terms[pl.ds(2 * dest, 2), :, at : at + wide] = mid.reshape(2, tall, wide)
         for part in range(cut):
             across(dest, part).start()
+
+    def compute_rest():
+        x = xbuf[...].reshape(2 * tall, width)
+        top = topbuf[...].reshape(2 * tall, width)
+        hid = hidbuf[...].reshape(2 * tall, units)
+        dgu = dgubuf[...].reshape(2 * tall, 2 * units)
+        wide = 512
         for at in range(0, width, wide):
             downbuf[:, :, at : at + wide] = nn(hid, wd_ref[:, at : at + wide]).astype(jnp.bfloat16).reshape(2, tall, wide)
+        for at in range(0, units, 128):
+            n = min(128, units - at)
+            g_down[at : at + n, :] += tn(hid[:, at : at + n], top)
+        for at in range(0, width, 256):
+            g_gu[at : at + 256, :] += tn(x[:, at : at + 256], dgu)
 
     def send_sum(right, dest, part, first, in_turn=True):
         mine = [terms.at[2 * dest + core, lines(part)], near.at[dest, lines(part)]]
@@ -1071,23 +1227,23 @@
 
         @pl.when(inside(dest) & (i + 1 - j > 0))
         def _():
-            top = pltpu.make_async_copy(top_ref.at[pl.ds(2 * dest, 2)], topbuf, local_sems.at[1])
-            top.start()
+            half = tall // 2
+            tops = [
+                pltpu.make_async_copy(
+                    ref.at[pl.ds(2 * dest, 2)], topbuf.at[:, pl.ds(at, half)], local_sems.at[1 + at // half]
+                )
+                for ref, at in ((top_first, 0), (top_second, half))
+            ]
+            for top in tops:
+                top.start()
             for part in range(cut):
                 over_came(sign, i, part)
             x = pltpu.make_async_copy(x_out.at[pl.ds(2 * dest, 2)], xbuf, local_sems.at[0])
             x.start()
-            top.wait()
+            for top in tops:
+                top.wait()
             x.wait()
             compute(dest)
-            saved = [
-                pltpu.make_async_copy(hidbuf, hid_out.at[pl.ds(2 * dest, 2)], local_sems.at[0]),
-                pltpu.make_async_copy(dgubuf, dgu_out.at[pl.ds(2 * dest, 2)], local_sems.at[1]),
-                pltpu.make_async_copy(downbuf, down_out.at[pl.ds(2 * dest, 2)], local_sems.at[2]),
-            ]
-            for copy in saved:
-                copy.start()
-
             @pl.when((chip == 0) & (dest > 0) & (dest < chips - 1))
             def _():
                 for part in range(cut):
@@ -1098,13 +1254,15 @@
                 for part in range(cut):
                     send_sum(False, dest, part, True, False)
 
-            for copy in saved:
-                copy.wait()
-
-    def distance(i, _):
+            compute_rest()
+            saved = pltpu.make_async_copy(downbuf, down_out.at[pl.ds(2 * dest, 2)], local_sems.at[2])
+            saved.start()
+            saved.wait()
+
+    def forward(i):
         for sign in (1, -1):
 
-            @pl.when((i > 0) & inside(chip + sign * i))
+            @pl.when((i > 0) & (i < chips) & inside(chip + sign * i))
             def _():
                 for part in range(cut):
                     along_came(sign, i, part)
@@ -1115,14 +1273,41 @@
 
                     over(sign, i, part).start()
 
+    def distance(i, _):
         def side(j, _):
             visit(i, j)
+
+            @pl.when((j == 0) & (i > 0) | (j == 1) & (i == 0))
+            def _():
+                forward(i + 1)
+
             return 0
 
         lax.fori_loop(0, 2, side, 0)
         return 0
 
+    g_gu[...] = jnp.zeros_like(g_gu)
+    g_down[...] = jnp.zeros_like(g_down)
     lax.fori_loop(0, chips, distance, 0)
+
+    def lower(i, _):
+        lines = pl.ds(pl.multiple_of(i * 16, 16), 16)
+        g_down_low[lines, :] = g_down[lines, :].astype(jnp.bfloat16)
+        return 0
+
+    lax.fori_loop(0, units // 16, lower, 0)
+    kept = pltpu.make_async_copy(g_down_low.at[pl.ds(pack * share, share)], g_down_out.at[pack], local_sems.at[2])
+    kept.start()
+
+    def swap(step):
+        peer = lax.rem(pack + step, packs)
+        return pltpu.make_async_remote_copy(
+            g_down_low.at[pl.ds(peer * share, share)], g_down_out.at[pack],
+            pack_send.at[step], pack_recv.at[step], pack_peer(step), MESH,
+        )
+
+    for turn in range(1, packs):
+        swap(turn).start()
 
     @pl.when(chip == 0)
     def _():
@@ -1181,6 +1366,18 @@
             sum_came(False, chip, part)
             add_into(mid_out.at[lines(part)], mine + [left_in, right_in])
 
+    def lower_gu(i, _):
+        lines = pl.ds(pl.multiple_of(i * 16, 16), 16)
+        g_gu_low[lines, :] = g_gu[lines, :].astype(jnp.bfloat16)
+        return 0
+
+    lax.fori_loop(0, width // 16, lower_gu, 0)
+    gu_kept = pltpu.make_async_copy(g_gu_low, g_gu_out, local_sems.at[1])
+    gu_kept.start()
+    for turn in range(1, packs):
+        swap(turn).wait()
+    kept.wait()
+    gu_kept.wait()
     for part in range(cut):
         for dest in range(chips):
             across(dest, part).wait_send()
@@ -1211,17 +1408,18 @@
                         over(sign, i, part).wait_send()
 
 
-def feed_forward(cid, block, top, w_gu, w_d, cut=2):
+def feed_forward(cid, block, tops, w_gu, w_d, cut=2):
     count = lax.axis_size("seq")
     chips = count // 2
     tall, width = block.shape
     units = w_d.shape[0]
+    packs = lax.axis_size("dp")
     bf16 = jnp.bfloat16
     outs = [
         shape_of((count, tall, width), bf16),
-        shape_of((count, tall, units), bf16),
-        shape_of((count, tall, 2 * units), bf16),
         shape_of((count, tall, width), bf16),
+        shape_of((width, 2 * units), bf16),
+        shape_of((packs, units // packs, width), bf16),
         shape_of((tall, width), jnp.float32),
     ]
     box = pltpu.VMEM((chips, tall, width), bf16)
@@ -1231,7 +1429,7 @@
     got = pl.pallas_call(
         functools.partial(feed_forward_kernel, cut),
         out_shape=outs,
-        in_specs=[anywhere] * 4,
+        in_specs=[anywhere] * 5,
         out_specs=[anywhere] * 4 + [vmem],
         scratch_shapes=[
             pltpu.VMEM(w_gu.shape, bf16),
@@ -1241,18 +1439,21 @@
             pltpu.VMEM((2, tall, units), bf16),
             pltpu.VMEM((2, tall, 2 * units), bf16),
             pltpu.VMEM((2, tall, width), bf16),
+            pltpu.VMEM((width, 2 * units), jnp.float32),
+            pltpu.VMEM((units, width), jnp.float32),
+            pltpu.VMEM((width, 2 * units), bf16),
+            pltpu.VMEM((units, width), bf16),
             pltpu.VMEM((count, tall, width), bf16),
             box, box, box, box,
-            dma(3),
+            dma(3), dma(packs), dma(packs),
         ] + [dma(2 * chips * cut)] * 6 + [dma(chips * cut)] * 2,
         compiler_params=pltpu.CompilerParams(
-            collective_id=cid, has_side_effects=True, vmem_limit_bytes=56 * 1024 * 1024
+            collective_id=cid, has_side_effects=True, vmem_limit_bytes=62 * 1024 * 1024
         ),
         cost_estimate=pl.CostEstimate(flops=flops, bytes_accessed=20 << 20, transcendentals=0),
         name="feed_forward",
-    )(block, top.reshape(count, tall, width), w_gu, w_d)
-    flat = [g.reshape(-1, g.shape[-1]) for g in got]
-    return flat
+    )(block, *tops, w_gu, w_d)
+    return got
 
 
 def cross_rows(left_side, right_side):
@@ -1370,8 +1571,9 @@
     bias_own = lax.dynamic_index_in_dim(lr_bias.reshape(outer, per_seq, heads // outer), place, 1, keepdims=False)
     bias_own = bias_own.reshape(heads).astype(floats)
 
-    later_top, rows_all = lax.optimization_barrier((grad_out[0], rows_all))
-    d_top = lax.all_gather(later_top, "seq", axis=0, tiled=True)
+    half = span // 2
+    later_top, rows_all = lax.optimization_barrier((grad_out[0, :half], rows_all))
+    top_first = lax.all_gather(later_top, "seq", axis=0)
     gu_mine = split_columns((w_gate_up,), unit_cuts)
 
     inputs = rows_all.astype(floats)
@@ -1397,6 +1599,8 @@
     )
     w_d = w_d.reshape(-1, w_d.shape[-1])
     mixed, *saved = results
+    later_top, mixed = lax.optimization_barrier((grad_out[0, half:], mixed))
+    top_second = lax.all_gather(later_top, "seq", axis=0)
 
     mean_own = jnp.mean(mixed, -1)
     spread_own = jnp.sum((mixed - mean_own[:, None]) ** 2, -1)
@@ -1408,28 +1612,38 @@
     normed_out = out_hat * post_gain + post_shift
     gelu_gate, gelu_pull = jax.vjp(jax.nn.gelu, gate_pre)
     gated_unit = (gelu_gate * normed_out).astype(bf16)
-    branch_terms, d_top = lax.optimization_barrier((dot(gated_unit, w_o).astype(bf16), d_top))
-    branch, w_gu = scatter_with("scatter_branch", 3, branch_terms, (), (gu_part.reshape(-1, gu_part.shape[-1]),))
+    pair = 2 * span
+    wide = 512
+
+    def branch_terms(dest, factors, terms):
+        unit = factors[0][dest * pair : (dest + 1) * pair, :]
+        for at in range(0, width, wide):
+            part = nn(unit, factors[1][:, at : at + wide]).astype(bf16)
+            terms[2 * dest : 2 * dest + 2, :, at : at + wide] = part.reshape(2, span, wide)
+
+    branch, w_gu = scatter_with(
+        "scatter_branch", 3, (span, width), (gated_unit, w_o), branch_terms,
+        Beside(gathers=(gu_part.reshape(-1, gu_part.shape[-1]),)),
+    )
     inputs = tokens[0].astype(floats)
     residual = inputs + branch
     scale_two = lax.rsqrt(jnp.mean(residual * residual, -1, keepdims=True) + EPSILON)
     normed_mid = residual * scale_two
-    x_two, hidden, d_gate_up, down, d_xtwo = feed_forward(5, (normed_mid * gain_two).astype(bf16), d_top, w_gu, w_d)
+    _, down, g_gate_up, g_down, d_xtwo = feed_forward(
+        5, (normed_mid * gain_two).astype(bf16), (top_first, top_second), w_gu, w_d
+    )
+    down = down.reshape(-1, width)
     pack_rows = lambda array: array.reshape((packs, -1) + array.shape[1:])
-    g_gate_up = pack_rows(cross_rows(x_two, d_gate_up).astype(bf16))
-    g_down = pack_rows(cross_rows(hidden, d_top).astype(bf16))
+    g_gate_up = pack_rows(g_gate_up)
+    g_down = add_packs(g_down)[:units]
     g_two = jnp.sum(d_xtwo * normed_mid, axis=0)
     d_mid = d_xtwo * gain_two
     d_residual = grad_out[0].astype(floats) + scale_two * (
         d_mid - normed_mid * jnp.mean(d_mid * normed_mid, -1, keepdims=True)
     )
-    d_branch, g_gate_up = gather_with(
-        "gather_branch", 6, d_residual.astype(bf16), (), [(g_gate_up, None, None)]
-    )
-    g_gate_up = add_packs(g_gate_up).astype(bf16)
-    down, d_branch = lax.optimization_barrier((down, d_branch))
-    down = lax.psum_scatter(down, "seq", scatter_dimension=0, tiled=True)
-    result = residual + down.astype(floats)
+    d_branch, g_gate_up = gather_with("gather_branch", 6, d_residual.astype(bf16), Beside(sums=(g_gate_up,)))
+    down_first, d_branch = lax.optimization_barrier((down[:, : width // 2], d_branch))
+    down_first = lax.psum_scatter(down_first, "seq", scatter_dimension=0, tiled=True)
     g_out = cross_rows(gated_unit, d_branch).astype(bf16)
     d_unit = cross_cols(d_branch, w_o)
     d_normed = d_unit * gelu_gate
@@ -1442,16 +1656,18 @@
     d_gate_pre = gelu_pull(d_unit * normed_out)[0].astype(bf16)
     place_rows = lambda array: array.reshape((per_seq, -1) + array.shape[1:])
     g_gate = pack_rows(cross_rows(x_one, d_gate_pre).astype(bf16))
-    d_qkv, d_rate, d_w0, d_c0, d_gain, d_shift, g_gate_up, g_down, g_gate, *g_outs = inner_backward(
+    d_qkv, d_rate, d_w0, d_c0, d_gain, d_shift, g_gate_up, g_gate, *g_outs = inner_backward(
         11, fresh, qkv, e_rows, d_mixed, saved, gain_t, shift_t, (place_rows(g_gate_up),),
-        [(g_down, None, None), (g_gate, None, None)] + [(pack_rows(g_out), None, None)] * aligned,
+        [(g_gate, None, None)] + [(pack_rows(g_out), None, None)] * aligned,
     )
     (g_gate_up,) = join_columns(g_gate_up, (w_gate_up.shape[1],), unit_cuts)
-    g_down = add_packs(g_down)[:units]
     if aligned:
         g_out = add_packs(g_outs[0])
     else:
         g_out = lax.psum_scatter(put_rows(g_out), both, scatter_dimension=0, tiled=True).astype(floats)
+    down_second, d_qkv = lax.optimization_barrier((down[:, width // 2 :], d_qkv))
+    down_second = lax.psum_scatter(down_second, "seq", scatter_dimension=0, tiled=True)
+    result = residual + jnp.concatenate([down_first, down_second], axis=1).astype(floats)
     d_rate = d_rate.reshape(blocks, heads, MB).transpose(0, 2, 1).reshape(length, heads)
     d_logit = (d_rate * (1.0 / HD) * lr_sigm * (1.0 - lr_sigm)).astype(bf16)
     g_qkv = cross_rows(x_one, d_qkv).astype(bf16)
@@ -1475,10 +1691,9 @@
         [d_w0.reshape(HD, heads, HD).transpose(1, 2, 0).reshape(mine, HD), g_vec, jnp.zeros((mine, extra - HD - 5), floats)],
         axis=1,
     )
-    swaps = [(pack_rows(g_beside), None, None), (pack_rows(g_qkv), None, None)]
-    d_xone, *got = scatter_with(
-        "scatter_first", 8, d_xone.astype(bf16), [(pack_rows(g_heads), None, None)] * aligned + swaps
-    )
+
+    swaps = [pack_rows(g_heads)] * aligned + [pack_rows(g_beside), pack_rows(g_qkv)]
+    d_xone, *got = scatter_with("scatter_first", 8, (span, width), (d_xone.astype(bf16),), None, Beside(swaps=swaps))
     if aligned:
         g_heads = add_packs(got[0])
     else:

time: 691 us -> 643 us (0.931)
  Pallas kernels: 538 us -> 500 us
  matrix products: 63.6 us -> 47.5 us
    pallas_call x1, Pallas kernels: 64.7 us -> 41.8 us  [inner_backward(): pl.pallas_call(functools.partial(backward_kernel, heads, per, len(seq_arr...]
    pallas_call x1, Pallas kernels: 52.7 us -> 41.4 us  [inner_forward(): pl.pallas_call(functools.partial(forward_kernel, heads, per, len(seq_arra...]
    dot_general x6 -> x4, matrix products: 26.8 us -> 15.8 us  [cross_rows(): lax.dot_general(left_side, right_side, (((0,), (0,)), ((), ())), preferre...]
    pallas_call x1, Pallas kernels: 101 us -> 94.3 us  [feed_forward(): pl.pallas_call(functools.partial(feed_forward_kernel, cut), out_shape=out...]
    unnamed x88 -> x86, local copies, waits for them, and re-layouts: 15.3 us -> 9.9 us
    dot_general x4 -> x3, matrix products: 20.3 us -> 17.2 us  [dot(): return jnp.dot(left_side, right_side, preferred_element_type=jnp.float32)]
  transfers between devices with their start and end apart: 2 -> 4, of which waited for: 0 -> 0; matrix products, arithmetic and copies ran while one was open for 13% -> 12% of each run, Pallas kernels for 33% -> 34%
where the time goes in v5:
time: 643 us; the launch traced here: 633 us
  Pallas kernels  500 us (78%)
  matrix products  47.5 us (7%)
  other arithmetic  35.6 us (6%)
  local copies, waits for them, and re-layouts  33.8 us (5%)
  between operations  14.9 us (2%)
    pallas_call x7, Pallas kernels, talk(): pl.pallas_call(kernel, out_shape=outs, in_specs=[where(i, in_vmem) for i...  316 us
    pallas_call x1, Pallas kernels, feed_forward(): pl.pallas_call(functools.partial(feed_forward_kernel, cut), out_shape=out...  94.3 us
    pallas_call x1, Pallas kernels, inner_backward(): pl.pallas_call(functools.partial(backward_kernel, heads, per, len(seq_arr...  41.8 us
    pallas_call x1, Pallas kernels, inner_forward(): pl.pallas_call(functools.partial(forward_kernel, heads, per, len(seq_arra...  41.4 us
    dot_general x3, matrix products, dot(): return jnp.dot(left_side, right_side, preferred_element_type=jnp.float32)  17.2 us
    dot_general x4, matrix products, cross_rows(): lax.dot_general(left_side, right_side, (((0,), (0,)), ((), ())), preferre...  15.8 us
    dot_general x2, matrix products, cross_cols(): lax.dot_general(left_side, right_side, (((1,), (1,)), ((), ())), preferre...  14.5 us
  transfers between devices with their start and end apart: 4, of which 0 were waited for; matrix products, arithmetic and copies ran while one was open for 12% of the time, Pallas kernels for 34%

profile of v5, /device:TPU:9, one launch (start us, length us, event | category | flops | bytes accessed | tf_op | source)
XLA Modules:
  0.0 632.7 jit_solution(6030223855507105349)
XLA Ops:
  7.2 1.9 slice_bitcast_fusion.2
  20.3 79.1 %first_exchange.1 = (bf16[4,8,64,1152]{3,2,1,0:T(8,128)(2,1)}, bf16[8,128,2048]{2,1,0:T(8,128)(2,1)}, bf16[4,64,2048]{2,1,0:T(8,128)(2,1)}, bf16[4,64,128]{2,1,0:T(8,128)(2,1)}) custom-call(bf16[8,64,1152]{2,1,0:T(8,128)(2,1)} %copy-done.1, bf16[128,2048]{1,0:T(8,128)(2,1)} %bitcast.151, bf16[64,2048]{1,0:T(8,128)(2,1)} %refs_2_.1, ...), custom_call_target="tpu_custom_call" | custom-call | tf_op jit(solution)/shard_map/first_exchange/pallas_call | solution.py:743
  99.5 2.7 slice_convert_fusion
  105.6 3.3 fusion.2
  109.0 3.7 broadcast_multiply_fusion
  117.8 8.3 %fusion.3.qkv_ref = f32[1024,768]{1,0:T(8,128)} fusion(bf16[1024,2048]{1,0:T(8,128)(2,1)} %copy-done.18, bf16[2048,1152]{1,0:T(8,128)(2,1)} %bitcast.170), kind=kOutput, calls=%fused_computation.8 | convolution fusion | flops 3221225472 | bytes 10485760 | tf_op jit(solution)/shard_map/dot_general | solution.py:1468
  126.1 41.4 %inner_forward.1 = (f32[1024,256]{1,0:T(8,128)S(1)}, bf16[64,64,256]{2,1,0:T(8,128)(2,1)}, f32[64,64,64]{2,1,0:T(8,128)}, f32[64,64,64]{2,1,0:T(8,128)}, f32[64,...) custom-call(s32[64]{0:T(128)S(1)} %add_convert_fusion.1.fresh_ref, ...), custom_call_target="tpu_custom_call" | custom-call | tf_op jit(solution)/shard_map/inner_forward/pallas_call | solution.py:137
  170.8 6.4 %share_moments.1 = f32[8,2,1024]{2,1,0:T(2,128)} custom-call(f32[2,1024]{1,0:T(2,128)} %pad_maximum_fusion.1.refs_0_), custom_call_target="tpu_custom_call" | custom-call | tf_op jit(solution)/shard_map/share_moments/pallas_call | solution.py:743
  177.2 1.6 copy.242
  179.9 5.3 multiply_convert_fusion.1
  185.2 64.7 %scatter_branch.1 = (f32[128,2048]{1,0:T(8,128)}, bf16[4,512,1408]{2,1,0:T(8,128)(2,1)}) custom-call(bf16[1024,256]{1,0:T(8,128)(2,1)} %get-tuple-element.147.refs_0_, bf16[256,2048]{1,0:T(8,128)(2,1)} %bitcast.160, bf16[512,1408]{1,0:T(8,128)(2,1)} %bitcast.144), custom_call_target="tpu_custom_call" | custom-call | tf_op jit(solution)/shard_map/scatter_branch/pallas_call | solution.py:743
  253.4 94.3 %feed_forward.1 = (bf16[8,128,2048]{2,1,0:T(8,128)(2,1)}, bf16[8,128,2048]{2,1,0:T(8,128)(2,1)}, bf16[2048,1408]{1,0:T(8,128)(2,1)}, bf16[4,176,2048]{2,1,0:T(8,128)(2,1)}, f32[128,2048]{1,0:T(8,128)}) custom-call(bf16[128,2048]{1,0:T(8,128)(2,1)} %multiply_convert_fusion.block_ref, bf16[8,64,2048]{2,1,0:T(8,128)(2,1)} %bitcast.221, ...), custom_call_target="tpu_custom_call" | custom-call | flops 17716740096 | bytes 20971520 | tf_op jit(solution)/shard_map/feed_forward/pallas_call | solution.py:1429
  347.7 4.8 fusion.49
  354.1 64.2 %gather_branch.1 = (bf16[8,128,2048]{2,1,0:T(8,128)(2,1)}, bf16[512,1408]{1,0:T(8,128)(2,1)}) custom-call(bf16[128,2048]{1,0:T(8,128)(2,1)} %fusion.46.refs_0_, bf16[4,512,1408]{2,1,0:T(8,128)(2,1)} %bitcast.152), custom_call_target="tpu_custom_call" | custom-call | tf_op jit(solution)/shard_map/gather_branch/pallas_call | solution.py:743
  418.4 4.6 convolution_convert_fusion.1
  423.0 3.7 multiply_reduce_fusion.2
  427.3 8.0 %share_sums.1 = f32[8,2,1024]{2,1,0:T(2,128)} custom-call(f32[2,1024]{1,0:T(2,128)} %pad_maximum_fusion.2.refs_0_), custom_call_target="tpu_custom_call" | custom-call | tf_op jit(solution)/shard_map/share_sums/pallas_call | solution.py:743
  436.3 3.7 convolution_convert_fusion.2
  441.0 41.8 %inner_backward.1 = (bf16[1024,768]{1,0:T(8,128)(2,1)}, f32[64,1,64]{2,1,0:T(1,128)S(1)}, f32[64,256]{1,0:T(8,128)S(1)}, f32[64,64]{1,0:T(8,128)S(1)}, f32[64,64...) custom-call(s32[64]{0:T(128)S(1)} %add_convert_fusion.1.fresh_ref, ...), custom_call_target="tpu_custom_call" | custom-call | tf_op jit(solution)/shard_map/inner_backward/pallas_call | solution.py:265
  488.2 10.7 %multiply_reduce_fusion = (f32[2048]{0:T(1024)S(1)}, bf16[1024,2048]{1,0:T(8,128)(2,1)}) fusion(bf16[1024,2048]{1,0:T(8,128)(2,1)} %bitcast.149, f32[1024]{0:T(1024)S(1)} %copy-done.29, bf16[2048,1152]{1,0:T(8,128)(2,1)} %bitcast.172, bf16[1024,128]{1,0:T(8,128)(2,1)} %pad.13, bf16[1024,256]{1,0:T(8,128)(2,1)} %copy-done.40, ...), kind=kOutput, calls=%fused_computation.5 | convolution fusion | flops 4849399808 | bytes 15478784 | tf_op jit(solution)/shard_map/dot_general | solution.py:1464
  499.0 2.6 fusion.7
  501.6 5.0 convolution_convert_fusion
  506.6 64.4 %scatter_first.1 = (f32[128,2048]{1,0:T(8,128)}, f32[4,64,128]{2,1,0:T(8,128)}, bf16[4,512,128]{2,1,0:T(8,128)(2,1)}, bf16[4,512,768]{2,1,0:T(8,128)(2,1)}) custom-call(bf16[8,128,2048]{2,1,0:T(8,128)(2,1)} %bitcast.153, f32[4,64,128]{2,1,0:T(8,128)} %concatenate.53.refs_1_, bf16[4,512,128]{2,1,0:T(8,128)(2,1)} %bitcast.179, bf16[4,512,768]{2,1,0:T(8,128)(2,1)} %bitcast.155), custom_call_target="tpu_custom_call" | custom-call | tf_op jit(solution)/shard_map/scatter_first/pallas_call | solution.py:743
  571.0 1.8 reduce.5
  573.0 2.8 reduce.3
  575.9 2.2 pad_maximum_fusion.refs_0_
  578.0 29.2 %return_columns.1.source = bf16[8,64,1152]{2,1,0:T(8,128)(2,1)} custom-call(bf16[8,64,1152]{2,1,0:T(8,128)(2,1)} %pad_maximum_fusion.refs_0_), custom_call_target="tpu_custom_call" | custom-call | tf_op jit(solution)/shard_map/return_columns/pallas_call | solution.py:743
  608.5 2.1 join_columns.2
  614.3 2.5 join_columns.3
  619.4 1.7 fusion.20
  621.1 1.6 convert_reduce_fusion
  622.8 3.1 fusion.36
  (207 shorter events, 44.7 us)
Async XLA Ops:
  7.2 12.4 %copy-start.30 = (bf16[64,64]{1,0:T(8,128)(2,1)S(1)}, bf16[64,64]{1,0:T(8,128)(2,1)}, u32[]{:S(2)}) copy-start(bf16[64,64]{1,0:T(8,128)(2,1)} %param.26) | copy-start | bytes 24580
  7.2 246.2 %all-gather.5.cloned.1.call-start = ((), (), s32[]{:S(2)}) async-start(), calls=%async_computation.4 | async-start | bytes 2359296 | tf_op jit(solution)/shard_map/all_gather | solution.py:1576
  99.4 154.0 %all-gather.7.cloned.1.call-start = ((), (), s32[]{:S(2)}) async-start(), calls=%async_computation.5 | async-start | bytes 2359296 | tf_op jit(solution)/shard_map/all_gather | solution.py:1603
  99.5 3.8 copy-start.13
  99.5 4.7 copy-start.38
  108.9 3.7 copy-start.18
  108.9 4.1 copy-start.26
  108.9 5.5 copy-start.4
  169.3 453.4 %reduce-scatter.5.cloned.1.call-start = ((), (), s32[]{:S(2)}) async-start(), calls=%async_computation.3 | async-start | bytes 2359296 | tf_op jit(solution)/shard_map/reduce_scatter | solution.py:1669
  179.9 70.0 %copy-start.16 = (bf16[1,128,2048]{2,1,0:T(8,128)(2,1)S(1)}, bf16[1,128,2048]{2,1,0:T(8,128)(2,1)}, u32[]{:S(2)}) copy-start(bf16[1,128,2048]{2,1,0:T(8,128)(2,1)} %param.18) | copy-start | bytes 1572868
  251.5 101.4 %copy-start.31 = (f32[128]{0:T(128)}, f32[128]{0:T(128)S(1)}, u32[]{:S(2)}) copy-start(f32[128]{0:T(128)S(1)} %add_rsqrt_fusion.3) | copy-start | bytes 1540
  347.7 4.8 copy-start.11
  347.7 4.8 copy-start.14
  347.7 5.2 copy-start.17
  352.9 65.4 %copy-start.33 = (f32[128]{0:T(128)}, f32[128]{0:T(128)S(1)}, u32[]{:S(2)}) copy-start(f32[128]{0:T(128)S(1)} %broadcast_multiply_fusion.7) | copy-start | bytes 1540
  354.1 64.3 %copy-start.27 = (bf16[1024,256]{1,0:T(8,128)(2,1)S(1)}, bf16[1024,256]{1,0:T(8,128)(2,1)}, u32[]{:S(2)}) copy-start(bf16[1024,256]{1,0:T(8,128)(2,1)} %get-tuple-element.147.refs_0_) | copy-start | bytes 1572868
  418.3 4.6 copy-start.24
  418.3 4.6 copy-start.36
  418.3 4.6 copy-start.39
  426.7 13.3 %copy-start.40 = (bf16[1024,256]{1,0:T(8,128)(2,1)}, bf16[1024,256]{1,0:T(8,128)(2,1)S(1)}, u32[]{:S(2)}) copy-start(bf16[1024,256]{1,0:T(8,128)(2,1)S(1)} %get-tuple-element.134) | copy-start | bytes 1572868
  436.3 4.6 copy-start.5
  436.3 4.6 copy-start.9
  482.8 5.5 copy-start.29
  482.8 139.9 %reduce-scatter.3.cloned.1.call-start = ((), (), s32[]{:S(2)}) async-start(), calls=%async_computation.2 | async-start | bytes 2359296 | tf_op jit(solution)/shard_map/reduce_scatter | solution.py:1646
  488.2 10.7 %copy-start.19 = (bf16[1024,2048]{1,0:T(8,128)(2,1)S(1)}, bf16[1024,2048]{1,0:T(8,128)(2,1)}, u32[]{:S(2)}) copy-start(bf16[1024,2048]{1,0:T(8,128)(2,1)} %copy-done.18) | copy-start | bytes 12582916
  575.8 38.4 %copy-start.2 = (bf16[8,64,1408]{2,1,0:T(8,128)(2,1)S(1)}, bf16[8,64,1408]{2,1,0:T(8,128)(2,1)}, u32[]{:S(2)}) copy-start(bf16[8,64,1408]{2,1,0:T(8,128)(2,1)} %get-tuple-element.103.source) | copy-start | bytes 4325380
  614.3 6.8 %copy-start.20 = (bf16[4,176,2048]{2,1,0:T(8,128)(2,1)S(1)}, bf16[4,176,2048]{2,1,0:T(8,128)(2,1)}, u32[]{:S(2)}) copy-start(bf16[4,176,2048]{2,1,0:T(8,128)(2,1)} %get-tuple-element.104) | copy-start | bytes 8650756
  616.8 6.0 copy-start.12
  616.8 6.0 copy-start.15
  616.8 6.0 copy-start.32
  616.8 6.0 copy-start.34
  616.8 6.0 copy-start.35
  (13 other events, 21.4 us)
Sparse Core Ops, SparseCore 0:
  99.5 28.8 all-gather.4
  169.4 30.4 all-gather.6
  482.9 29.7 reduce-scatter.4
  514.9 47.6 reduce-scatter.2

commit v6 on v5

--- a/solution.py
+++ b/solution.py
@@ -806,26 +806,49 @@
 def columns_out(wires, source, out):
     mine, me, count, packs = lax.axis_index("dp"), lax.axis_index("seq"), lax.axis_size("seq"), lax.axis_size("dp")
     own = wires.keep(source.at[me], out.at[mine, me])
-    sent, onward = [], []
+    square = packs == 4
+    bit = lax.rem(mine, 2)
+    flip = {1: mine + 1 - 2 * bit, 2: lax.rem(mine + 2, 4)}
+    sent, onward, turned_on = [], {}, []
     for step in range(1, count):
         sent.append(wires.copy(source.at[lax.rem(me + step, count)], out.at[mine, me], seq_peer(step)))
         sent[-1].start()
-    for step in range(1, packs):
-        onward.append(wires.copy(source.at[me], out.at[mine, me], pack_peer(step)))
-        onward[-1].start()
+
+    def pass_on(k):
+        slot = lax.rem(me + count - k, count)
+        came = source.at[me] if k == 0 else out.at[mine, slot]
+        for way in (1, 2) if square else range(1, packs):
+            device = {"dp": flip[way]} if square else pack_peer(way)
+            onward[k, way] = wires.copy(came, out.at[mine, slot], device)
+            onward[k, way].start()
+
+    def turn(k):
+        way = 1 + k % 2
+        onward[k, way].wait_recv()
+        came = out.at[flip[way], lax.rem(me + count - k, count)]
+        turned_on.append(wires.copy(came, came, {"dp": flip[3 - way]}))
+        turned_on[-1].start()
+
+    pass_on(0)
     own.start()
-    for step in range(1, count):
+    for k in range(1, count):
         yield True
-        sent[step - 1].wait_recv()
-        came = out.at[mine, lax.rem(me + count - step, count)]
-        for other in range(1, packs):
-            onward.append(wires.copy(came, came, pack_peer(other)))
-            onward[-1].start()
+        sent[k - 1].wait_recv()
+        pass_on(k)
+        if square:
+            turn(k - 1)
     yield True
+    if square:
+        turn(count - 1)
+    yield PATIENT
     own.wait()
     for copy in sent:
         copy.wait_send()
-    for copy in onward:
+    for (k, way), copy in onward.items():
+        copy.wait_send()
+        if not square or way != 1 + k % 2:
+            copy.wait_recv()
+    for copy in turned_on:
         copy.wait()
 
 
@@ -1075,8 +1098,8 @@
 
 def feed_forward_kernel(
     cut, block_ref, top_first, top_second, wgu_hbm, wd_hbm,
-    x_out, down_out, g_gu_out, g_down_out, mid_out,
-    wgu_ref, wd_ref, xbuf, topbuf, hidbuf, dgubuf, downbuf, g_gu, g_down, g_gu_low, g_down_low,
+    down_out, g_gu_out, g_down_out, mid_out,
+    wgu_ref, wd_ref, x_out, tops, hidbuf, dgubuf, downbuf, g_gu, g_down, g_gu_low, g_down_low,
     terms, near, from_left, from_right, outbox,
     local_sems, pack_send, pack_recv, line_send, line_recv, near_send, near_recv, sum_send, sum_recv, across_send, across_recv,
 ):
@@ -1139,7 +1162,7 @@
             sum_send.at[at], sum_recv.at[at], on_line(2 if right else -2), MESH,
         )
 
-    own = Kept(block_ref, x_out.at[me], xbuf.at[0], local_sems.at[0])
+    own = pltpu.make_async_copy(block_ref, x_out.at[me], local_sems.at[0])
     for part in range(cut):
         for sign in (1, -1):
 
@@ -1148,7 +1171,10 @@
                 along(sign, 0, part, block_ref).start()
 
         over(1, 0, part, block_ref).start()
+    half = tall // 2
     weights = [
+        pltpu.make_async_copy(top_first, tops.at[:, pl.ds(0, half)], local_sems.at[3]),
+        pltpu.make_async_copy(top_second, tops.at[:, pl.ds(half, half)], local_sems.at[4]),
         pltpu.make_async_copy(wgu_hbm, wgu_ref, local_sems.at[1]),
         pltpu.make_async_copy(wd_hbm, wd_ref, local_sems.at[2]),
     ]
@@ -1160,8 +1186,8 @@
         copy.wait()
 
     def compute(dest):
-        x = xbuf[...].reshape(2 * tall, width)
-        top = topbuf[...].reshape(2 * tall, width)
+        x = x_out[pl.ds(2 * dest, 2)].reshape(2 * tall, width)
+        top = tops[pl.ds(2 * dest, 2)].reshape(2 * tall, width)
         for at, n in unit_groups(units):
             both = nn(x, wgu_ref[:, 2 * at : 2 * at + 2 * n])
             gate, up = both[:, :n], both[:, n:]
@@ -1181,9 +1207,9 @@
         for part in range(cut):
             across(dest, part).start()
 
-    def compute_rest():
-        x = xbuf[...].reshape(2 * tall, width)
-        top = topbuf[...].reshape(2 * tall, width)
+    def compute_rest(dest):
+        x = x_out[pl.ds(2 * dest, 2)].reshape(2 * tall, width)
+        top = tops[pl.ds(2 * dest, 2)].reshape(2 * tall, width)
         hid = hidbuf[...].reshape(2 * tall, units)
         dgu = dgubuf[...].reshape(2 * tall, 2 * units)
         wide = 512
@@ -1218,6 +1244,9 @@
         there = (from_left if right else from_right).at[dest, lines(part)]
         pltpu.make_async_remote_copy(there, there, sum_send.at[at], sum_recv.at[at], sibling(), MESH).wait_recv()
 
+    def saved(dest):
+        return pltpu.make_async_copy(downbuf, down_out.at[pl.ds(2 * dest, 2)], local_sems.at[2])
+
     def inside(dest):
         return (dest >= 0) & (dest < chips)
 
@@ -1227,22 +1256,8 @@
 
         @pl.when(inside(dest) & (i + 1 - j > 0))
         def _():
-            half = tall // 2
-            tops = [
-                pltpu.make_async_copy(
-                    ref.at[pl.ds(2 * dest, 2)], topbuf.at[:, pl.ds(at, half)], local_sems.at[1 + at // half]
-                )
-                for ref, at in ((top_first, 0), (top_second, half))
-            ]
-            for top in tops:
-                top.start()
             for part in range(cut):
                 over_came(sign, i, part)
-            x = pltpu.make_async_copy(x_out.at[pl.ds(2 * dest, 2)], xbuf, local_sems.at[0])
-            x.start()
-            for top in tops:
-                top.wait()
-            x.wait()
             compute(dest)
             @pl.when((chip == 0) & (dest > 0) & (dest < chips - 1))
             def _():
@@ -1254,10 +1269,12 @@
                 for part in range(cut):
                     send_sum(False, dest, part, True, False)
 
-            compute_rest()
-            saved = pltpu.make_async_copy(downbuf, down_out.at[pl.ds(2 * dest, 2)], local_sems.at[2])
-            saved.start()
-            saved.wait()
+            @pl.when(i + j > 0)
+            def _():
+                saved(dest).wait()
+
+            compute_rest(dest)
+            saved(dest).start()
 
     def forward(i):
         for sign in (1, -1):
@@ -1289,6 +1306,7 @@
     g_gu[...] = jnp.zeros_like(g_gu)
     g_down[...] = jnp.zeros_like(g_down)
     lax.fori_loop(0, chips, distance, 0)
+    saved(chip).wait()
 
     def lower(i, _):
         lines = pl.ds(pl.multiple_of(i * 16, 16), 16)
@@ -1366,18 +1384,38 @@
             sum_came(False, chip, part)
             add_into(mid_out.at[lines(part)], mine + [left_in, right_in])
 
-    def lower_gu(i, _):
-        lines = pl.ds(pl.multiple_of(i * 16, 16), 16)
-        g_gu_low[lines, :] = g_gu[lines, :].astype(jnp.bfloat16)
+    chunk = g_gu_low.shape[1]
+
+    def gu_copy(at):
+        slot = lax.rem(at, 2)
+        return pltpu.make_async_copy(
+            g_gu_low.at[slot], g_gu_out.at[pl.ds(at * chunk, chunk)], local_sems.at[3 + slot]
+        )
+
+    def lower_gu(at, _):
+        @pl.when(at > 1)
+        def _():
+            gu_copy(at - 2).wait()
+
+        slot = lax.rem(at, 2)
+
+        def some(i, _):
+            there = pl.ds(pl.multiple_of(i * 16, 16), 16)
+            came = pl.ds(pl.multiple_of(at * chunk + i * 16, 16), 16)
+            g_gu_low[slot, there, :] = g_gu[came, :].astype(jnp.bfloat16)
+            return 0
+
+        lax.fori_loop(0, chunk // 16, some, 0)
+        gu_copy(at).start()
         return 0
 
-    lax.fori_loop(0, width // 16, lower_gu, 0)
-    gu_kept = pltpu.make_async_copy(g_gu_low, g_gu_out, local_sems.at[1])
-    gu_kept.start()
+    chunks = width // chunk
+    lax.fori_loop(0, chunks, lower_gu, 0)
+    for at in range(max(chunks - 2, 0), chunks):
+        gu_copy(at).wait()
     for turn in range(1, packs):
         swap(turn).wait()
     kept.wait()
-    gu_kept.wait()
     for part in range(cut):
         for dest in range(chips):
             across(dest, part).wait_send()
@@ -1416,7 +1454,6 @@
     packs = lax.axis_size("dp")
     bf16 = jnp.bfloat16
     outs = [
-        shape_of((count, tall, width), bf16),
         shape_of((count, tall, width), bf16),
         shape_of((width, 2 * units), bf16),
         shape_of((packs, units // packs, width), bf16),
@@ -1430,22 +1467,22 @@
         functools.partial(feed_forward_kernel, cut),
         out_shape=outs,
         in_specs=[anywhere] * 5,
-        out_specs=[anywhere] * 4 + [vmem],
+        out_specs=[anywhere] * 3 + [vmem],
         scratch_shapes=[
             pltpu.VMEM(w_gu.shape, bf16),
             pltpu.VMEM(w_d.shape, bf16),
-            pltpu.VMEM((2, tall, width), bf16),
-            pltpu.VMEM((2, tall, width), bf16),
+            pltpu.VMEM((count, tall, width), bf16),
+            pltpu.VMEM((count, tall, width), bf16),
             pltpu.VMEM((2, tall, units), bf16),
             pltpu.VMEM((2, tall, 2 * units), bf16),
             pltpu.VMEM((2, tall, width), bf16),
             pltpu.VMEM((width, 2 * units), jnp.float32),
             pltpu.VMEM((units, width), jnp.float32),
-            pltpu.VMEM((width, 2 * units), bf16),
+            pltpu.VMEM((2, 256, 2 * units), bf16),
             pltpu.VMEM((units, width), bf16),
             pltpu.VMEM((count, tall, width), bf16),
             box, box, box, box,
-            dma(3), dma(packs), dma(packs),
+            dma(5), dma(packs), dma(packs),
         ] + [dma(2 * chips * cut)] * 6 + [dma(chips * cut)] * 2,
         compiler_params=pltpu.CompilerParams(
             collective_id=cid, has_side_effects=True, vmem_limit_bytes=62 * 1024 * 1024
@@ -1629,7 +1666,7 @@
     residual = inputs + branch
     scale_two = lax.rsqrt(jnp.mean(residual * residual, -1, keepdims=True) + EPSILON)
     normed_mid = residual * scale_two
-    _, down, g_gate_up, g_down, d_xtwo = feed_forward(
+    down, g_gate_up, g_down, d_xtwo = feed_forward(
         5, (normed_mid * gain_two).astype(bf16), (top_first, top_second), w_gu, w_d
     )
     down = down.reshape(-1, width)

time: 643 us -> 633 us (0.984)
  Pallas kernels: 500 us -> 490 us
where the time goes in v6:
time: 633 us; the launch traced here: 623 us
  Pallas kernels  490 us (77%)
  matrix products  47.7 us (8%)
  other arithmetic  35.6 us (6%)
  local copies, waits for them, and re-layouts  33.9 us (5%)
  between operations  14.9 us (2%)
    pallas_call x7, Pallas kernels, talk(): pl.pallas_call(kernel, out_shape=outs, in_specs=[where(i, in_vmem) for i...  311 us
    pallas_call x1, Pallas kernels, feed_forward(): pl.pallas_call(functools.partial(feed_forward_kernel, cut), out_shape=out...  89.1 us
    pallas_call x1, Pallas kernels, inner_forward(): pl.pallas_call(functools.partial(forward_kernel, heads, per, len(seq_arra...  42.3 us
    pallas_call x1, Pallas kernels, inner_backward(): pl.pallas_call(functools.partial(backward_kernel, heads, per, len(seq_arr...  41.8 us
    dot_general x3, matrix products, dot(): return jnp.dot(left_side, right_side, preferred_element_type=jnp.float32)  17.3 us
    dot_general x4, matrix products, cross_rows(): lax.dot_general(left_side, right_side, (((0,), (0,)), ((), ())), preferre...  15.9 us
    dot_general x2, matrix products, cross_cols(): lax.dot_general(left_side, right_side, (((1,), (1,)), ((), ())), preferre...  14.6 us
  transfers between devices with their start and end apart: 4, of which 0 were waited for; matrix products, arithmetic and copies ran while one was open for 12% of the time, Pallas kernels for 34%

profile of v6, /device:TPU:9, one launch (start us, length us, event | category | flops | bytes accessed | tf_op | source)
XLA Modules:
  0.0 623.0 jit_solution(12741524504653143882)
XLA Ops:
  7.2 1.9 slice_bitcast_fusion.2
  20.3 74.8 %first_exchange.1 = (bf16[4,8,64,1152]{3,2,1,0:T(8,128)(2,1)}, bf16[8,128,2048]{2,1,0:T(8,128)(2,1)}, bf16[4,64,2048]{2,1,0:T(8,128)(2,1)}, bf16[4,64,128]{2,1,0:T(8,128)(2,1)}) custom-call(bf16[8,64,1152]{2,1,0:T(8,128)(2,1)} %copy-done.1, bf16[128,2048]{1,0:T(8,128)(2,1)} %bitcast.151, bf16[64,2048]{1,0:T(8,128)(2,1)} %refs_2_.1, ...), custom_call_target="tpu_custom_call" | custom-call | tf_op jit(solution)/shard_map/first_exchange/pallas_call | solution.py:743
  95.2 2.7 slice_convert_fusion
  101.3 3.3 fusion.2
  104.7 3.7 broadcast_multiply_fusion
  113.6 8.3 %fusion.3.qkv_ref = f32[1024,768]{1,0:T(8,128)} fusion(bf16[1024,2048]{1,0:T(8,128)(2,1)} %copy-done.18, bf16[2048,1152]{1,0:T(8,128)(2,1)} %bitcast.170), kind=kOutput, calls=%fused_computation.8 | convolution fusion | flops 3221225472 | bytes 10485760 | tf_op jit(solution)/shard_map/dot_general | solution.py:1505
  121.9 42.3 %inner_forward.1 = (f32[1024,256]{1,0:T(8,128)S(1)}, bf16[64,64,256]{2,1,0:T(8,128)(2,1)}, f32[64,64,64]{2,1,0:T(8,128)}, f32[64,64,64]{2,1,0:T(8,128)}, f32[64,...) custom-call(s32[64]{0:T(128)S(1)} %add_convert_fusion.1.fresh_ref, ...), custom_call_target="tpu_custom_call" | custom-call | tf_op jit(solution)/shard_map/inner_forward/pallas_call | solution.py:137
  167.5 6.4 %share_moments.1 = f32[8,2,1024]{2,1,0:T(2,128)} custom-call(f32[2,1024]{1,0:T(2,128)} %pad_maximum_fusion.1.refs_0_), custom_call_target="tpu_custom_call" | custom-call | tf_op jit(solution)/shard_map/share_moments/pallas_call | solution.py:743
  173.8 1.6 copy.242
  176.6 5.3 multiply_convert_fusion.1
  181.8 65.5 %scatter_branch.1 = (f32[128,2048]{1,0:T(8,128)}, bf16[4,512,1408]{2,1,0:T(8,128)(2,1)}) custom-call(bf16[1024,256]{1,0:T(8,128)(2,1)} %get-tuple-element.147.refs_0_, bf16[256,2048]{1,0:T(8,128)(2,1)} %bitcast.160, bf16[512,1408]{1,0:T(8,128)(2,1)} %bitcast.144), custom_call_target="tpu_custom_call" | custom-call | tf_op jit(solution)/shard_map/scatter_branch/pallas_call | solution.py:743
  250.8 89.1 %feed_forward.1 = (bf16[8,128,2048]{2,1,0:T(8,128)(2,1)}, bf16[2048,1408]{1,0:T(8,128)(2,1)}, bf16[4,176,2048]{2,1,0:T(8,128)(2,1)}, f32[128,2048]{1,0:T(8,128)}) custom-call(bf16[128,2048]{1,0:T(8,128)(2,1)} %multiply_convert_fusion.block_ref, bf16[8,64,2048]{2,1,0:T(8,128)(2,1)} %bitcast.221, bf16[8,64,2048]{2,1,0:T(8,128)(2,1)} %bitcast.222, ...), custom_call_target="tpu_custom_call" | custom-call | flops 17716740096 | bytes 20971520 | tf_op jit(solution)/shard_map/feed_forward/pallas_call | solution.py:1466
  339.9 4.8 fusion.49
  346.2 62.0 %gather_branch.1 = (bf16[8,128,2048]{2,1,0:T(8,128)(2,1)}, bf16[512,1408]{1,0:T(8,128)(2,1)}) custom-call(bf16[128,2048]{1,0:T(8,128)(2,1)} %fusion.46.refs_0_, bf16[4,512,1408]{2,1,0:T(8,128)(2,1)} %bitcast.152), custom_call_target="tpu_custom_call" | custom-call | tf_op jit(solution)/shard_map/gather_branch/pallas_call | solution.py:743
  408.3 4.6 convolution_convert_fusion.1
  412.9 3.7 multiply_reduce_fusion.2
  417.3 8.1 %share_sums.1 = f32[8,2,1024]{2,1,0:T(2,128)} custom-call(f32[2,1024]{1,0:T(2,128)} %pad_maximum_fusion.2.refs_0_), custom_call_target="tpu_custom_call" | custom-call | tf_op jit(solution)/shard_map/share_sums/pallas_call | solution.py:743
  426.4 3.7 convolution_convert_fusion.2
  431.0 41.8 %inner_backward.1 = (bf16[1024,768]{1,0:T(8,128)(2,1)}, f32[64,1,64]{2,1,0:T(1,128)S(1)}, f32[64,256]{1,0:T(8,128)S(1)}, f32[64,64]{1,0:T(8,128)S(1)}, f32[64,64...) custom-call(s32[64]{0:T(128)S(1)} %add_convert_fusion.1.fresh_ref, ...), custom_call_target="tpu_custom_call" | custom-call | tf_op jit(solution)/shard_map/inner_backward/pallas_call | solution.py:265
  478.3 10.9 %multiply_reduce_fusion = (f32[2048]{0:T(1024)S(1)}, bf16[1024,2048]{1,0:T(8,128)(2,1)}) fusion(bf16[1024,2048]{1,0:T(8,128)(2,1)} %bitcast.149, f32[1024]{0:T(1024)S(1)} %copy-done.29, bf16[2048,1152]{1,0:T(8,128)(2,1)} %bitcast.172, bf16[1024,128]{1,0:T(8,128)(2,1)} %pad.13, bf16[1024,256]{1,0:T(8,128)(2,1)} %copy-done.40, ...), kind=kOutput, calls=%fused_computation.5 | convolution fusion | flops 4849399808 | bytes 15478784 | tf_op jit(solution)/shard_map/dot_general | solution.py:1501
  489.2 2.6 fusion.7
  491.8 5.0 convolution_convert_fusion
  496.8 64.5 %scatter_first.1 = (f32[128,2048]{1,0:T(8,128)}, f32[4,64,128]{2,1,0:T(8,128)}, bf16[4,512,128]{2,1,0:T(8,128)(2,1)}, bf16[4,512,768]{2,1,0:T(8,128)(2,1)}) custom-call(bf16[8,128,2048]{2,1,0:T(8,128)(2,1)} %bitcast.153, f32[4,64,128]{2,1,0:T(8,128)} %concatenate.53.refs_1_, bf16[4,512,128]{2,1,0:T(8,128)(2,1)} %bitcast.179, bf16[4,512,768]{2,1,0:T(8,128)(2,1)} %bitcast.155), custom_call_target="tpu_custom_call" | custom-call | tf_op jit(solution)/shard_map/scatter_first/pallas_call | solution.py:743
  561.3 1.8 reduce.5
  563.4 2.8 reduce.3
  566.2 2.2 pad_maximum_fusion.refs_0_
  568.4 29.2 %return_columns.1.source = bf16[8,64,1152]{2,1,0:T(8,128)(2,1)} custom-call(bf16[8,64,1152]{2,1,0:T(8,128)(2,1)} %pad_maximum_fusion.refs_0_), custom_call_target="tpu_custom_call" | custom-call | tf_op jit(solution)/shard_map/return_columns/pallas_call | solution.py:743
  598.8 2.1 join_columns.2
  604.6 2.5 join_columns.3
  609.7 1.7 fusion.20
  611.4 1.6 convert_reduce_fusion
  613.1 3.1 fusion.36
  (207 shorter events, 44.7 us)
Async XLA Ops:
  7.2 12.4 %copy-start.30 = (bf16[64,64]{1,0:T(8,128)(2,1)S(1)}, bf16[64,64]{1,0:T(8,128)(2,1)}, u32[]{:S(2)}) copy-start(bf16[64,64]{1,0:T(8,128)(2,1)} %param.26) | copy-start | bytes 24580
  7.2 243.6 %all-gather.5.cloned.1.call-start = ((), (), s32[]{:S(2)}) async-start(), calls=%async_computation.4 | async-start | bytes 2359296 | tf_op jit(solution)/shard_map/all_gather | solution.py:1613
  95.2 155.6 %all-gather.7.cloned.1.call-start = ((), (), s32[]{:S(2)}) async-start(), calls=%async_computation.5 | async-start | bytes 2359296 | tf_op jit(solution)/shard_map/all_gather | solution.py:1640
  95.2 3.8 copy-start.13
  95.2 4.7 copy-start.38
  104.6 3.7 copy-start.18
  104.7 4.1 copy-start.26
  104.7 5.5 copy-start.4
  165.9 447.1 %reduce-scatter.5.cloned.1.call-start = ((), (), s32[]{:S(2)}) async-start(), calls=%async_computation.3 | async-start | bytes 2359296 | tf_op jit(solution)/shard_map/reduce_scatter | solution.py:1706
  176.6 70.7 %copy-start.16 = (bf16[1,128,2048]{2,1,0:T(8,128)(2,1)S(1)}, bf16[1,128,2048]{2,1,0:T(8,128)(2,1)}, u32[]{:S(2)}) copy-start(bf16[1,128,2048]{2,1,0:T(8,128)(2,1)} %param.18) | copy-start | bytes 1572868
  248.8 96.2 %copy-start.31 = (f32[128]{0:T(128)}, f32[128]{0:T(128)S(1)}, u32[]{:S(2)}) copy-start(f32[128]{0:T(128)S(1)} %add_rsqrt_fusion.3) | copy-start | bytes 1540
  339.8 4.8 copy-start.11
  339.9 4.8 copy-start.14
  339.9 5.2 copy-start.17
  345.1 63.2 %copy-start.33 = (f32[128]{0:T(128)}, f32[128]{0:T(128)S(1)}, u32[]{:S(2)}) copy-start(f32[128]{0:T(128)S(1)} %broadcast_multiply_fusion.7) | copy-start | bytes 1540
  346.2 62.1 %copy-start.27 = (bf16[1024,256]{1,0:T(8,128)(2,1)S(1)}, bf16[1024,256]{1,0:T(8,128)(2,1)}, u32[]{:S(2)}) copy-start(bf16[1024,256]{1,0:T(8,128)(2,1)} %get-tuple-element.147.refs_0_) | copy-start | bytes 1572868
  408.3 4.6 copy-start.24
  408.3 4.6 copy-start.36
  408.3 4.6 copy-start.39
  416.7 13.4 %copy-start.40 = (bf16[1024,256]{1,0:T(8,128)(2,1)}, bf16[1024,256]{1,0:T(8,128)(2,1)S(1)}, u32[]{:S(2)}) copy-start(bf16[1024,256]{1,0:T(8,128)(2,1)S(1)} %get-tuple-element.134) | copy-start | bytes 1572868
  426.4 4.6 copy-start.5
  426.4 4.6 copy-start.9
  472.9 5.5 copy-start.29
  472.9 140.2 %reduce-scatter.3.cloned.1.call-start = ((), (), s32[]{:S(2)}) async-start(), calls=%async_computation.2 | async-start | bytes 2359296 | tf_op jit(solution)/shard_map/reduce_scatter | solution.py:1683
  478.3 10.9 %copy-start.19 = (bf16[1024,2048]{1,0:T(8,128)(2,1)S(1)}, bf16[1024,2048]{1,0:T(8,128)(2,1)}, u32[]{:S(2)}) copy-start(bf16[1024,2048]{1,0:T(8,128)(2,1)} %copy-done.18) | copy-start | bytes 12582916
  566.2 38.4 %copy-start.2 = (bf16[8,64,1408]{2,1,0:T(8,128)(2,1)S(1)}, bf16[8,64,1408]{2,1,0:T(8,128)(2,1)}, u32[]{:S(2)}) copy-start(bf16[8,64,1408]{2,1,0:T(8,128)(2,1)} %get-tuple-element.103.source) | copy-start | bytes 4325380
  604.6 6.8 %copy-start.20 = (bf16[4,176,2048]{2,1,0:T(8,128)(2,1)S(1)}, bf16[4,176,2048]{2,1,0:T(8,128)(2,1)}, u32[]{:S(2)}) copy-start(bf16[4,176,2048]{2,1,0:T(8,128)(2,1)} %get-tuple-element.104) | copy-start | bytes 8650756
  607.1 6.0 copy-start.12
  607.1 6.0 copy-start.15
  607.1 6.0 copy-start.32
  607.1 6.0 copy-start.34
  607.1 6.0 copy-start.35
  (13 other events, 21.4 us)
Sparse Core Ops, SparseCore 0:
  95.3 29.5 all-gather.4
  166.0 30.9 all-gather.6
  473.0 30.4 reduce-scatter.4
  505.7 47.1 reduce-scatter.2

commit v7 on v6

--- a/solution.py
+++ b/solution.py
@@ -69,12 +69,14 @@
 def forward_kernel(heads, per, over_seq, over_dp, fresh_ref, qkv_ref, e_ref, w0_ref, c0_ref, gain_ref, shift_ref, *refs):
     moved = over_seq + over_dp
     sources, refs = refs[:moved], refs[moved:]
+    near_out, refs = refs[7 + moved], refs[: 7 + moved] + refs[8 + moved :]
     mixed_ref, wsave_ref, hat_ref, slope_ref, gap_ref, bar_ref, rows_ref = refs[:7]
     results, (w_ref, c_ref, send_sems, recv_sems, *rooms) = refs[7 : 7 + moved], refs[7 + moved :]
     jobs = [swap_seq] * over_seq + [spread_dp] * over_dp
     beside(
-        ("seq", "dp"), send_sems, recv_sems, rooms,
-        lambda wires: [job(wires, a, b) for job, a, b in zip(jobs, sources, results)],
+        ("seq", "dp", "cross"), send_sems, recv_sems, rooms,
+        lambda wires: [job(wires, a, b) for job, a, b in zip(jobs, sources, results)]
+        + [near_pieces(wires, sources[0], near_out)],
     )
     hi = heads * HD
     own, unit, same, later, _ = head_masks(heads)
@@ -148,15 +150,16 @@
             pl.BlockSpec((per, HD, hi), lambda i: (i, 0, 0)),
             save, save, save, save,
             pl.BlockSpec((per, 4, ht), lambda i: (i, 0, 0)),
-        ] + [pl.BlockSpec(memory_space=pl.ANY)] * len(arrays),
+        ] + [pl.BlockSpec(memory_space=pl.ANY)] * (len(arrays) + 1),
         out_shape=[
             jax.ShapeDtypeStruct((tokens, hi), f32),
             jax.ShapeDtypeStruct((blocks, HD, hi), jnp.bfloat16),
         ] + [jax.ShapeDtypeStruct((blocks, HD, ht), f32)] * 4 + [jax.ShapeDtypeStruct((blocks, 4, ht), f32)]
         + [shape_of(a.shape, a.dtype) for a in seq_arrays]
-        + [shape_of((packs,) + a.shape, a.dtype) for a in dp_arrays],
+        + [shape_of((packs,) + a.shape, a.dtype) for a in dp_arrays]
+        + [shape_of((packs,) + arrays[0].shape, arrays[0].dtype)],
         scratch_shapes=[pltpu.VMEM((HD, hi), f32), pltpu.VMEM((HD, ht), f32)]
-        + wire_sems(len(seq_arrays) * lax.axis_size("seq") + len(dp_arrays) * packs)
+        + wire_sems(len(seq_arrays) * lax.axis_size("seq") + len(dp_arrays) * packs + 2 * packs)
         + [room(a.shape[1:], a.dtype) for a in seq_arrays] + [room(a.shape, a.dtype) for a in dp_arrays],
         compiler_params=pltpu.CompilerParams(
             vmem_limit_bytes=48 * 1024 * 1024, collective_id=cid, has_side_effects=True
@@ -374,6 +377,10 @@
         for step in range(1, lax.axis_size("dp")):
             greet(pack_peer(step))
         peers += lax.axis_size("dp") - 1
+    if "cross" in groups:
+        for step in range(1, lax.axis_size("dp")):
+            greet({**pack_peer(step), **sibling()})
+        peers += lax.axis_size("dp") - 1
     if "seq" in groups:
         for step in range(1, count):
             greet(seq_peer(step))
@@ -849,6 +856,62 @@
         if not square or way != 1 + k % 2:
             copy.wait_recv()
     for copy in turned_on:
+        copy.wait()
+
+
+def near_pieces(wires, source, out):
+    mine, me, packs = lax.axis_index("dp"), lax.axis_index("seq"), lax.axis_size("dp")
+    other = sibling()["seq"]
+    sent = []
+    for step in range(1, packs):
+        peer = pack_peer(step)
+        sent.append(wires.begin(wires.copy(source.at[me], out.at[mine, me], peer)))
+        sent.append(wires.begin(wires.copy(source.at[other], out.at[mine, me], {**peer, **sibling()})))
+    yield True
+    for copy in sent:
+        copy.wait()
+
+
+def far_pieces(wires, source, out, idle=1):
+    mine, me, count, packs = lax.axis_index("dp"), lax.axis_index("seq"), lax.axis_size("seq"), lax.axis_size("dp")
+    bit = lax.rem(mine, 2)
+    flip = {1: mine + 1 - 2 * bit, 2: lax.rem(mine + 2, 4)}
+    sent, turned = {}, []
+
+    def slot(j):
+        return lax.rem(me // 2 * 2 + 2 + j, count)
+
+    def send(j, way, device):
+        sent[j, way] = wires.copy(source.at[slot(j)], out.at[mine, slot(j)], device)
+        sent[j, way].start()
+
+    if packs != 4:
+        for j in range(count - 2):
+            for step in range(1, packs):
+                send(j, step, pack_peer(step))
+        yield PATIENT
+        for copy in sent.values():
+            copy.wait()
+        return
+    for j in range(count - 2):
+        send(j, 1 + j % 2, {"dp": flip[1 + j % 2]})
+    for _ in range(idle):
+        yield True
+    for j in range(count - 2):
+        way = 1 + j % 2
+        if j % 2 == 0:
+            yield True
+        sent[j, way].wait_recv()
+        came = out.at[flip[way], slot(j)]
+        turned.append(wires.copy(came, came, {"dp": flip[3 - way]}))
+        turned[-1].start()
+        send(j, 3 - way, {"dp": flip[3 - way]})
+    yield PATIENT
+    for (j, way), copy in sent.items():
+        copy.wait_send()
+        if way != 1 + j % 2:
+            copy.wait_recv()
+    for copy in turned:
         copy.wait()
 
 
@@ -962,9 +1025,9 @@
 
 
 class Beside:
-    def __init__(self, gathers=(), swaps=(), sums=()):
-        self.gathers, self.swaps, self.sums = list(gathers), list(swaps), list(sums)
-        self.arrays = self.gathers + self.swaps + self.sums
+    def __init__(self, gathers=(), swaps=(), sums=(), pieces=()):
+        self.gathers, self.swaps, self.sums, self.pieces = list(gathers), list(swaps), list(sums), list(pieces)
+        self.arrays = self.gathers + self.swaps + self.sums + self.pieces
         packs = lax.axis_size("dp")
         self.outs = [shape_of((packs,) + a.shape, a.dtype) for a in self.gathers]
         self.outs += [shape_of(a.shape, a.dtype) for a in self.swaps]
@@ -973,7 +1036,8 @@
             fold = can_fold(a)
             self.outs.append(shape_of(a.shape[1:] if fold else a.shape, a.dtype))
             self.scratch += fold_scratch(a) if fold else []
-        self.copies = HALVES * len(self.gathers) + packs * len(self.swaps) + 16 * len(self.sums)
+        self.outs += [shape_of((packs,) + a.shape, a.dtype) for a in self.pieces]
+        self.copies = len(self.pieces) * packs * lax.axis_size("seq") + HALVES * len(self.gathers) + packs * len(self.swaps) + 16 * len(self.sums)
         self.job_rooms = [room(a.shape, a.dtype) for a in self.gathers if can_halve(a)]
         self.patient_rooms = [room(a.shape, a.dtype) for a in self.gathers if not can_halve(a)]
         self.patient_rooms += [room(a.shape[1:], a.dtype) for a in self.swaps]
@@ -991,13 +1055,16 @@
                 scratch = scratch[3:]
             else:
                 patient.append(swap_dp(wires, a, b))
+        p = s + len(self.sums)
+        jobs += [far_pieces(wires, a, b) for a, b in zip(ins[p:], results[p:])]
         return jobs, patient
 
     def finish(self, got):
         g, s = len(self.gathers), len(self.gathers) + len(self.swaps)
         got = list(got)
         done = [r.reshape((-1,) + a.shape[1:]) for r, a in zip(got[:g], self.gathers)] + got[g:s]
-        return done + [r if can_fold(a) else add_packs(r).astype(r.dtype) for r, a in zip(got[s:], self.sums)]
+        done += [r if can_fold(a) else add_packs(r).astype(r.dtype) for r, a in zip(got[s:], self.sums)]
+        return done + got[s + len(self.sums) :]
 
 
 def scatter_with(name, cid, out_shape, factors, product, beside, cut=2):
@@ -1097,7 +1164,7 @@
 
 
 def feed_forward_kernel(
-    cut, block_ref, top_first, top_second, wgu_hbm, wd_hbm,
+    cut, block_ref, top_first, top_second, own_cols, near_cols, far_cols, wd_first, wd_second,
     down_out, g_gu_out, g_down_out, mid_out,
     wgu_ref, wd_ref, x_out, tops, hidbuf, dgubuf, downbuf, g_gu, g_down, g_gu_low, g_down_low,
     terms, near, from_left, from_right, outbox,
@@ -1175,13 +1242,35 @@
     weights = [
         pltpu.make_async_copy(top_first, tops.at[:, pl.ds(0, half)], local_sems.at[3]),
         pltpu.make_async_copy(top_second, tops.at[:, pl.ds(half, half)], local_sems.at[4]),
-        pltpu.make_async_copy(wgu_hbm, wgu_ref, local_sems.at[1]),
-        pltpu.make_async_copy(wd_hbm, wd_ref, local_sems.at[2]),
+        pltpu.make_async_copy(wd_first, wd_ref.at[:, pl.ds(0, width // 2)], local_sems.at[2]),
+        pltpu.make_async_copy(wd_second, wd_ref.at[:, pl.ds(width // 2, width // 2)], local_sems.at[5]),
     ]
     own.start()
     for copy in weights:
         copy.start()
+    deep = own_cols.shape[1]
+
+    def fetch(at, _):
+        from_pack, place = at // count, lax.rem(at, count)
+        there = wgu_ref.at[pl.ds(pl.multiple_of(at * deep, deep), deep)]
+
+        @pl.when(from_pack == pack)
+        def _():
+            pltpu.make_async_copy(own_cols.at[place], there, local_sems.at[1]).start()
+
+        @pl.when((from_pack != pack) & (place // 2 == chip))
+        def _():
+            pltpu.make_async_copy(near_cols.at[from_pack, place], there, local_sems.at[1]).start()
+
+        @pl.when((from_pack != pack) & (place // 2 != chip))
+        def _():
+            pltpu.make_async_copy(far_cols.at[from_pack, place], there, local_sems.at[1]).start()
+
+        return 0
+
+    lax.fori_loop(0, packs * count, fetch, 0)
     own.wait()
+    pltpu.make_async_copy(wgu_ref, wgu_ref, local_sems.at[1]).wait()
     for copy in weights:
         copy.wait()
 
@@ -1446,11 +1535,11 @@
                         over(sign, i, part).wait_send()
 
 
-def feed_forward(cid, block, tops, w_gu, w_d, cut=2):
+def feed_forward(cid, block, tops, columns, downs, cut=2):
     count = lax.axis_size("seq")
     chips = count // 2
     tall, width = block.shape
-    units = w_d.shape[0]
+    units = downs[0].shape[0]
     packs = lax.axis_size("dp")
     bf16 = jnp.bfloat16
     outs = [
@@ -1466,11 +1555,11 @@
     got = pl.pallas_call(
         functools.partial(feed_forward_kernel, cut),
         out_shape=outs,
-        in_specs=[anywhere] * 5,
+        in_specs=[anywhere] * 8,
         out_specs=[anywhere] * 3 + [vmem],
         scratch_shapes=[
-            pltpu.VMEM(w_gu.shape, bf16),
-            pltpu.VMEM(w_d.shape, bf16),
+            pltpu.VMEM((width, 2 * units), bf16),
+            pltpu.VMEM((units, width), bf16),
             pltpu.VMEM((count, tall, width), bf16),
             pltpu.VMEM((count, tall, width), bf16),
             pltpu.VMEM((2, tall, units), bf16),
@@ -1482,14 +1571,14 @@
             pltpu.VMEM((units, width), bf16),
             pltpu.VMEM((count, tall, width), bf16),
             box, box, box, box,
-            dma(5), dma(packs), dma(packs),
+            dma(6), dma(packs), dma(packs),
         ] + [dma(2 * chips * cut)] * 6 + [dma(chips * cut)] * 2,
         compiler_params=pltpu.CompilerParams(
             collective_id=cid, has_side_effects=True, vmem_limit_bytes=62 * 1024 * 1024
         ),
         cost_estimate=pl.CostEstimate(flops=flops, bytes_accessed=20 << 20, transcendentals=0),
         name="feed_forward",
-    )(block, *tops, w_gu, w_d)
+    )(block, *tops, *columns, *downs)
     return got
 
 
@@ -1591,9 +1680,11 @@
     vectors = jnp.stack([b_init, tnorm_w, tnorm_b, post_w, post_b], axis=1)
     head_rows = jnp.concatenate([w_init, vectors, jnp.zeros((rows, extra - HD - 5), bf16)], axis=1)
     over_dp = (w_out, head_rows) if aligned else ()
+    down_rows = jnp.pad(w_down, ((0, filled - units), (0, 0)))
     w_mix, rows_all, *got = first_exchange(
-        split_columns((w_qkv, w_gate, beside_cols), mix_cuts), tokens[0], over_dp
+        split_columns((w_qkv, w_gate, beside_cols), mix_cuts), tokens[0], over_dp + (down_rows[:, : width // 2],)
     )
+    *got, w_d_first = got
     if aligned:
         w_o, head_rows = got
     else:
@@ -1630,11 +1721,11 @@
     init_b = vec_own[:, 0].reshape(heads, HD)
     init_b = (init_b - jnp.mean(init_b, -1, keepdims=True)).reshape(-1)
     gain_t, shift_t = by_token(vec_own[:, 1]), by_token(vec_own[:, 2])
-    *results, gu_part, w_d = inner_forward(
+    *results, gu_part, w_d_second, gu_near = inner_forward(
         10, fresh, qkv, e_rows, init_w, by_token(init_b), gain_t, shift_t, (gu_mine,),
-        (jnp.pad(w_down, ((0, filled - units), (0, 0))),),
+        (down_rows[:, width // 2 :],),
     )
-    w_d = w_d.reshape(-1, w_d.shape[-1])
+    w_d_second = w_d_second.reshape(-1, width // 2)
     mixed, *saved = results
     later_top, mixed = lax.optimization_barrier((grad_out[0, half:], mixed))
     top_second = lax.all_gather(later_top, "seq", axis=0)
@@ -1658,16 +1749,16 @@
             part = nn(unit, factors[1][:, at : at + wide]).astype(bf16)
             terms[2 * dest : 2 * dest + 2, :, at : at + wide] = part.reshape(2, span, wide)
 
-    branch, w_gu = scatter_with(
+    branch, gu_far = scatter_with(
         "scatter_branch", 3, (span, width), (gated_unit, w_o), branch_terms,
-        Beside(gathers=(gu_part.reshape(-1, gu_part.shape[-1]),)),
+        Beside(pieces=(gu_part,)),
     )
     inputs = tokens[0].astype(floats)
     residual = inputs + branch
     scale_two = lax.rsqrt(jnp.mean(residual * residual, -1, keepdims=True) + EPSILON)
     normed_mid = residual * scale_two
     down, g_gate_up, g_down, d_xtwo = feed_forward(
-        5, (normed_mid * gain_two).astype(bf16), (top_first, top_second), w_gu, w_d
+        5, (normed_mid * gain_two).astype(bf16), (top_first, top_second), (gu_part, gu_near, gu_far), (w_d_first, w_d_second)
     )
     down = down.reshape(-1, width)
     pack_rows = lambda array: array.reshape((packs, -1) + array.shape[1:])

time: 633 us -> 614 us (0.970)
  Pallas kernels: 490 us -> 474 us
    pallas_call x7, Pallas kernels: 311 us -> 296 us  [talk(): pl.pallas_call(kernel, out_shape=outs, in_specs=[where(i, in_vmem) for i...]
  transfers between devices with their start and end apart: 4 -> 4, of which waited for: 0 -> 0; matrix products, arithmetic and copies ran while one was open for 12% -> 12% of each run, Pallas kernels for 34% -> 33%
where the time goes in v7:
time: 614 us; the launch traced here: 610 us
  Pallas kernels  474 us (77%)
  matrix products  49 us (8%)
  other arithmetic  35.5 us (6%)
  local copies, waits for them, and re-layouts  35.2 us (6%)
  between operations  14.8 us (2%)
    pallas_call x7, Pallas kernels, talk(): pl.pallas_call(kernel, out_shape=outs, in_specs=[where(i, in_vmem) for i...  296 us
    pallas_call x1, Pallas kernels, feed_forward(): pl.pallas_call(functools.partial(feed_forward_kernel, cut), out_shape=out...  87.1 us
    pallas_call x1, Pallas kernels, inner_forward(): pl.pallas_call(functools.partial(forward_kernel, heads, per, len(seq_arra...  42.4 us
    pallas_call x1, Pallas kernels, inner_backward(): pl.pallas_call(functools.partial(backward_kernel, heads, per, len(seq_arr...  42 us
    dot_general x3, matrix products, dot(): return jnp.dot(left_side, right_side, preferred_element_type=jnp.float32)  17.3 us
    dot_general x4, matrix products, cross_rows(): lax.dot_general(left_side, right_side, (((0,), (0,)), ((), ())), preferre...  16.1 us
    dot_general x2, matrix products, cross_cols(): lax.dot_general(left_side, right_side, (((1,), (1,)), ((), ())), preferre...  15.6 us
  transfers between devices with their start and end apart: 4, of which 0 were waited for; matrix products, arithmetic and copies ran while one was open for 12% of the time, Pallas kernels for 33%

profile of v7, /device:TPU:9, one launch (start us, length us, event | category | flops | bytes accessed | tf_op | source)
XLA Modules:
  0.0 609.9 jit_solution(9744990520021026377)
XLA Ops:
  7.2 1.9 slice_bitcast_fusion.2
  15.8 1.9 pad_slice_fusion
  22.2 76.0 %first_exchange.1 = (bf16[4,8,64,1152]{3,2,1,0:T(8,128)(2,1)}, bf16[8,128,2048]{2,1,0:T(8,128)(2,1)}, bf16[4,64,2048]{2,1,0:T(8,128)(2,1)}, bf16[4,64,128]{2,1,0:T(8,128)(2,1)}, bf16[4,176,1024]{2,1,0:T(8,128)(2,1)}) custom-call(bf16[8,64,1152]{2,1,0:T(8,128)(2,1)} %copy-done.1, bf16[128,2048]{1,0:T(8,128)(2,1)} %bitcast.150, bf16[64,2048]{1,0:T(8,128)(2,1)} %refs_2_.1, ...), custom_call_target="tpu_custom_call" | custom-call | tf_op jit(solution)/shard_map/first_exchange/pallas_call | solution.py:750
  98.6 2.7 slice_convert_fusion
  104.1 3.3 fusion.2
  107.4 3.7 broadcast_multiply_fusion
  115.7 8.4 %fusion.3.qkv_ref = f32[1024,768]{1,0:T(8,128)} fusion(bf16[1024,2048]{1,0:T(8,128)(2,1)} %copy-done.17, bf16[2048,1152]{1,0:T(8,128)(2,1)} %bitcast.169), kind=kOutput, calls=%fused_computation.8 | convolution fusion | flops 3221225472 | bytes 10485760 | tf_op jit(solution)/shard_map/dot_general | solution.py:1594
  124.1 42.4 %inner_forward.1 = (f32[1024,256]{1,0:T(8,128)S(1)}, bf16[64,64,256]{2,1,0:T(8,128)(2,1)}, f32[64,64,64]{2,1,0:T(8,128)}, f32[64,64,64]{2,1,0:T(8,128)}, f32[64,...) custom-call(s32[64]{0:T(128)S(1)} %add_convert_fusion.1.fresh_ref, ...), custom_call_target="tpu_custom_call" | custom-call | tf_op jit(solution)/shard_map/inner_forward/pallas_call | solution.py:139
  170.3 6.1 share_moments.1
  176.4 1.7 copy.242
  179.2 5.3 multiply_convert_fusion.1
  184.5 51.5 %scatter_branch.1 = (f32[128,2048]{1,0:T(8,128)}, bf16[4,8,64,1408]{3,2,1,0:T(8,128)(2,1)}) custom-call(bf16[1024,256]{1,0:T(8,128)(2,1)} %get-tuple-element.153.refs_0_, bf16[256,2048]{1,0:T(8,128)(2,1)} %bitcast.159, bf16[8,64,1408]{2,1,0:T(8,128)(2,1)} %copy-done.3), custom_call_target="tpu_custom_call" | custom-call | tf_op jit(solution)/shard_map/scatter_branch/pallas_call | solution.py:750
  239.5 87.1 %feed_forward.1 = (bf16[8,128,2048]{2,1,0:T(8,128)(2,1)}, bf16[2048,1408]{1,0:T(8,128)(2,1)}, bf16[4,176,2048]{2,1,0:T(8,128)(2,1)}, f32[128,2048]{1,0:T(8,128)}) custom-call(bf16[128,2048]{1,0:T(8,128)(2,1)} %multiply_convert_fusion.block_ref, bf16[8,64,2048]{2,1,0:T(8,128)(2,1)} %bitcast.218, bf16[8,64,2048]{2,1,0:T(8,128)(2,1)} %bitcast.219, ...), custom_call_target="tpu_custom_call" | custom-call | flops 17716740096 | bytes 20971520 | tf_op jit(solution)/shard_map/feed_forward/pallas_call | solution.py:1555
  326.7 4.9 fusion.49
  333.1 59.5 %gather_branch.1 = (bf16[8,128,2048]{2,1,0:T(8,128)(2,1)}, bf16[512,1408]{1,0:T(8,128)(2,1)}) custom-call(bf16[128,2048]{1,0:T(8,128)(2,1)} %fusion.46.refs_0_, bf16[4,512,1408]{2,1,0:T(8,128)(2,1)} %bitcast.151), custom_call_target="tpu_custom_call" | custom-call | tf_op jit(solution)/shard_map/gather_branch/pallas_call | solution.py:750
  392.6 4.7 convolution_convert_fusion.1
  397.3 4.8 multiply_reduce_fusion.2
  402.7 9.6 %share_sums.1 = f32[8,2,1024]{2,1,0:T(2,128)} custom-call(f32[2,1024]{1,0:T(2,128)} %pad_maximum_fusion.2.refs_0_), custom_call_target="tpu_custom_call" | custom-call | tf_op jit(solution)/shard_map/share_sums/pallas_call | solution.py:750
  413.2 3.8 convolution_convert_fusion.2
  417.9 42.0 %inner_backward.1 = (bf16[1024,768]{1,0:T(8,128)(2,1)}, f32[64,1,64]{2,1,0:T(1,128)S(1)}, f32[64,256]{1,0:T(8,128)S(1)}, f32[64,64]{1,0:T(8,128)S(1)}, f32[64,64...) custom-call(s32[64]{0:T(128)S(1)} %add_convert_fusion.1.fresh_ref, ...), custom_call_target="tpu_custom_call" | custom-call | tf_op jit(solution)/shard_map/inner_backward/pallas_call | solution.py:268
  465.4 10.8 %multiply_reduce_fusion = (f32[2048]{0:T(1024)S(1)}, bf16[1024,2048]{1,0:T(8,128)(2,1)}) fusion(bf16[1024,2048]{1,0:T(8,128)(2,1)} %bitcast.148, f32[1024]{0:T(1024)S(1)} %add_rsqrt_fusion.1, bf16[2048,1152]{1,0:T(8,128)(2,1)} %bitcast.171, bf16[1024,128]{1,0:T(8,128)(2,1)} %pad.13, bf16[1024,256]{1,0:T(8,128)(2,1)} %get-tuple-element.138, ...), kind=kOutput, calls=%fused_computation.5 | convolution fusion | flops 4849399808 | bytes 15478784 | tf_op jit(solution)/shard_map/dot_general | solution.py:1590
  476.2 2.6 fusion.7
  478.8 5.0 convolution_convert_fusion
  483.8 64.8 %scatter_first.1 = (f32[128,2048]{1,0:T(8,128)}, f32[4,64,128]{2,1,0:T(8,128)}, bf16[4,512,128]{2,1,0:T(8,128)(2,1)}, bf16[4,512,768]{2,1,0:T(8,128)(2,1)}) custom-call(bf16[8,128,2048]{2,1,0:T(8,128)(2,1)} %bitcast.152, f32[4,64,128]{2,1,0:T(8,128)} %concatenate.53.refs_1_, bf16[4,512,128]{2,1,0:T(8,128)(2,1)} %bitcast.178, bf16[4,512,768]{2,1,0:T(8,128)(2,1)} %bitcast.154), custom_call_target="tpu_custom_call" | custom-call | tf_op jit(solution)/shard_map/scatter_first/pallas_call | solution.py:750
  548.6 1.8 reduce.5
  550.6 2.8 reduce.3
  553.4 2.2 pad_maximum_fusion.refs_0_
  555.6 28.9 %return_columns.1.source = bf16[8,64,1152]{2,1,0:T(8,128)(2,1)} custom-call(bf16[8,64,1152]{2,1,0:T(8,128)(2,1)} %pad_maximum_fusion.refs_0_), custom_call_target="tpu_custom_call" | custom-call | tf_op jit(solution)/shard_map/return_columns/pallas_call | solution.py:750
  585.7 2.1 join_columns.2
  591.5 2.5 join_columns.3
  596.6 1.7 fusion.20
  600.0 3.1 fusion.36
  (195 shorter events, 45.9 us)
Async XLA Ops:
  7.2 14.3 %copy-start.26 = (bf16[64,64]{1,0:T(8,128)(2,1)S(1)}, bf16[64,64]{1,0:T(8,128)(2,1)}, u32[]{:S(2)}) copy-start(bf16[64,64]{1,0:T(8,128)(2,1)} %param.26) | copy-start | bytes 24580
  7.2 232.3 %all-gather.5.cloned.1.call-start = ((), (), s32[]{:S(2)}) async-start(), calls=%async_computation.4 | async-start | bytes 2359296 | tf_op jit(solution)/shard_map/all_gather | solution.py:1704
  98.2 141.3 %all-gather.7.cloned.1.call-start = ((), (), s32[]{:S(2)}) async-start(), calls=%async_computation.5 | async-start | bytes 2359296 | tf_op jit(solution)/shard_map/all_gather | solution.py:1731
  98.6 3.8 copy-start.12
  98.6 4.7 copy-start.34
  107.4 3.7 copy-start.17
  107.4 4.0 copy-start.25
  112.9 1.4 copy-start.4
  168.7 431.2 %reduce-scatter.5.cloned.1.call-start = ((), (), s32[]{:S(2)}) async-start(), calls=%async_computation.3 | async-start | bytes 2359296 | tf_op jit(solution)/shard_map/reduce_scatter | solution.py:1797
  179.2 56.8 %copy-start.15 = (bf16[1,128,2048]{2,1,0:T(8,128)(2,1)S(1)}, bf16[1,128,2048]{2,1,0:T(8,128)(2,1)}, u32[]{:S(2)}) copy-start(bf16[1,128,2048]{2,1,0:T(8,128)(2,1)} %param.18) | copy-start | bytes 1572868
  237.6 94.3 %copy-start.27 = (f32[128]{0:T(128)}, f32[128]{0:T(128)S(1)}, u32[]{:S(2)}) copy-start(f32[128]{0:T(128)S(1)} %add_rsqrt_fusion.3) | copy-start | bytes 1540
  326.6 4.9 copy-start.10
  326.6 4.9 copy-start.13
  326.7 5.3 copy-start.16
  331.9 60.6 %copy-start.29 = (f32[128]{0:T(128)}, f32[128]{0:T(128)S(1)}, u32[]{:S(2)}) copy-start(f32[128]{0:T(128)S(1)} %broadcast_multiply_fusion.7) | copy-start | bytes 1540
  392.5 4.8 copy-start.23
  392.5 4.8 copy-start.32
  413.2 3.8 copy-start.24
  413.2 4.7 copy-start.5
  459.9 140.0 %reduce-scatter.3.cloned.1.call-start = ((), (), s32[]{:S(2)}) async-start(), calls=%async_computation.2 | async-start | bytes 2359296 | tf_op jit(solution)/shard_map/reduce_scatter | solution.py:1774
  465.4 10.8 %copy-start.18 = (bf16[1024,2048]{1,0:T(8,128)(2,1)S(1)}, bf16[1024,2048]{1,0:T(8,128)(2,1)}, u32[]{:S(2)}) copy-start(bf16[1024,2048]{1,0:T(8,128)(2,1)} %copy-done.17) | copy-start | bytes 12582916
  476.2 2.6 copy-start.33
  553.4 38.1 %copy-start.2 = (bf16[8,64,1408]{2,1,0:T(8,128)(2,1)S(1)}, bf16[8,64,1408]{2,1,0:T(8,128)(2,1)}, u32[]{:S(2)}) copy-start(bf16[8,64,1408]{2,1,0:T(8,128)(2,1)} %get-tuple-element.107.source) | copy-start | bytes 4325380
  584.5 1.3 copy-start
  591.5 2.5 copy-start.21
  591.5 3.4 copy-start.22
  591.5 6.8 %copy-start.19 = (bf16[4,176,2048]{2,1,0:T(8,128)(2,1)S(1)}, bf16[4,176,2048]{2,1,0:T(8,128)(2,1)}, u32[]{:S(2)}) copy-start(bf16[4,176,2048]{2,1,0:T(8,128)(2,1)} %get-tuple-element.108) | copy-start | bytes 8650756
  594.0 6.0 copy-start.11
  594.0 6.0 copy-start.14
  594.0 6.0 copy-start.28
  594.0 6.0 copy-start.30
  594.0 6.0 copy-start.31
  (7 other events, 7.0 us)
Sparse Core Ops, SparseCore 0:
  98.3 29.5 all-gather.4
  168.8 31.9 all-gather.6
  460.1 29.9 reduce-scatter.4
  492.3 47.9 reduce-scatter.2
